TPU v7x, 32 devices: a whole 2x2x4 slice. The times are simulated.
32 devices in a mesh: ctx: 8 (over y, x, core), tp: 4 (over z).
Axes of the slice: x: 2, y: 2, z: 4, core: 2. Of those that a mesh axis runs over, the one named last changes fastest.
Arguments:
- saved_input: bfloat16 [4096, 4096], P('tp', 'ctx'), may hold values from -8 to 8
- query: bfloat16 [4096, 4096], P('tp', 'ctx'), may hold values from -6 to 6
- key: bfloat16 [4096, 4096], P('tp', 'ctx'), may hold values from -6 to 6
- value: bfloat16 [4096, 4096], P('tp', 'ctx'), may hold values from -6 to 6
- grad_out: bfloat16 [4096, 4096], P('tp', 'ctx'), may hold values from -6 to 6
- filters: bfloat16 [256, 128], P('tp'), may hold values from -0.59765625 to 0.59765625
Outputs:
- grad_query: bfloat16 [4096, 4096], P('tp', 'ctx')
- grad_key: bfloat16 [4096, 4096], P('tp', 'ctx')
- grad_value: bfloat16 [4096, 4096], P('tp', 'ctx')
- grad_filters: float32 [256, 128], P('tp')
- grad_weight: float32 [4096, 4096], P('ctx', 'tp')
All inputs are finite; a program needn't handle non-finite values.
Results may differ from a plain program's by a relative error of at most 0.005.
Values may be sent and summed in bfloat16 or wider, within the bound.
No kernel may reach another device: no remote copies, remote signals or barrier semaphores. Data moves between devices by JAX's collectives and lax.ppermute only.
A program may use at most 128 MiB of HBM per device.

v0:
```python
import functools
import jax, jax.numpy as jnp
from jax import lax
from jax.experimental import pallas as pl
from jax.experimental.pallas import tpu as pltpu
from jax.sharding import PartitionSpec as P

F32, BF16 = jnp.float32, jnp.bfloat16

def conv_kernel(width, taps, q_ref, k_ref, v_ref, go_ref, kvh_ref, ggh_ref, f_ref, gq_ref, gk_ref, gv_ref, gf_ref, low_ref, high_ref):
    rows, toks = q_ref.shape
    blocks = toks // taps
    for g in range(rows // width):
        r = slice(g * width, (g + 1) * width)
        k = k_ref[r, :].astype(F32)
        v = v_ref[r, :].astype(F32)
        go = go_ref[r, :].astype(F32)
        kv = (k * v).astype(BF16)
        gg = (q_ref[r, :].astype(F32) * go).astype(BF16)
        kvb = [kvh_ref[r, :]] + [kv[:, n * taps:(n + 1) * taps] for n in range(blocks)]
        ggb = [gg[:, n * taps:(n + 1) * taps] for n in range(blocks)] + [ggh_ref[r, :]]
        f = f_ref[g:g + 1, :].astype(F32)
        padded = jnp.concatenate([f, jnp.zeros_like(f)], axis=1)
        band = pltpu.roll(jnp.broadcast_to(padded, (taps, 2 * taps)), 0, 1, stride=1, stride_axis=0).astype(BF16)
        kv_all = jnp.concatenate(kvb, axis=0)
        y = jnp.dot(kv_all, band, preferred_element_type=F32)
        conv = jnp.concatenate(
            [y[(n + 1) * width:(n + 2) * width, :taps] + y[n * width:(n + 1) * width, taps:] for n in range(blocks)], axis=1)
        gq_ref[r, :] = (go * conv).astype(BF16)
        pairs = jnp.concatenate([jnp.concatenate(ggb[:-1], axis=0), jnp.concatenate(ggb[1:], axis=0)], axis=1)
        m = lax.dot_general(pairs, band, (((1,), (1,)), ((), ())), preferred_element_type=F32)
        mixed = jnp.concatenate([m[n * width:(n + 1) * width] for n in range(blocks)], axis=1)
        gk_ref[r, :] = (mixed * v).astype(BF16)
        gv_ref[r, :] = (mixed * k).astype(BF16)
        x = lax.dot_general(kv_all[width:], pairs, (((0,), (0,)), ((), ())), preferred_element_type=F32)
        total = x[:8]
        for a in range(8, taps, 8):
            total = total + pltpu.roll(x[a:a + 8], 2 * taps - a, 1)
        low_ref[8 * g:8 * g + 8, :] = total[:, :taps]
        high_ref[8 * g:8 * g + 8, :] = total[:, taps:]
    lags = rows // width
    total = low_ref[pl.ds(0, lags, stride=8), :]
    for b in range(1, 8):
        both = jnp.concatenate([ref[pl.ds(b, lags, stride=8), :] for ref in (low_ref, high_ref)], axis=1)
        total = total + pltpu.roll(both, 2 * taps - b, 1)[:, :taps]
    gf_ref[...] = total

def conv_call(query, key, value, grad_out, kvh, ggh, filters, step=8):
    channels, toks = key.shape
    groups, taps = filters.shape
    width = channels // groups
    rows = step * width
    wide = pl.BlockSpec((rows, toks), lambda i: (i, 0))
    halo = pl.BlockSpec((rows, taps), lambda i: (i, 0))
    filt = pl.BlockSpec((step, taps), lambda i: (i, 0))
    big = jax.ShapeDtypeStruct((channels, toks), BF16)
    return pl.pallas_call(
        functools.partial(conv_kernel, width, taps),
        grid=(groups // step,),
        in_specs=[wide] * 4 + [halo] * 2 + [filt],
        out_specs=[wide] * 3 + [filt],
        out_shape=[big] * 3 + [jax.ShapeDtypeStruct((groups, taps), F32)],
        scratch_shapes=[pltpu.VMEM((8 * step, taps), F32)] * 2,
        compiler_params=pltpu.CompilerParams(vmem_limit_bytes=48 * 2**20),
        name="conv",
    )(query, key, value, grad_out, kvh, ggh, filters)


def place(relative, bits):
    index = 0
    for bit in bits[1:]:
        index = index * 2 + ((relative >> bit) & 1)
    return ((relative >> bits[0]) & 1) == 1, index


def product_kernel(tp_count, orders, offsets, spot_ref, *refs):
    sources, (own_ref, sibling_ref), outs = refs[: len(offsets)], refs[len(offsets) : len(offsets) + 2], refs[len(offsets) + 2 :]
    side = pl.program_id(0) // (pl.num_programs(0) // 2)
    toks = own_ref.shape[1]
    z, chip = spot_ref[0], spot_ref[1]
    for offset, source in zip(offsets, sources):
        owner = z + offset

        @pl.when((owner >= 0) & (owner < tp_count))
        def _():
            for part in range(source.shape[0]):
                contract = (((1,), (1,)), ((), ()))
                total = lax.dot_general(
                    source[part, :, :toks], own_ref[...], contract, preferred_element_type=F32
                ) + lax.dot_general(
                    source[part, :, toks:], sibling_ref[...], contract, preferred_element_type=F32
                )
                relative = (owner * source.shape[0] + part) ^ chip
                for order, bits in enumerate(orders):
                    goes, index = place(relative, bits)

                    @pl.when((side == order) & goes)
                    def _():
                        outs[2 * order][index] = total.astype(BF16)

                    @pl.when((side == order) & jnp.logical_not(goes))
                    def _():
                        outs[2 * order + 1][index] = total


def product_call(tp_count, orders, offsets, spot, sources, own, sibling):
    channels, toks = own.shape
    parts, rows, _ = sources[0].shape
    tile = min(256, channels // 2)
    steps = channels // tile
    half = tp_count * parts // 2
    whole = pl.BlockSpec(sources[0].shape, lambda i, s: (0, 0, 0))
    tokens = pl.BlockSpec((tile, toks), lambda i, s: (i, 0))
    first = pl.BlockSpec((half, rows, tile), lambda i, s: (0, 0, jnp.minimum(i, steps // 2 - 1)))
    second = pl.BlockSpec((half, rows, tile), lambda i, s: (0, 0, jnp.maximum(i - steps // 2, 0)))
    shape = (half, rows, channels // 2)
    return pl.pallas_call(
        functools.partial(product_kernel, tp_count, orders, offsets),
        grid_spec=pltpu.PrefetchScalarGridSpec(
            num_scalar_prefetch=1,
            grid=(steps,),
            in_specs=[whole] * len(sources) + [tokens] * 2,
            out_specs=[first, first, second, second],
        ),
        out_shape=[jax.ShapeDtypeStruct(shape, kind) for kind in (BF16, F32, BF16, F32)],
        compiler_params=pltpu.CompilerParams(vmem_limit_bytes=40 * 2**20),
        cost_estimate=pl.CostEstimate(
            flops=2 * 2 * half * rows * channels * 2 * toks,
            bytes_accessed=len(sources) * sources[0].size * 2 + own.size * 4 + 2 * half * rows * channels * 3,
            transcendentals=0,
        ),
        name="product",
    )(spot, *sources, own, sibling)


CHUNKS = 4


def along(axis, count, step):
    return lambda value, low, high: lax.ppermute(
        value, axis, [(i, i + step) for i in range(count) if low <= i < high and 0 <= i + step < count]
    )


def shards(saved_input, query, key, value, grad_out, filters):
    channels, toks = key.shape
    groups, taps = filters.shape
    width = channels // groups
    ctx_count, tp_count = lax.axis_size("ctx"), lax.axis_size("tp")
    ctx, z = lax.axis_index("ctx"), lax.axis_index("tp")
    chip, core = ctx // 2, ctx % 2
    chips = ctx_count // 2
    bits = tuple(range(chips.bit_length() - 1))
    orders = (bits, bits[::-1])
    total_tokens = toks * ctx_count

    def flip(array, distance):
        return lax.ppermute(array, "ctx", [(i, i ^ distance) for i in range(ctx_count)])

    parts = chips // tp_count
    rows = saved_input.shape[0] // (2 * parts)
    by_core = saved_input.reshape(parts, 2, rows, toks)
    mine = lax.dynamic_index_in_dim(by_core, core, 1, keepdims=False)
    theirs = lax.dynamic_index_in_dim(by_core, 1 - core, 1, keepdims=False)
    block = jnp.concatenate([mine, flip(theirs, 1)], axis=2)

    def product(a, b):
        return (a.astype(F32) * b.astype(F32)).astype(BF16)

    before = product(key[:, toks - taps :], value[:, toks - taps :])
    after = product(query[:, :taps], grad_out[:, :taps])
    kvh = lax.ppermute(before, "ctx", [(i, i + 1) for i in range(ctx_count - 1)])
    ggh = lax.ppermute(after, "ctx", [(i + 1, i) for i in range(ctx_count - 1)])

    right, left = along("tp", tp_count, 1), along("tp", tp_count, -1)
    size = rows // CHUNKS
    gathered = []
    for c in range(CHUNKS):
        piece = block[:, c * size : (c + 1) * size]
        sources = [(0, piece)]
        up, down = piece, piece
        for s in range(1, tp_count):
            up = right(up, s - 1, tp_count)
            down = left(down, 0, tp_count - s + 1)
            sources += [(-s, up), (s, down)]
        gathered.append(sources)

    grad_query, grad_key, grad_value, lag_sums = conv_call(query, key, value, grad_out, kvh, ggh, filters)
    sibling = flip(grad_value, 1)

    distance = 1
    while distance < ctx_count:
        lag_sums = lag_sums + flip(lag_sums, distance)
        distance *= 2
    grad_filters = lag_sums * (total_tokens * width) ** (-0.5)

    spot = jnp.stack([z, chip]).astype(jnp.int32)
    done = []
    for sources in gathered:
        outs = product_call(
            tp_count, orders, [o for o, _ in sources], spot, [a for _, a in sources], grad_value, sibling
        )
        columns = []
        for order, path in enumerate(orders):
            send, keep = outs[2 * order], outs[2 * order + 1]
            for stage, bit in enumerate(path):
                keep = keep + flip(send, 2 << bit).astype(F32)
                if stage + 1 < len(path):
                    count = keep.shape[0] // 2
                    send, keep = keep[count:].astype(BF16), keep[:count]
            columns.append(keep[0] * total_tokens ** (-0.5))
        done.append(jnp.concatenate(columns, axis=1))
    grad_weight = jnp.concatenate(done, axis=0)
    return (grad_query, grad_key, grad_value, grad_filters, grad_weight)


def solution(mesh):
    placed = (P("tp", "ctx"),) * 5 + (P("tp", None),)
    return jax.shard_map(
        shards,
        mesh=mesh,
        in_specs=placed,
        out_specs=(P("tp", "ctx"),) * 3 + (P("tp", None), P("ctx", "tp")),
        check_vma=False,
    )
```

profile of v0, /device:TPU:0, one launch (start us, length us, event | category | flops | bytes accessed | tf_op | source)
XLA Modules:
  0.0 151.9 jit_solution(4854765381939272742)
XLA Ops:
  0.7 1.4 dynamic-slice_bitcast_fusion.1
  2.6 1.1 multiply_convert_fusion.1
  3.8 2.0 %collective-permute-start = (bf16[1024,128]{1,0:T(8,128)(2,1)S(1)}, bf16[1024,128]{1,0:T(8,128)(2,1)S(1)}, u32[]{:S(2)}, u32[]{:S(2)}) collective-permute-start(bf16[1024,128]{1,0:T(8,128)(2,1)S(1)} %multiply_convert_fusion.1), channel_id=1, source_target_pairs={{0,4},{4,8},{8,12},{12,16},{16,20},{20,24},{24,28},{1,5},{5,9},{9,... | collective-permute-start | bytes 786440 | tf_op jit(solution)/shard_map/ppermute | solution.py:172
  5.8 1.0 multiply_convert_fusion
  6.8 1.3 collective-permute-start.1
  8.3 4.8 %collective-permute-start.37 = (bf16[1,128,1024]{2,1,0:T(8,128)(2,1)S(1)}, bf16[1,128,1024]{2,1,0:T(8,128)(2,1)S(1)}, u32[]{:S(2)}, u32[]{:S(2)}) collective-permute-start(bf16[1,128,1024]{2,1,0:T(8,128)(2,1)S(1)} %get-tuple-element.47.refs_0_), channel_id=1, source_target_pairs={{0,1},{1,2},{2,3},{4,5},{5,6},{6,7},{8,9},{9,10},{10,11},{12,13},{... | collective-permute-start | bytes 786440 | tf_op jit(solution)/shard_map/ppermute | solution.py:140
  13.1 1.3 collective-permute-start.38
  14.4 7.8 %conv.1 = (bf16[1024,512]{1,0:T(8,128)(2,1)}, bf16[1024,512]{1,0:T(8,128)(2,1)}, bf16[1024,512]{1,0:T(8,128)(2,1)}, f32[64,128]{1,0:T(8,128)S(1)}) custom-call(bf16[1024,512]{1,0:T(8,128)(2,1)S(1)} %copy-done, bf16[1024,512]{1,0:T(8,128)(2,1)S(1)} %copy-done.1, bf16[1024,512]{1,0:T(8,128)(2,1)S(1)} %copy-done.2, bf16[1024,512]{1,0:T(8,128)(2,1)S(1)} %copy-done.3, ...), custom_call_target="tpu_custom_call" | custom-call | tf_op jit(solution)/shard_map/conv/pallas_call | solution.py:57
  22.2 2.6 %collective-permute-start.2 = (f32[64,128]{1,0:T(8,128)S(1)}, f32[64,128]{1,0:T(8,128)S(1)}, u32[]{:S(2)}, u32[]{:S(2)}) collective-permute-start(f32[64,128]{1,0:T(8,128)S(1)} %get-tuple-element.28), channel_id=1, source_target_pairs={{0,4},{4,0},{8,12},{12,8},{16,20},{20,16},{24,28},{28,24},{1,5},{5... | collective-permute-start | bytes 98312 | tf_op jit(solution)/shard_map/ppermute | solution.py:158
  24.8 0.9 collective-permute-done.2
  25.7 2.4 %collective-permute-start.3 = (f32[64,128]{1,0:T(8,128)S(1)}, f32[64,128]{1,0:T(8,128)S(1)}, u32[]{:S(2)}, u32[]{:S(2)}) collective-permute-start(f32[64,128]{1,0:T(8,128)S(1)} %add.70), channel_id=1, source_target_pairs={{0,8},{4,12},{8,0},{12,4},{16,24},{20,28},{24,16},{28,20},{1,9},{5... | collective-permute-start | bytes 98312 | tf_op jit(solution)/shard_map/ppermute | solution.py:158
  28.1 3.5 %collective-permute-start.27 = (bf16[1,128,1024]{2,1,0:T(8,128)(2,1)S(1)}, bf16[1,128,1024]{2,1,0:T(8,128)(2,1)S(1)}, u32[]{:S(2)}, u32[]{:S(2)}) collective-permute-start(bf16[1,128,1024]{2,1,0:T(8,128)(2,1)S(1)} %get-tuple-element.48.refs_0_), channel_id=1, source_target_pairs={{0,1},{1,2},{2,3},{4,5},{5,6},{6,7},{8,9},{9,10},{10,11},{12,13},{... | collective-permute-start | bytes 786440 | tf_op jit(solution)/shard_map/ppermute | solution.py:140
  31.6 1.5 collective-permute-start.4
  33.1 1.3 collective-permute-start.28
  34.4 1.2 collective-permute-done.4
  35.6 3.4 %collective-permute-start.17 = (bf16[1,128,1024]{2,1,0:T(8,128)(2,1)S(1)}, bf16[1,128,1024]{2,1,0:T(8,128)(2,1)S(1)}, u32[]{:S(2)}, u32[]{:S(2)}) collective-permute-start(bf16[1,128,1024]{2,1,0:T(8,128)(2,1)S(1)} %get-tuple-element.46.refs_0_), channel_id=1, source_target_pairs={{0,1},{1,2},{2,3},{4,5},{5,6},{6,7},{8,9},{9,10},{10,11},{12,13},{... | collective-permute-start | bytes 786440 | tf_op jit(solution)/shard_map/ppermute | solution.py:140
  39.1 1.3 collective-permute-start.18
  40.4 4.6 %collective-permute-start.6 = (bf16[1,128,1024]{2,1,0:T(8,128)(2,1)S(1)}, bf16[1,128,1024]{2,1,0:T(8,128)(2,1)S(1)}, u32[]{:S(2)}, u32[]{:S(2)}) collective-permute-start(bf16[1,128,1024]{2,1,0:T(8,128)(2,1)S(1)} %get-tuple-element.45.refs_0_), channel_id=1, source_target_pairs={{0,1},{1,2},{2,3},{4,5},{5,6},{6,7},{8,9},{9,10},{10,11},{12,13},{... | collective-permute-start | bytes 786440 | tf_op jit(solution)/shard_map/ppermute | solution.py:140
  45.0 1.3 collective-permute-start.7
  46.3 1.4 collective-permute-start.39
  48.1 1.3 collective-permute-start.40
  49.4 0.7 copy-done.6
  50.8 4.8 %collective-permute-done.7.refs_2_ = bf16[1,128,1024]{2,1,0:T(8,128)(2,1)S(1)} collective-permute-done((bf16[1,128,1024]{2,1,0:T(8,128)(2,1)S(1)}, bf16[1,128,1024]{2,1,0:T(8,128)(2,1)S(1)}, u32[]{:S(2)}, u32[]{:S(2)}) %collective-permute-start.7) | collective-permute-done | bytes 262176 | tf_op jit(solution)/shard_map/ppermute | solution.py:140
  55.6 1.3 collective-permute-start.30
  56.9 0.7 copy-done.10
  58.3 3.3 %collective-permute-done.40.refs_4_ = bf16[1,128,1024]{2,1,0:T(8,128)(2,1)} collective-permute-done((bf16[1,128,1024]{2,1,0:T(8,128)(2,1)S(1)}, bf16[1,128,1024]{2,1,0:T(8,128)(2,1)}, u32[]{:S(2)}, u32[]{:S(2)}) %collective-permute-start.40) | collective-permute-done | bytes 262176 | tf_op jit(solution)/shard_map/ppermute | solution.py:140
  61.5 1.3 collective-permute-start.20
  62.8 0.7 copy-done.8
  63.5 1.4 collective-permute-start.8
  64.9 3.3 %collective-permute-done.30.refs_4_ = bf16[1,128,1024]{2,1,0:T(8,128)(2,1)S(1)} collective-permute-done((bf16[1,128,1024]{2,1,0:T(8,128)(2,1)S(1)}, bf16[1,128,1024]{2,1,0:T(8,128)(2,1)S(1)}, u32[]{:S(2)}, u32[]{:S(2)}) %collective-permute-start.30) | collective-permute-done | bytes 262176 | tf_op jit(solution)/shard_map/ppermute | solution.py:140
  68.2 1.3 collective-permute-start.9
  69.5 1.4 collective-permute-start.41
  70.8 3.4 %collective-permute-done.20.refs_4_ = bf16[1,128,1024]{2,1,0:T(8,128)(2,1)S(1)} collective-permute-done((bf16[1,128,1024]{2,1,0:T(8,128)(2,1)S(1)}, bf16[1,128,1024]{2,1,0:T(8,128)(2,1)S(1)}, u32[]{:S(2)}, u32[]{:S(2)}) %collective-permute-start.20) | collective-permute-done | bytes 262176 | tf_op jit(solution)/shard_map/ppermute | solution.py:140
  74.9 1.3 collective-permute-start.42
  77.0 6.0 %collective-permute-done.9.refs_4_ = bf16[1,128,1024]{2,1,0:T(8,128)(2,1)} collective-permute-done((bf16[1,128,1024]{2,1,0:T(8,128)(2,1)S(1)}, bf16[1,128,1024]{2,1,0:T(8,128)(2,1)}, u32[]{:S(2)}, u32[]{:S(2)}) %collective-permute-start.9) | collective-permute-done | bytes 262176 | tf_op jit(solution)/shard_map/ppermute | solution.py:140
  83.0 1.3 collective-permute-start.32
  85.0 3.6 %collective-permute-done.42.refs_6_ = bf16[1,128,1024]{2,1,0:T(8,128)(2,1)} collective-permute-done((bf16[1,128,1024]{2,1,0:T(8,128)(2,1)}, bf16[1,128,1024]{2,1,0:T(8,128)(2,1)}, u32[]{:S(2)}, u32[]{:S(2)}) %collective-permute-start.42) | collective-permute-done | bytes 262176 | tf_op jit(solution)/shard_map/ppermute | solution.py:140
  88.6 1.3 collective-permute-start.22
  91.2 1.3 collective-permute-start.11
  92.5 1.2 copy-done.5
  93.7 0.9 copy-done.7
  94.7 7.4 %product.7 = (bf16[2,128,512]{2,1,0:T(8,128)(2,1)S(1)}, f32[2,128,512]{2,1,0:T(8,128)S(1)}, bf16[2,128,512]{2,1,0:T(8,128)(2,1)S(1)}, f32[2,128,512]{2,1,0:T(8,128)S(1)}) custom-call(s32[2]{0:T(128)S(1)} %pad_add_fusion.spot_ref, bf16[1,128,1024]{2,1,0:T(8,128)(2,1)S(1)} %get-tuple-element.47.refs_0_, ...), custom_call_target="tpu_custom_call" | custom-call | flops 1073741824 | bytes 5505024 | tf_op jit(solution)/shard_map/product/pallas_call | solution.py:117
  102.1 1.5 collective-permute-start.45
  103.6 6.2 %product.6 = (bf16[2,128,512]{2,1,0:T(8,128)(2,1)S(1)}, f32[2,128,512]{2,1,0:T(8,128)S(1)}, bf16[2,128,512]{2,1,0:T(8,128)(2,1)S(1)}, f32[2,128,512]{2,1,0:T(8,128)S(1)}) custom-call(s32[2]{0:T(128)S(1)} %pad_add_fusion.spot_ref, bf16[1,128,1024]{2,1,0:T(8,128)(2,1)S(1)} %get-tuple-element.48.refs_0_, ...), custom_call_target="tpu_custom_call" | custom-call | flops 1073741824 | bytes 5505024 | tf_op jit(solution)/shard_map/product/pallas_call | solution.py:117
  109.9 1.5 collective-permute-start.43
  111.9 6.2 %product.5 = (bf16[2,128,512]{2,1,0:T(8,128)(2,1)S(1)}, f32[2,128,512]{2,1,0:T(8,128)S(1)}, bf16[2,128,512]{2,1,0:T(8,128)(2,1)S(1)}, f32[2,128,512]{2,1,0:T(8,128)S(1)}) custom-call(s32[2]{0:T(128)S(1)} %pad_add_fusion.spot_ref, bf16[1,128,1024]{2,1,0:T(8,128)(2,1)S(1)} %get-tuple-element.46.refs_0_, ...), custom_call_target="tpu_custom_call" | custom-call | flops 1073741824 | bytes 5505024 | tf_op jit(solution)/shard_map/product/pallas_call | solution.py:117
  118.1 0.8 collective-permute-start.33
  118.9 1.4 collective-permute-start.25
  120.3 7.2 %product.4 = (bf16[2,128,512]{2,1,0:T(8,128)(2,1)S(1)}, f32[2,128,512]{2,1,0:T(8,128)S(1)}, bf16[2,128,512]{2,1,0:T(8,128)(2,1)S(1)}, f32[2,128,512]{2,1,0:T(8,128)S(1)}) custom-call(s32[2]{0:T(128)S(1)} %pad_add_fusion.spot_ref, bf16[1,128,1024]{2,1,0:T(8,128)(2,1)S(1)} %get-tuple-element.45.refs_0_, ...), custom_call_target="tpu_custom_call" | custom-call | flops 1073741824 | bytes 5505024 | tf_op jit(solution)/shard_map/product/pallas_call | solution.py:117
  127.6 1.5 collective-permute-start.23
  129.8 0.8 collective-permute-start.13
  130.7 1.4 collective-permute-start.46
  132.2 1.6 %collective-permute-start.44 = (bf16[1,128,512]{2,1,0:T(8,128)(2,1)S(1)}, bf16[1,128,512]{2,1,0:T(8,128)(2,1)S(1)}, u32[]{:S(2)}, u32[]{:S(2)}) collective-permute-start(bf16[1,128,512]{2,1,0:T(8,128)(2,1)S(1)} %slice.197), channel_id=1, source_target_pairs={{0,16},{4,20},{8,24},{12,28},{16,0},{20,4},{24,8},{28,12},{1,17},{... | collective-permute-start | bytes 393224 | tf_op jit(solution)/shard_map/ppermute | solution.py:158
  133.9 2.9 %collective-permute-done.23 = bf16[2,128,512]{2,1,0:T(8,128)(2,1)S(1)} collective-permute-done((bf16[2,128,512]{2,1,0:T(8,128)(2,1)S(1)}, bf16[2,128,512]{2,1,0:T(8,128)(2,1)S(1)}, u32[]{:S(2)}, u32[]{:S(2)}) %collective-permute-start.23) | collective-permute-done | bytes 262176 | tf_op jit(solution)/shard_map/ppermute | solution.py:158
  136.9 1.4 collective-permute-start.36
  139.1 2.7 %collective-permute-done.13 = bf16[2,128,512]{2,1,0:T(8,128)(2,1)S(1)} collective-permute-done((bf16[2,128,512]{2,1,0:T(8,128)(2,1)S(1)}, bf16[2,128,512]{2,1,0:T(8,128)(2,1)S(1)}, u32[]{:S(2)}, u32[]{:S(2)}) %collective-permute-start.13) | collective-permute-done | bytes 262176 | tf_op jit(solution)/shard_map/ppermute | solution.py:158
  141.8 1.4 collective-permute-start.26
  143.3 1.0 collective-permute-start.24
  144.4 0.9 collective-permute-start.16
  145.3 1.6 %collective-permute-start.14 = (bf16[1,128,512]{2,1,0:T(8,128)(2,1)S(1)}, bf16[1,128,512]{2,1,0:T(8,128)(2,1)S(1)}, u32[]{:S(2)}, u32[]{:S(2)}) collective-permute-start(bf16[1,128,512]{2,1,0:T(8,128)(2,1)S(1)} %slice.203), channel_id=1, source_target_pairs={{0,16},{4,20},{8,24},{12,28},{16,0},{20,4},{24,8},{28,12},{1,17},{... | collective-permute-start | bytes 393224 | tf_op jit(solution)/shard_map/ppermute | solution.py:158
  147.0 1.4 collective-permute-done.24
  148.4 1.0 collective-permute-done.16
  149.5 0.9 collective-permute-done.14
  150.4 1.5 maximum_maximum_fusion
  (108 shorter events, 8.6 us)
Async XLA Ops:
  0.6 2.0 %copy-start.1 = (bf16[1024,512]{1,0:T(8,128)(2,1)S(1)}, bf16[1024,512]{1,0:T(8,128)(2,1)}, u32[]{:S(2)}) copy-start(bf16[1024,512]{1,0:T(8,128)(2,1)} %k_ref.1) | copy-start | bytes 3145732
  0.6 5.1 %copy-start = (bf16[1024,512]{1,0:T(8,128)(2,1)S(1)}, bf16[1024,512]{1,0:T(8,128)(2,1)}, u32[]{:S(2)}) copy-start(bf16[1024,512]{1,0:T(8,128)(2,1)} %q_ref.1) | copy-start | bytes 3145732
  2.1 12.3 %copy-start.2 = (bf16[1024,512]{1,0:T(8,128)(2,1)S(1)}, bf16[1024,512]{1,0:T(8,128)(2,1)}, u32[]{:S(2)}) copy-start(bf16[1024,512]{1,0:T(8,128)(2,1)} %v_ref.1) | copy-start | bytes 3145732
  2.1 12.3 %copy-start.3 = (bf16[1024,512]{1,0:T(8,128)(2,1)S(1)}, bf16[1024,512]{1,0:T(8,128)(2,1)}, u32[]{:S(2)}) copy-start(bf16[1024,512]{1,0:T(8,128)(2,1)} %go_ref.1) | copy-start | bytes 3145732
  2.1 12.3 %copy-start.4 = (bf16[64,128]{1,0:T(8,128)(2,1)S(1)}, bf16[64,128]{1,0:T(8,128)(2,1)}, u32[]{:S(2)}) copy-start(bf16[64,128]{1,0:T(8,128)(2,1)} %f_ref.1) | copy-start | bytes 49156
  2.1 6.0 %collective-permute-start.5 = (bf16[1,512,512]{2,1,0:T(8,128)(2,1)S(1)}, bf16[1,512,512]{2,1,0:T(8,128)(2,1)S(1)}, u32[]{:S(2)}, u32[]{:S(2)}) collective-permute-start(bf16[1,512,512]{2,1,0:T(8,128)(2,1)S(1)} %get-tuple-element.50), channel_id=1, source_target_pairs={{0,4},{4,0},{8,12},{12,8},{16,20},{20,16},{24,28},{28,24},{1,5},{5... | collective-permute-start | bytes 1572872 | tf_op jit(solution)/shard_map/ppermute | solution.py:158
  3.8 10.6 %collective-permute-start = (bf16[1024,128]{1,0:T(8,128)(2,1)S(1)}, bf16[1024,128]{1,0:T(8,128)(2,1)S(1)}, u32[]{:S(2)}, u32[]{:S(2)}) collective-permute-start(bf16[1024,128]{1,0:T(8,128)(2,1)S(1)} %multiply_convert_fusion.1), channel_id=1, source_target_pairs={{0,4},{4,8},{8,12},{12,16},{16,20},{20,24},{24,28},{1,5},{5,9},{9,... | collective-permute-start | bytes 786440 | tf_op jit(solution)/shard_map/ppermute | solution.py:172
  6.8 7.6 %collective-permute-start.1 = (bf16[1024,128]{1,0:T(8,128)(2,1)S(1)}, bf16[1024,128]{1,0:T(8,128)(2,1)S(1)}, u32[]{:S(2)}, u32[]{:S(2)}) collective-permute-start(bf16[1024,128]{1,0:T(8,128)(2,1)S(1)} %multiply_convert_fusion), channel_id=1, source_target_pairs={{4,0},{8,4},{12,8},{16,12},{20,16},{24,20},{28,24},{5,1},{9,5},{13... | collective-permute-start | bytes 786440 | tf_op jit(solution)/shard_map/ppermute | solution.py:173
  8.3 30.8 %collective-permute-start.37 = (bf16[1,128,1024]{2,1,0:T(8,128)(2,1)S(1)}, bf16[1,128,1024]{2,1,0:T(8,128)(2,1)S(1)}, u32[]{:S(2)}, u32[]{:S(2)}) collective-permute-start(bf16[1,128,1024]{2,1,0:T(8,128)(2,1)S(1)} %get-tuple-element.47.refs_0_), channel_id=1, source_target_pairs={{0,1},{1,2},{2,3},{4,5},{5,6},{6,7},{8,9},{9,10},{10,11},{12,13},{... | collective-permute-start | bytes 786440 | tf_op jit(solution)/shard_map/ppermute | solution.py:140
  13.1 27.3 %collective-permute-start.38 = (bf16[1,128,1024]{2,1,0:T(8,128)(2,1)S(1)}, bf16[1,128,1024]{2,1,0:T(8,128)(2,1)S(1)}, u32[]{:S(2)}, u32[]{:S(2)}) collective-permute-start(bf16[1,128,1024]{2,1,0:T(8,128)(2,1)S(1)} %get-tuple-element.47.refs_0_), channel_id=1, source_target_pairs={{1,0},{2,1},{3,2},{5,4},{6,5},{7,6},{9,8},{10,9},{11,10},{13,12},{... | collective-permute-start | bytes 786440 | tf_op jit(solution)/shard_map/ppermute | solution.py:140
  22.2 3.5 %collective-permute-start.2 = (f32[64,128]{1,0:T(8,128)S(1)}, f32[64,128]{1,0:T(8,128)S(1)}, u32[]{:S(2)}, u32[]{:S(2)}) collective-permute-start(f32[64,128]{1,0:T(8,128)S(1)} %get-tuple-element.28), channel_id=1, source_target_pairs={{0,4},{4,0},{8,12},{12,8},{16,20},{20,16},{24,28},{28,24},{1,5},{5... | collective-permute-start | bytes 98312 | tf_op jit(solution)/shard_map/ppermute | solution.py:158
  25.7 5.9 %collective-permute-start.3 = (f32[64,128]{1,0:T(8,128)S(1)}, f32[64,128]{1,0:T(8,128)S(1)}, u32[]{:S(2)}, u32[]{:S(2)}) collective-permute-start(f32[64,128]{1,0:T(8,128)S(1)} %add.70), channel_id=1, source_target_pairs={{0,8},{4,12},{8,0},{12,4},{16,24},{20,28},{24,16},{28,20},{1,9},{5... | collective-permute-start | bytes 98312 | tf_op jit(solution)/shard_map/ppermute | solution.py:158
  28.1 16.9 %collective-permute-start.27 = (bf16[1,128,1024]{2,1,0:T(8,128)(2,1)S(1)}, bf16[1,128,1024]{2,1,0:T(8,128)(2,1)S(1)}, u32[]{:S(2)}, u32[]{:S(2)}) collective-permute-start(bf16[1,128,1024]{2,1,0:T(8,128)(2,1)S(1)} %get-tuple-element.48.refs_0_), channel_id=1, source_target_pairs={{0,1},{1,2},{2,3},{4,5},{5,6},{6,7},{8,9},{9,10},{10,11},{12,13},{... | collective-permute-start | bytes 786440 | tf_op jit(solution)/shard_map/ppermute | solution.py:140
  31.6 4.0 %collective-permute-start.4 = (f32[64,128]{1,0:T(8,128)S(1)}, f32[64,128]{1,0:T(8,128)S(1)}, u32[]{:S(2)}, u32[]{:S(2)}) collective-permute-start(f32[64,128]{1,0:T(8,128)S(1)} %add.71), channel_id=1, source_target_pairs={{0,16},{4,20},{8,24},{12,28},{16,0},{20,4},{24,8},{28,12},{1,17},{... | collective-permute-start | bytes 98312 | tf_op jit(solution)/shard_map/ppermute | solution.py:158
  33.1 12.0 %collective-permute-start.28 = (bf16[1,128,1024]{2,1,0:T(8,128)(2,1)S(1)}, bf16[1,128,1024]{2,1,0:T(8,128)(2,1)S(1)}, u32[]{:S(2)}, u32[]{:S(2)}) collective-permute-start(bf16[1,128,1024]{2,1,0:T(8,128)(2,1)S(1)} %get-tuple-element.48.refs_0_), channel_id=1, source_target_pairs={{1,0},{2,1},{3,2},{5,4},{6,5},{7,6},{9,8},{10,9},{11,10},{13,12},{... | collective-permute-start | bytes 786440 | tf_op jit(solution)/shard_map/ppermute | solution.py:140
  35.6 10.7 %collective-permute-start.17 = (bf16[1,128,1024]{2,1,0:T(8,128)(2,1)S(1)}, bf16[1,128,1024]{2,1,0:T(8,128)(2,1)S(1)}, u32[]{:S(2)}, u32[]{:S(2)}) collective-permute-start(bf16[1,128,1024]{2,1,0:T(8,128)(2,1)S(1)} %get-tuple-element.46.refs_0_), channel_id=1, source_target_pairs={{0,1},{1,2},{2,3},{4,5},{5,6},{6,7},{8,9},{9,10},{10,11},{12,13},{... | collective-permute-start | bytes 786440 | tf_op jit(solution)/shard_map/ppermute | solution.py:140
  39.1 9.1 %collective-permute-start.18 = (bf16[1,128,1024]{2,1,0:T(8,128)(2,1)S(1)}, bf16[1,128,1024]{2,1,0:T(8,128)(2,1)S(1)}, u32[]{:S(2)}, u32[]{:S(2)}) collective-permute-start(bf16[1,128,1024]{2,1,0:T(8,128)(2,1)S(1)} %get-tuple-element.46.refs_0_), channel_id=1, source_target_pairs={{1,0},{2,1},{3,2},{5,4},{6,5},{7,6},{9,8},{10,9},{11,10},{13,12},{... | collective-permute-start | bytes 786440 | tf_op jit(solution)/shard_map/ppermute | solution.py:140
  40.4 9.7 %collective-permute-start.6 = (bf16[1,128,1024]{2,1,0:T(8,128)(2,1)S(1)}, bf16[1,128,1024]{2,1,0:T(8,128)(2,1)S(1)}, u32[]{:S(2)}, u32[]{:S(2)}) collective-permute-start(bf16[1,128,1024]{2,1,0:T(8,128)(2,1)S(1)} %get-tuple-element.45.refs_0_), channel_id=1, source_target_pairs={{0,1},{1,2},{2,3},{4,5},{5,6},{6,7},{8,9},{9,10},{10,11},{12,13},{... | collective-permute-start | bytes 786440 | tf_op jit(solution)/shard_map/ppermute | solution.py:140
  44.9 45.6 %collective-permute-start.12 = (bf16[1024,512]{1,0:T(8,128)(2,1)}, bf16[1024,512]{1,0:T(8,128)(2,1)S(1)}, u32[]{:S(2)}, u32[]{:S(2)}) collective-permute-start(bf16[1024,512]{1,0:T(8,128)(2,1)} %get-tuple-element.22.refs_7_), channel_id=1, source_target_pairs={{0,4},{4,0},{8,12},{12,8},{16,20},{20,16},{24,28},{28,24},{1,5},{5... | collective-permute-start | bytes 3145736 | tf_op jit(solution)/shard_map/ppermute | solution.py:158
  45.0 10.6 %collective-permute-start.7 = (bf16[1,128,1024]{2,1,0:T(8,128)(2,1)S(1)}, bf16[1,128,1024]{2,1,0:T(8,128)(2,1)S(1)}, u32[]{:S(2)}, u32[]{:S(2)}) collective-permute-start(bf16[1,128,1024]{2,1,0:T(8,128)(2,1)S(1)} %get-tuple-element.45.refs_0_), channel_id=1, source_target_pairs={{1,0},{2,1},{3,2},{5,4},{6,5},{7,6},{9,8},{10,9},{11,10},{13,12},{... | collective-permute-start | bytes 786440 | tf_op jit(solution)/shard_map/ppermute | solution.py:140
  46.3 11.3 %collective-permute-start.39 = (bf16[1,128,1024]{2,1,0:T(8,128)(2,1)S(1)}, bf16[1,128,1024]{2,1,0:T(8,128)(2,1)}, u32[]{:S(2)}, u32[]{:S(2)}) collective-permute-start(bf16[1,128,1024]{2,1,0:T(8,128)(2,1)S(1)} %collective-permute-done.37.refs_1_), channel_id=1, source_target_pairs={{1,2},{2,3},{5,6},{6,7},{9,10},{10,11},{13,14},{14,15},{17,18},{18... | collective-permute-start | bytes 786440 | tf_op jit(solution)/shard_map/ppermute | solution.py:140
  48.1 13.4 %collective-permute-start.40 = (bf16[1,128,1024]{2,1,0:T(8,128)(2,1)S(1)}, bf16[1,128,1024]{2,1,0:T(8,128)(2,1)}, u32[]{:S(2)}, u32[]{:S(2)}) collective-permute-start(bf16[1,128,1024]{2,1,0:T(8,128)(2,1)S(1)} %collective-permute-done.38.refs_2_), channel_id=1, source_target_pairs={{1,0},{2,1},{5,4},{6,5},{9,8},{10,9},{13,12},{14,13},{17,16},{18,1... | collective-permute-start | bytes 786440 | tf_op jit(solution)/shard_map/ppermute | solution.py:140
  50.1 13.4 %collective-permute-start.29 = (bf16[1,128,1024]{2,1,0:T(8,128)(2,1)S(1)}, bf16[1,128,1024]{2,1,0:T(8,128)(2,1)S(1)}, u32[]{:S(2)}, u32[]{:S(2)}) collective-permute-start(bf16[1,128,1024]{2,1,0:T(8,128)(2,1)S(1)} %collective-permute-done.27.refs_1_), channel_id=1, source_target_pairs={{1,2},{2,3},{5,6},{6,7},{9,10},{10,11},{13,14},{14,15},{17,18},{18... | collective-permute-start | bytes 786440 | tf_op jit(solution)/shard_map/ppermute | solution.py:140
  55.6 12.5 %collective-permute-start.30 = (bf16[1,128,1024]{2,1,0:T(8,128)(2,1)S(1)}, bf16[1,128,1024]{2,1,0:T(8,128)(2,1)S(1)}, u32[]{:S(2)}, u32[]{:S(2)}) collective-permute-start(bf16[1,128,1024]{2,1,0:T(8,128)(2,1)S(1)} %collective-permute-done.28.refs_2_), channel_id=1, source_target_pairs={{1,0},{2,1},{5,4},{6,5},{9,8},{10,9},{13,12},{14,13},{17,16},{18,1... | collective-permute-start | bytes 786440 | tf_op jit(solution)/shard_map/ppermute | solution.py:140
  56.9 0.7 copy-start.10
  57.6 11.8 %collective-permute-start.19 = (bf16[1,128,1024]{2,1,0:T(8,128)(2,1)S(1)}, bf16[1,128,1024]{2,1,0:T(8,128)(2,1)S(1)}, u32[]{:S(2)}, u32[]{:S(2)}) collective-permute-start(bf16[1,128,1024]{2,1,0:T(8,128)(2,1)S(1)} %collective-permute-done.17.refs_1_), channel_id=1, source_target_pairs={{1,2},{2,3},{5,6},{6,7},{9,10},{10,11},{13,14},{14,15},{17,18},{18... | collective-permute-start | bytes 786440 | tf_op jit(solution)/shard_map/ppermute | solution.py:140
  61.5 12.6 %collective-permute-start.20 = (bf16[1,128,1024]{2,1,0:T(8,128)(2,1)S(1)}, bf16[1,128,1024]{2,1,0:T(8,128)(2,1)S(1)}, u32[]{:S(2)}, u32[]{:S(2)}) collective-permute-start(bf16[1,128,1024]{2,1,0:T(8,128)(2,1)S(1)} %collective-permute-done.18.refs_2_), channel_id=1, source_target_pairs={{1,0},{2,1},{5,4},{6,5},{9,8},{10,9},{13,12},{14,13},{17,16},{18,1... | collective-permute-start | bytes 786440 | tf_op jit(solution)/shard_map/ppermute | solution.py:140
  63.5 10.7 %copy-start.16 = (bf16[1,128,1024]{2,1,0:T(8,128)(2,1)}, bf16[1,128,1024]{2,1,0:T(8,128)(2,1)S(1)}, u32[]{:S(2)}) copy-start(bf16[1,128,1024]{2,1,0:T(8,128)(2,1)S(1)} %collective-permute-done.29.refs_3_) | copy-start | bytes 786436
  63.5 12.7 %collective-permute-start.8 = (bf16[1,128,1024]{2,1,0:T(8,128)(2,1)S(1)}, bf16[1,128,1024]{2,1,0:T(8,128)(2,1)}, u32[]{:S(2)}, u32[]{:S(2)}) collective-permute-start(bf16[1,128,1024]{2,1,0:T(8,128)(2,1)S(1)} %collective-permute-done.6.refs_1_), channel_id=1, source_target_pairs={{1,2},{2,3},{5,6},{6,7},{9,10},{10,11},{13,14},{14,15},{17,18},{18... | collective-permute-start | bytes 786440 | tf_op jit(solution)/shard_map/ppermute | solution.py:140
  68.2 6.0 %copy-start.18 = (bf16[1,128,1024]{2,1,0:T(8,128)(2,1)}, bf16[1,128,1024]{2,1,0:T(8,128)(2,1)S(1)}, u32[]{:S(2)}) copy-start(bf16[1,128,1024]{2,1,0:T(8,128)(2,1)S(1)} %collective-permute-done.30.refs_4_) | copy-start | bytes 786436
  68.2 14.8 %collective-permute-start.9 = (bf16[1,128,1024]{2,1,0:T(8,128)(2,1)S(1)}, bf16[1,128,1024]{2,1,0:T(8,128)(2,1)}, u32[]{:S(2)}, u32[]{:S(2)}) collective-permute-start(bf16[1,128,1024]{2,1,0:T(8,128)(2,1)S(1)} %collective-permute-done.7.refs_2_), channel_id=1, source_target_pairs={{1,0},{2,1},{5,4},{6,5},{9,8},{10,9},{13,12},{14,13},{17,16},{18,1... | collective-permute-start | bytes 786440 | tf_op jit(solution)/shard_map/ppermute | solution.py:140
  69.5 4.7 %copy-start.12 = (bf16[1,128,1024]{2,1,0:T(8,128)(2,1)}, bf16[1,128,1024]{2,1,0:T(8,128)(2,1)S(1)}, u32[]{:S(2)}) copy-start(bf16[1,128,1024]{2,1,0:T(8,128)(2,1)S(1)} %collective-permute-done.19.refs_3_) | copy-start | bytes 786436
  69.5 14.8 %collective-permute-start.41 = (bf16[1,128,1024]{2,1,0:T(8,128)(2,1)}, bf16[1,128,1024]{2,1,0:T(8,128)(2,1)}, u32[]{:S(2)}, u32[]{:S(2)}) collective-permute-start(bf16[1,128,1024]{2,1,0:T(8,128)(2,1)} %collective-permute-done.39.refs_3_), channel_id=1, source_target_pairs={{2,3},{6,7},{10,11},{14,15},{18,19},{22,23},{26,27},{30,31}} | collective-permute-start | bytes 786440 | tf_op jit(solution)/shard_map/ppermute | solution.py:140
  74.9 13.7 %collective-permute-start.42 = (bf16[1,128,1024]{2,1,0:T(8,128)(2,1)}, bf16[1,128,1024]{2,1,0:T(8,128)(2,1)}, u32[]{:S(2)}, u32[]{:S(2)}) collective-permute-start(bf16[1,128,1024]{2,1,0:T(8,128)(2,1)} %collective-permute-done.40.refs_4_), channel_id=1, source_target_pairs={{1,0},{5,4},{9,8},{13,12},{17,16},{21,20},{25,24},{29,28}} | collective-permute-start | bytes 786440 | tf_op jit(solution)/shard_map/ppermute | solution.py:140
  76.2 15.0 %collective-permute-start.31 = (bf16[1,128,1024]{2,1,0:T(8,128)(2,1)}, bf16[1,128,1024]{2,1,0:T(8,128)(2,1)S(1)}, u32[]{:S(2)}, u32[]{:S(2)}) collective-permute-start(bf16[1,128,1024]{2,1,0:T(8,128)(2,1)} %copy-done.16), channel_id=1, source_target_pairs={{2,3},{6,7},{10,11},{14,15},{18,19},{22,23},{26,27},{30,31}} | collective-permute-start | bytes 786440 | tf_op jit(solution)/shard_map/ppermute | solution.py:140
  83.0 19.1 %collective-permute-start.32 = (bf16[1,128,1024]{2,1,0:T(8,128)(2,1)}, bf16[1,128,1024]{2,1,0:T(8,128)(2,1)S(1)}, u32[]{:S(2)}, u32[]{:S(2)}) collective-permute-start(bf16[1,128,1024]{2,1,0:T(8,128)(2,1)} %copy-done.18), channel_id=1, source_target_pairs={{1,0},{5,4},{9,8},{13,12},{17,16},{21,20},{25,24},{29,28}} | collective-permute-start | bytes 786440 | tf_op jit(solution)/shard_map/ppermute | solution.py:140
  84.3 25.6 %collective-permute-start.21 = (bf16[1,128,1024]{2,1,0:T(8,128)(2,1)}, bf16[1,128,1024]{2,1,0:T(8,128)(2,1)S(1)}, u32[]{:S(2)}, u32[]{:S(2)}) collective-permute-start(bf16[1,128,1024]{2,1,0:T(8,128)(2,1)} %copy-done.12), channel_id=1, source_target_pairs={{2,3},{6,7},{10,11},{14,15},{18,19},{22,23},{26,27},{30,31}} | collective-permute-start | bytes 786440 | tf_op jit(solution)/shard_map/ppermute | solution.py:140
  88.6 22.8 %collective-permute-start.22 = (bf16[1,128,1024]{2,1,0:T(8,128)(2,1)}, bf16[1,128,1024]{2,1,0:T(8,128)(2,1)S(1)}, u32[]{:S(2)}, u32[]{:S(2)}) collective-permute-start(bf16[1,128,1024]{2,1,0:T(8,128)(2,1)} %copy-done.14), channel_id=1, source_target_pairs={{1,0},{5,4},{9,8},{13,12},{17,16},{21,20},{25,24},{29,28}} | collective-permute-start | bytes 786440 | tf_op jit(solution)/shard_map/ppermute | solution.py:140
  90.5 27.5 %collective-permute-start.10 = (bf16[1,128,1024]{2,1,0:T(8,128)(2,1)}, bf16[1,128,1024]{2,1,0:T(8,128)(2,1)S(1)}, u32[]{:S(2)}, u32[]{:S(2)}) collective-permute-start(bf16[1,128,1024]{2,1,0:T(8,128)(2,1)} %collective-permute-done.8.refs_3_), channel_id=1, source_target_pairs={{2,3},{6,7},{10,11},{14,15},{18,19},{22,23},{26,27},{30,31}} | collective-permute-start | bytes 786440 | tf_op jit(solution)/shard_map/ppermute | solution.py:140
  91.2 27.6 %collective-permute-start.11 = (bf16[1,128,1024]{2,1,0:T(8,128)(2,1)}, bf16[1,128,1024]{2,1,0:T(8,128)(2,1)S(1)}, u32[]{:S(2)}, u32[]{:S(2)}) collective-permute-start(bf16[1,128,1024]{2,1,0:T(8,128)(2,1)} %collective-permute-done.9.refs_4_), channel_id=1, source_target_pairs={{1,0},{5,4},{9,8},{13,12},{17,16},{21,20},{25,24},{29,28}} | collective-permute-start | bytes 786440 | tf_op jit(solution)/shard_map/ppermute | solution.py:140
  92.5 1.2 copy-start.5
  93.7 0.9 copy-start.7
  94.7 8.9 %copy-start.11 = (bf16[1,128,1024]{2,1,0:T(8,128)(2,1)S(1)}, bf16[1,128,1024]{2,1,0:T(8,128)(2,1)}, u32[]{:S(2)}) copy-start(bf16[1,128,1024]{2,1,0:T(8,128)(2,1)} %copy-done.10) | copy-start | bytes 786436
  94.7 8.9 %copy-start.17 = (bf16[1,128,1024]{2,1,0:T(8,128)(2,1)S(1)}, bf16[1,128,1024]{2,1,0:T(8,128)(2,1)}, u32[]{:S(2)}) copy-start(bf16[1,128,1024]{2,1,0:T(8,128)(2,1)} %copy-done.16) | copy-start | bytes 786436
  94.7 8.9 %copy-start.19 = (bf16[1,128,1024]{2,1,0:T(8,128)(2,1)S(1)}, bf16[1,128,1024]{2,1,0:T(8,128)(2,1)}, u32[]{:S(2)}) copy-start(bf16[1,128,1024]{2,1,0:T(8,128)(2,1)} %copy-done.18) | copy-start | bytes 786436
  102.1 9.8 %copy-start.9 = (bf16[1,128,1024]{2,1,0:T(8,128)(2,1)S(1)}, bf16[1,128,1024]{2,1,0:T(8,128)(2,1)}, u32[]{:S(2)}) copy-start(bf16[1,128,1024]{2,1,0:T(8,128)(2,1)} %copy-done.8) | copy-start | bytes 786436
  102.1 9.7 %copy-start.13 = (bf16[1,128,1024]{2,1,0:T(8,128)(2,1)S(1)}, bf16[1,128,1024]{2,1,0:T(8,128)(2,1)}, u32[]{:S(2)}) copy-start(bf16[1,128,1024]{2,1,0:T(8,128)(2,1)} %copy-done.12) | copy-start | bytes 786436
  102.1 9.7 %copy-start.15 = (bf16[1,128,1024]{2,1,0:T(8,128)(2,1)S(1)}, bf16[1,128,1024]{2,1,0:T(8,128)(2,1)}, u32[]{:S(2)}) copy-start(bf16[1,128,1024]{2,1,0:T(8,128)(2,1)} %copy-done.14) | copy-start | bytes 786436
  102.1 25.4 %collective-permute-start.45 = (bf16[2,128,512]{2,1,0:T(8,128)(2,1)S(1)}, bf16[2,128,512]{2,1,0:T(8,128)(2,1)S(1)}, u32[]{:S(2)}, u32[]{:S(2)}) collective-permute-start(bf16[2,128,512]{2,1,0:T(8,128)(2,1)S(1)} %get-tuple-element.44), channel_id=1, source_target_pairs={{0,16},{4,20},{8,24},{12,28},{16,0},{20,4},{24,8},{28,12},{1,17},{... | collective-permute-start | bytes 786440 | tf_op jit(solution)/shard_map/ppermute | solution.py:158
  109.9 19.3 %collective-permute-start.43 = (bf16[2,128,512]{2,1,0:T(8,128)(2,1)S(1)}, bf16[2,128,512]{2,1,0:T(8,128)(2,1)S(1)}, u32[]{:S(2)}, u32[]{:S(2)}) collective-permute-start(bf16[2,128,512]{2,1,0:T(8,128)(2,1)S(1)} %get-tuple-element.42), channel_id=1, source_target_pairs={{0,8},{4,12},{8,0},{12,4},{16,24},{20,28},{24,16},{28,20},{1,9},{5... | collective-permute-start | bytes 786440 | tf_op jit(solution)/shard_map/ppermute | solution.py:158
  111.4 18.4 %collective-permute-start.35 = (bf16[2,128,512]{2,1,0:T(8,128)(2,1)S(1)}, bf16[2,128,512]{2,1,0:T(8,128)(2,1)S(1)}, u32[]{:S(2)}, u32[]{:S(2)}) collective-permute-start(bf16[2,128,512]{2,1,0:T(8,128)(2,1)S(1)} %get-tuple-element.40), channel_id=1, source_target_pairs={{0,16},{4,20},{8,24},{12,28},{16,0},{20,4},{24,8},{28,12},{1,17},{... | collective-permute-start | bytes 786440 | tf_op jit(solution)/shard_map/ppermute | solution.py:158
  118.1 12.6 %collective-permute-start.33 = (bf16[2,128,512]{2,1,0:T(8,128)(2,1)S(1)}, bf16[2,128,512]{2,1,0:T(8,128)(2,1)S(1)}, u32[]{:S(2)}, u32[]{:S(2)}) collective-permute-start(bf16[2,128,512]{2,1,0:T(8,128)(2,1)S(1)} %get-tuple-element.38), channel_id=1, source_target_pairs={{0,8},{4,12},{8,0},{12,4},{16,24},{20,28},{24,16},{28,20},{1,9},{5... | collective-permute-start | bytes 786440 | tf_op jit(solution)/shard_map/ppermute | solution.py:158
  118.9 13.3 %collective-permute-start.25 = (bf16[2,128,512]{2,1,0:T(8,128)(2,1)S(1)}, bf16[2,128,512]{2,1,0:T(8,128)(2,1)S(1)}, u32[]{:S(2)}, u32[]{:S(2)}) collective-permute-start(bf16[2,128,512]{2,1,0:T(8,128)(2,1)S(1)} %get-tuple-element.36), channel_id=1, source_target_pairs={{0,16},{4,20},{8,24},{12,28},{16,0},{20,4},{24,8},{28,12},{1,17},{... | collective-permute-start | bytes 786440 | tf_op jit(solution)/shard_map/ppermute | solution.py:158
  127.6 9.3 %collective-permute-start.23 = (bf16[2,128,512]{2,1,0:T(8,128)(2,1)S(1)}, bf16[2,128,512]{2,1,0:T(8,128)(2,1)S(1)}, u32[]{:S(2)}, u32[]{:S(2)}) collective-permute-start(bf16[2,128,512]{2,1,0:T(8,128)(2,1)S(1)} %get-tuple-element.34), channel_id=1, source_target_pairs={{0,8},{4,12},{8,0},{12,4},{16,24},{20,28},{24,16},{28,20},{1,9},{5... | collective-permute-start | bytes 786440 | tf_op jit(solution)/shard_map/ppermute | solution.py:158
  129.2 9.3 %collective-permute-start.15 = (bf16[2,128,512]{2,1,0:T(8,128)(2,1)S(1)}, bf16[2,128,512]{2,1,0:T(8,128)(2,1)S(1)}, u32[]{:S(2)}, u32[]{:S(2)}) collective-permute-start(bf16[2,128,512]{2,1,0:T(8,128)(2,1)S(1)} %get-tuple-element.32), channel_id=1, source_target_pairs={{0,16},{4,20},{8,24},{12,28},{16,0},{20,4},{24,8},{28,12},{1,17},{... | collective-permute-start | bytes 786440 | tf_op jit(solution)/shard_map/ppermute | solution.py:158
  129.8 12.0 %collective-permute-start.13 = (bf16[2,128,512]{2,1,0:T(8,128)(2,1)S(1)}, bf16[2,128,512]{2,1,0:T(8,128)(2,1)S(1)}, u32[]{:S(2)}, u32[]{:S(2)}) collective-permute-start(bf16[2,128,512]{2,1,0:T(8,128)(2,1)S(1)} %get-tuple-element.30), channel_id=1, source_target_pairs={{0,8},{4,12},{8,0},{12,4},{16,24},{20,28},{24,16},{28,20},{1,9},{5... | collective-permute-start | bytes 786440 | tf_op jit(solution)/shard_map/ppermute | solution.py:158
  130.7 12.7 %collective-permute-start.46 = (bf16[1,128,512]{2,1,0:T(8,128)(2,1)S(1)}, bf16[1,128,512]{2,1,0:T(8,128)(2,1)S(1)}, u32[]{:S(2)}, u32[]{:S(2)}) collective-permute-start(bf16[1,128,512]{2,1,0:T(8,128)(2,1)S(1)} %slice.196), channel_id=1, source_target_pairs={{0,8},{4,12},{8,0},{12,4},{16,24},{20,28},{24,16},{28,20},{1,9},{5... | collective-permute-start | bytes 393224 | tf_op jit(solution)/shard_map/ppermute | solution.py:158
  132.2 12.2 %collective-permute-start.44 = (bf16[1,128,512]{2,1,0:T(8,128)(2,1)S(1)}, bf16[1,128,512]{2,1,0:T(8,128)(2,1)S(1)}, u32[]{:S(2)}, u32[]{:S(2)}) collective-permute-start(bf16[1,128,512]{2,1,0:T(8,128)(2,1)S(1)} %slice.197), channel_id=1, source_target_pairs={{0,16},{4,20},{8,24},{12,28},{16,0},{20,4},{24,8},{28,12},{1,17},{... | collective-permute-start | bytes 393224 | tf_op jit(solution)/shard_map/ppermute | solution.py:158
  136.9 8.4 %collective-permute-start.36 = (bf16[1,128,512]{2,1,0:T(8,128)(2,1)S(1)}, bf16[1,128,512]{2,1,0:T(8,128)(2,1)S(1)}, u32[]{:S(2)}, u32[]{:S(2)}) collective-permute-start(bf16[1,128,512]{2,1,0:T(8,128)(2,1)S(1)} %slice.198), channel_id=1, source_target_pairs={{0,8},{4,12},{8,0},{12,4},{16,24},{20,28},{24,16},{28,20},{1,9},{5... | collective-permute-start | bytes 393224 | tf_op jit(solution)/shard_map/ppermute | solution.py:158
  138.5 8.4 %collective-permute-start.34 = (bf16[1,128,512]{2,1,0:T(8,128)(2,1)S(1)}, bf16[1,128,512]{2,1,0:T(8,128)(2,1)S(1)}, u32[]{:S(2)}, u32[]{:S(2)}) collective-permute-start(bf16[1,128,512]{2,1,0:T(8,128)(2,1)S(1)} %slice.199), channel_id=1, source_target_pairs={{0,16},{4,20},{8,24},{12,28},{16,0},{20,4},{24,8},{28,12},{1,17},{... | collective-permute-start | bytes 393224 | tf_op jit(solution)/shard_map/ppermute | solution.py:158
  141.8 5.2 %collective-permute-start.26 = (bf16[1,128,512]{2,1,0:T(8,128)(2,1)S(1)}, bf16[1,128,512]{2,1,0:T(8,128)(2,1)S(1)}, u32[]{:S(2)}, u32[]{:S(2)}) collective-permute-start(bf16[1,128,512]{2,1,0:T(8,128)(2,1)S(1)} %slice.200), channel_id=1, source_target_pairs={{0,8},{4,12},{8,0},{12,4},{16,24},{20,28},{24,16},{28,20},{1,9},{5... | collective-permute-start | bytes 393224 | tf_op jit(solution)/shard_map/ppermute | solution.py:158
  143.3 5.0 %collective-permute-start.24 = (bf16[1,128,512]{2,1,0:T(8,128)(2,1)S(1)}, bf16[1,128,512]{2,1,0:T(8,128)(2,1)S(1)}, u32[]{:S(2)}, u32[]{:S(2)}) collective-permute-start(bf16[1,128,512]{2,1,0:T(8,128)(2,1)S(1)} %slice.201), channel_id=1, source_target_pairs={{0,16},{4,20},{8,24},{12,28},{16,0},{20,4},{24,8},{28,12},{1,17},{... | collective-permute-start | bytes 393224 | tf_op jit(solution)/shard_map/ppermute | solution.py:158
  144.4 5.0 %collective-permute-start.16 = (bf16[1,128,512]{2,1,0:T(8,128)(2,1)S(1)}, bf16[1,128,512]{2,1,0:T(8,128)(2,1)S(1)}, u32[]{:S(2)}, u32[]{:S(2)}) collective-permute-start(bf16[1,128,512]{2,1,0:T(8,128)(2,1)S(1)} %slice.202), channel_id=1, source_target_pairs={{0,8},{4,12},{8,0},{12,4},{16,24},{20,28},{24,16},{28,20},{1,9},{5... | collective-permute-start | bytes 393224 | tf_op jit(solution)/shard_map/ppermute | solution.py:158
  145.3 5.0 %collective-permute-start.14 = (bf16[1,128,512]{2,1,0:T(8,128)(2,1)S(1)}, bf16[1,128,512]{2,1,0:T(8,128)(2,1)S(1)}, u32[]{:S(2)}, u32[]{:S(2)}) collective-permute-start(bf16[1,128,512]{2,1,0:T(8,128)(2,1)S(1)} %slice.203), channel_id=1, source_target_pairs={{0,16},{4,20},{8,24},{12,28},{16,0},{20,4},{24,8},{28,12},{1,17},{... | collective-permute-start | bytes 393224 | tf_op jit(solution)/shard_map/ppermute | solution.py:158
  (3 other events, 2.1 us)
where the time goes:
time: 153 us; the launch traced here: 152 us
  starting transfers between devices  67.9 us (44%)
  waiting for transfers between devices  35.8 us (23%)
  Pallas kernels  34.8 us (23%)
  local copies, waits for them, and re-layouts  6.57 us (4%)
  other arithmetic  5.35 us (3%)
    ppermute x24, starting transfers between devices, along(): lax.ppermute(value, axis, [(i, i + step) for i in range(count) if low <=...  39.2 us
    pallas_call x4, Pallas kernels, product_call(): pl.pallas_call(functools.partial(product_kernel, tp_count, orders, offset...  27 us
    ppermute x21, starting transfers between devices, flip(): lax.ppermute(array, 'ctx', [(i, i ^ distance) for i in range(ctx_count)])  25.4 us
    ppermute x24, waiting for transfers between devices, along(): lax.ppermute(value, axis, [(i, i + step) for i in range(count) if low <=...  24.8 us
    ppermute x21, waiting for transfers between devices, flip(): lax.ppermute(array, 'ctx', [(i, i ^ distance) for i in range(ctx_count)])  11 us
    pallas_call x1, Pallas kernels, conv_call(): pl.pallas_call(functools.partial(conv_kernel, width, taps), grid=(groups...  7.76 us
    unnamed x40, local copies, waits for them, and re-layouts  5 us
  transfers between devices with their start and end apart: 47, of which 14 were waited for; matrix products, arithmetic and copies ran while one was open for 3% of the time, Pallas kernels for 23%

commit v1 on v0

v1 whole, which is shorter than its diff:
```python
import functools
import jax, jax.numpy as jnp
from jax import lax
from jax.experimental import pallas as pl
from jax.experimental.pallas import tpu as pltpu
from jax.sharding import PartitionSpec as P

F32, BF16 = jnp.float32, jnp.bfloat16
SHARES, TILE = (12, 11, 9), 512

def conv_kernel(width, taps, q_ref, k_ref, v_ref, go_ref, kvh_ref, ggh_ref, f_ref, after_ref, gq_ref, gk_ref, gv_ref, gf_ref, turned_ref, low_ref, high_ref):
    del after_ref
    rows, toks = q_ref.shape
    blocks = toks // taps
    for g in range(rows // width):
        r = slice(g * width, (g + 1) * width)
        k = k_ref[r, :].astype(F32)
        v = v_ref[r, :].astype(F32)
        go = go_ref[r, :].astype(F32)
        kv = (k * v).astype(BF16)
        gg = (q_ref[r, :].astype(F32) * go).astype(BF16)
        kvb = [kvh_ref[r, :]] + [kv[:, n * taps:(n + 1) * taps] for n in range(blocks)]
        ggb = [gg[:, n * taps:(n + 1) * taps] for n in range(blocks)] + [ggh_ref[r, :]]
        f = f_ref[g:g + 1, :].astype(F32)
        padded = jnp.concatenate([f, jnp.zeros_like(f)], axis=1)
        band = pltpu.roll(jnp.broadcast_to(padded, (taps, 2 * taps)), 0, 1, stride=1, stride_axis=0).astype(BF16)
        kv_all = jnp.concatenate(kvb, axis=0)
        y = jnp.dot(kv_all, band, preferred_element_type=F32)
        conv = jnp.concatenate(
            [y[(n + 1) * width:(n + 2) * width, :taps] + y[n * width:(n + 1) * width, taps:] for n in range(blocks)], axis=1)
        gq_ref[r, :] = (go * conv).astype(BF16)
        pairs = jnp.concatenate([jnp.concatenate(ggb[:-1], axis=0), jnp.concatenate(ggb[1:], axis=0)], axis=1)
        m = lax.dot_general(pairs, band, (((1,), (1,)), ((), ())), preferred_element_type=F32)
        mixed = jnp.concatenate([m[n * width:(n + 1) * width] for n in range(blocks)], axis=1)
        gk_ref[r, :] = (mixed * v).astype(BF16)
        gv_ref[r, :] = (mixed * k).astype(BF16)
        x = lax.dot_general(kv_all[width:], pairs, (((0,), (0,)), ((), ())), preferred_element_type=F32)
        total = x[:8]
        for a in range(8, taps, 8):
            total = total + pltpu.roll(x[a:a + 8], 2 * taps - a, 1)
        low_ref[8 * g:8 * g + 8, :] = total[:, :taps]
        high_ref[8 * g:8 * g + 8, :] = total[:, taps:]
    turned_ref[...] = gv_ref[...].T
    lags = rows // width
    total = low_ref[pl.ds(0, lags, stride=8), :]
    for b in range(1, 8):
        both = jnp.concatenate([ref[pl.ds(b, lags, stride=8), :] for ref in (low_ref, high_ref)], axis=1)
        total = total + pltpu.roll(both, 2 * taps - b, 1)[:, :taps]
    gf_ref[...] = total

def conv_call(query, key, value, grad_out, kvh, ggh, filters, after, step=8):
    channels, toks = key.shape
    groups, taps = filters.shape
    width = channels // groups
    rows = step * width
    wide = pl.BlockSpec((rows, toks), lambda i: (i, 0))
    halo = pl.BlockSpec((rows, taps), lambda i: (i, 0))
    filt = pl.BlockSpec((step, taps), lambda i: (i, 0))
    big = jax.ShapeDtypeStruct((channels, toks), BF16)
    return pl.pallas_call(
        functools.partial(conv_kernel, width, taps),
        grid=(groups // step,),
        in_specs=[wide] * 4 + [halo] * 2 + [filt, pl.BlockSpec(memory_space=pl.ANY)],
        out_specs=[wide] * 3 + [filt, pl.BlockSpec((toks, rows), lambda i: (0, i))],
        out_shape=[big] * 3 + [jax.ShapeDtypeStruct((groups, taps), F32), jax.ShapeDtypeStruct((toks, channels), BF16)],
        scratch_shapes=[pltpu.VMEM((8 * step, taps), F32)] * 2,
        compiler_params=pltpu.CompilerParams(vmem_limit_bytes=48 * 2**20),
        cost_estimate=pl.CostEstimate(
            flops=8 * channels * toks * 2 * taps, bytes_accessed=16 * channels * toks, transcendentals=0
        ),
        name="conv",
    )(query, key, value, grad_out, kvh, ggh, filters, after)


def first_leaves(relative, bits):
    index = 0
    for bit in bits[1:]:
        index = index * 2 + ((relative >> bit) & 1)
    return ((relative >> bits[0]) & 1) == 1, index


def product_kernel(orders, count, spot_ref, *refs):
    sources, (own_ref, sibling_ref), outs, rows_ref = refs[:count], refs[count : count + 2], refs[-1 - 2 * len(orders) : -1], refs[-1]
    blocks, size, _ = rows_ref.shape
    toks = own_ref.shape[0]

    @pl.when(pl.program_id(0) == 0)
    def _():
        entry = 1
        for source in sources:
            for element in range(source.shape[0]):
                owner = spot_ref[entry]
                entry += 1

                @pl.when(owner >= 0)
                def _():
                    for part in range(source.shape[1]):
                        rows_ref[(owner * source.shape[1] + part) ^ spot_ref[0]] = source[element, part]

    rows = rows_ref[...].reshape(blocks * size, 2 * toks)
    total = jnp.dot(rows[:, :toks], own_ref[...], preferred_element_type=F32)
    total = total + jnp.dot(rows[:, toks:], sibling_ref[...], preferred_element_type=F32)
    side = pl.program_id(0) // (pl.num_programs(0) // len(orders))
    for order, bits in enumerate(orders):

        @pl.when(side == order)
        def _():
            for relative in range(blocks):
                goes, index = first_leaves(relative, bits)
                block = total[relative * size : (relative + 1) * size]
                if goes:
                    outs[2 * order][index] = block.astype(BF16)
                else:
                    outs[2 * order + 1][index] = block


def product_call(orders, blocks, spot, sources, own, sibling, after):
    toks, channels = own.shape
    size = sources[0].shape[2]
    tile = min(TILE, channels // 2)
    steps = channels // tile
    run = steps // len(orders)
    half = blocks // 2
    tokens = pl.BlockSpec((toks, tile), lambda i, s: (0, i))
    sides = [
        pl.BlockSpec((half, size, tile), lambda i, s, begin=n * run: (0, 0, jnp.clip(i - begin, 0, run - 1)))
        for n in range(len(orders))
    ]
    shape = (half, size, channels // len(orders))
    return pl.pallas_call(
        functools.partial(product_kernel, orders, len(sources)),
        grid_spec=pltpu.PrefetchScalarGridSpec(
            num_scalar_prefetch=1,
            grid=(steps,),
            in_specs=[pl.BlockSpec(a.shape, lambda i, s: (0, 0, 0, 0)) for a in sources]
            + [tokens] * 2
            + [pl.BlockSpec(memory_space=pl.ANY)] * len(after),
            out_specs=[side for side in sides for _ in range(2)],
            scratch_shapes=[pltpu.VMEM((blocks, size, 2 * toks), BF16)],
        ),
        out_shape=[jax.ShapeDtypeStruct(shape, kind) for kind in (BF16, F32) * len(orders)],
        compiler_params=pltpu.CompilerParams(vmem_limit_bytes=40 * 2**20),
        cost_estimate=pl.CostEstimate(
            flops=4 * blocks * size * channels * toks,
            bytes_accessed=sum(a.size for a in sources) * 2 + own.size * 4 + blocks * size * channels * 3,
            transcendentals=0,
        ),
        name="product",
    )(spot, *sources, own, sibling, *after)


def owners_of(z, count):
    if count == 1:
        return [z]
    group = count // 2
    return owners_of(z, group) + owners_of(facing(z, group), group)


def facing(z, group):
    return jnp.where((z // group) % 2 == 0, (z // group + 1) * group, (z // group) * group - 1)


def hop_pairs(count, group, hop):
    pairs = []
    for base in range(0, count, 2 * group):
        low, high = base + group - 1 - hop, base + group + hop
        pairs += [(low, high), (high, low)] if hop == 0 else [(low + 1, low), (high - 1, high)]
    return pairs


def hop_of(z, group):
    return jnp.where((z // group) % 2 == 0, group - 1 - z % group, z % group)


def gather_groups(piece, axis):
    count, z = lax.axis_size(axis), lax.axis_index(axis)
    stack, owners, group = piece, [z], 1
    while 2 * group < count:
        merged = arrived = lax.ppermute(stack, axis, hop_pairs(count, group, 0))
        for hop in range(1, group):
            arrived = lax.ppermute(arrived, axis, hop_pairs(count, group, hop))
            merged = jnp.where(hop_of(z, group) == hop, arrived, merged)
        stack = [stack, merged] if 4 * group >= count else jnp.concatenate([stack, merged], axis=0)
        owners = owners + owners_of(facing(z, group), group)
        group *= 2
    return stack, owners


def gather_swap(stack, owners, axis):
    count, z = lax.axis_size(axis), lax.axis_index(axis)
    group = count // 2
    arrived = lax.ppermute(stack, axis, hop_pairs(count, group, 0))
    return [stack, arrived], owners + [jnp.where(hop_of(z, group) == 0, owner, -1) for owner in owners_of(facing(z, group), group)]


def gather_rest(arrays, owners, axis, after):
    count, z = lax.axis_size(axis), lax.axis_index(axis)
    group, arrived = count // 2, tied(arrays[-1], after)
    for hop in range(1, group):
        arrived = lax.ppermute(arrived, axis, hop_pairs(count, group, hop))
        arrays = arrays + [arrived]
        owners = owners + [jnp.where(hop_of(z, group) == hop, owner, -1) for owner in owners_of(facing(z, group), group)]
    return arrays, owners


def tied(array, after):
    return lax.optimization_barrier((array, *after))[0] if after else array


def chunk_sizes(rows):
    sizes = [max(16, rows * share // 32 // 16 * 16) for share in SHARES[:-1]]
    return sizes + [rows - sum(sizes)]


def shards(saved_input, query, key, value, grad_out, filters):
    channels, toks = key.shape
    groups, taps = filters.shape
    width = channels // groups
    ctx_count, tp_count = lax.axis_size("ctx"), lax.axis_size("tp")
    ctx = lax.axis_index("ctx")
    chip, core = ctx // 2, ctx % 2
    chips = ctx_count // 2
    bits = tuple(range(chips.bit_length() - 1))
    across = (bits, bits[::-1])
    total_tokens = toks * ctx_count

    def flip(array, distance):
        return lax.ppermute(array, "ctx", [(i, i ^ distance) for i in range(ctx_count)])

    parts = chips // tp_count
    rows = saved_input.shape[0] // (2 * parts)
    by_core = saved_input.reshape(parts, 2, rows, toks)
    mine = lax.dynamic_index_in_dim(by_core, core, 1, keepdims=False)
    theirs = lax.dynamic_index_in_dim(by_core, 1 - core, 1, keepdims=False)
    received = flip(theirs, 1)
    sizes = chunk_sizes(rows)
    parted = []
    for low, high in ((0, sizes[0]), (sizes[0], rows)):
        piece = jnp.concatenate([mine[:, low:high], received[:, low:high]], axis=2)[None]
        halves, owners = gather_groups(piece, "tp")
        parted.append(halves)

    def product(a, b):
        return (a.astype(F32) * b.astype(F32)).astype(BF16)

    before = product(key[:, toks - taps :], value[:, toks - taps :])
    after = product(query[:, :taps], grad_out[:, :taps])
    kvh = lax.ppermute(before, "ctx", [(i, i + 1) for i in range(ctx_count - 1)])
    ggh = lax.ppermute(after, "ctx", [(i + 1, i) for i in range(ctx_count - 1)])

    grad_query, grad_key, grad_value, lag_sums, turned = conv_call(
        query, key, value, grad_out, kvh, ggh, filters, parted[0][1]
    )
    sibling = flip(turned, 1)
    stacks, start = [jnp.concatenate(parted[0], axis=0)], 0
    halves = lax.optimization_barrier((*parted[1], lag_sums))[:2]
    for size in sizes[1:]:
        stacks.append(jnp.concatenate([half[:, :, start : start + size] for half in halves], axis=0))
        start += size

    done, products, sums = [], [], []
    swapped = [gather_swap(stack, owners, "tp") for stack in stacks]
    for number, state in enumerate(swapped):
        arrays, holders = gather_rest(*state, "tp", products[-2:-1] if number else stacks[1:])
        ahead = [arrays[-1] for arrays, _ in swapped[number + 1 : number + 2]]
        orders = across
        spot = jnp.stack([chip] + holders).astype(jnp.int32)
        outs = product_call(orders, chips, spot, arrays, turned, sibling, products[-1:] + ahead)
        products.append(outs[0])
        columns, sums = [], []
        for order, path in enumerate(orders):
            send, keep = outs[2 * order], outs[2 * order + 1]
            for stage, bit in enumerate(path):
                keep = keep + flip(send, 2 << bit).astype(F32)
                if stage + 1 < len(path):
                    count = keep.shape[0] // 2
                    send, keep = keep[count:].astype(BF16), keep[:count]
                    sums.append(send)
            columns.append(keep[0] * total_tokens ** (-0.5))
        done.append(jnp.concatenate(columns, axis=1))
    lag_sums, distance = tied(lag_sums, products[-2:-1]), 1
    while distance < ctx_count:
        lag_sums = lag_sums + flip(lag_sums, distance)
        distance *= 2
    grad_filters = lag_sums * (total_tokens * width) ** (-0.5)
    grad_weight = jnp.concatenate(done, axis=0)
    return (grad_query, grad_key, grad_value, grad_filters, grad_weight)


def solution(mesh):
    placed = (P("tp", "ctx"),) * 5 + (P("tp", None),)
    return jax.shard_map(
        shards,
        mesh=mesh,
        in_specs=placed,
        out_specs=(P("tp", "ctx"),) * 3 + (P("tp", None), P("ctx", "tp")),
        check_vma=False,
    )
```

time: 153 us -> 123 us (0.80)
  starting transfers between devices: 67.9 us -> 31.9 us
  waiting for transfers between devices: 35.8 us -> 64.1 us
  Pallas kernels: 34.8 us -> 20.5 us
  local copies, waits for them, and re-layouts: 6.57 us -> 1.69 us
  other arithmetic: 5.35 us -> 3.43 us
    ppermute x24 -> x8, starting transfers between devices: 39.2 us -> 11.6 us  [the longest x3 4.6 us: gather_swap(): arrived = lax.ppermute(stack, axis, hop_pairs(count, group, 0))]
    pallas_call x4 -> x3, Pallas kernels: 27 us -> 12.2 us  [product_call(): pl.pallas_call(functools.partial(product_kernel, orders, len(sources)), g...]
    ppermute x21 -> x17, waiting for transfers between devices: 11 us -> 25.2 us  [flip(): lax.ppermute(array, 'ctx', [(i, i ^ distance) for i in range(ctx_count)])]
    ppermute x24 -> x8, waiting for transfers between devices: 24.8 us -> 38.9 us  [the longest x3 28.9 us: gather_rest(): arrived = lax.ppermute(arrived, axis, hop_pairs(count, group, hop))]
    ppermute x21 -> x17, starting transfers between devices: 25.4 us -> 17.3 us  [flip(): lax.ppermute(array, 'ctx', [(i, i ^ distance) for i in range(ctx_count)])]
    unnamed x40 -> x10, local copies, waits for them, and re-layouts: 5 us -> 0.03 us
    convert_element_type x2, other arithmetic: 2.14 us -> 0.15 us  [product(): return (a.astype(F32) * b.astype(F32)).astype(BF16)]
  transfers between devices with their start and end apart: 47 -> 27, of which waited for: 14 -> 14; matrix products, arithmetic and copies ran while one was open for 3% -> 2% of each run, Pallas kernels for 23% -> 17%
where the time goes in v1:
time: 123 us
  waiting for transfers between devices  64.1 us (52%)
  starting transfers between devices  31.9 us (26%)
  Pallas kernels  20.5 us (17%)
  other arithmetic  3.43 us (3%)
  local copies, waits for them, and re-layouts  1.69 us (1%)
    ppermute x3, waiting for transfers between devices, gather_rest(): arrived = lax.ppermute(arrived, axis, hop_pairs(count, group, hop))  28.9 us
    ppermute x17, waiting for transfers between devices, flip(): lax.ppermute(array, 'ctx', [(i, i ^ distance) for i in range(ctx_count)])  25.2 us
    ppermute x17, starting transfers between devices, flip(): lax.ppermute(array, 'ctx', [(i, i ^ distance) for i in range(ctx_count)])  17.3 us
    pallas_call x3, Pallas kernels, product_call(): pl.pallas_call(functools.partial(product_kernel, orders, len(sources)), g...  12.2 us
    ppermute x2, waiting for transfers between devices, gather_groups(): merged = arrived = lax.ppermute(stack, axis, hop_pairs(count, group, 0))  9.95 us
    pallas_call x1, Pallas kernels, conv_call(): pl.pallas_call(functools.partial(conv_kernel, width, taps), grid=(groups...  8.36 us
    ppermute x3, starting transfers between devices, gather_swap(): arrived = lax.ppermute(stack, axis, hop_pairs(count, group, 0))  4.6 us
    ppermute x3, starting transfers between devices, gather_rest(): arrived = lax.ppermute(arrived, axis, hop_pairs(count, group, hop))  3.86 us
  transfers between devices with their start and end apart: 27, of which 14 were waited for; matrix products, arithmetic and copies ran while one was open for 2% of the time, Pallas kernels for 17%

profile of v1, /device:TPU:0, one launch (start us, length us, event | category | flops | bytes accessed | tf_op | source)
XLA Modules:
  0.0 122.7 jit_solution(2006513209591109463)
XLA Ops:
  0.7 1.3 %dynamic-slice_bitcast_fusion.1 = (bf16[1,512,512]{2,1,0:T(8,128)(2,1)S(1)}, bf16[1,512,512]{2,1,0:T(8,128)(2,1)S(1)}) fusion(bf16[1,2,512,512]{3,2,1,0:T(8,128)(2,1)} %bitcast.28, s32[]{:T(128)S(6)} %select_n.230, s32[]{:T(128)S(6)} %select_n.231), kind=kLoop, calls=%fused_computation.12 | loop fusion | bytes 2097160 | tf_op jit(solution)/shard_map/jit(dynamic_index_in_dim)/squeeze | solution.py:233
  1.9 0.5 collective-permute-start.2
  2.5 0.0 copy-start
  2.5 0.0 copy-start.3
  2.5 1.5 %collective-permute-done.2 = bf16[1,512,512]{2,1,0:T(8,128)(2,1)S(1)} collective-permute-done((bf16[1,512,512]{2,1,0:T(8,128)(2,1)S(1)}, bf16[1,512,512]{2,1,0:T(8,128)(2,1)S(1)}, u32[]{:S(2)}, u32[]{:S(2)}) %collective-permute-start.2) | collective-permute-done | bytes 524320 | tf_op jit(solution)/shard_map/ppermute | solution.py:228
  4.0 3.0 %collective-permute-start.3 = (bf16[1,1,192,1024]{3,2,1,0:T(8,128)(2,1)S(1)}, bf16[1,1,192,1024]{3,2,1,0:T(8,128)(2,1)S(1)}, u32[]{:S(2)}, u32[]{:S(2)}) collective-permute-start(bf16[1,1,192,1024]{3,2,1,0:T(8,128)(2,1)S(1)} %maximum_bitcast_fusion.1), channel_id=1, source_target_pairs={{0,1},{1,0},{2,3},{3,2},{4,5},{5,4},{6,7},{7,6},{8,9},{9,8},{10,11... | collective-permute-start | bytes 1179656 | tf_op jit(solution)/shard_map/ppermute | solution.py:179
  7.1 0.0 copy-start.4
  7.1 0.1 maximum_bitcast_fusion
  7.2 0.1 collective-permute-start.4
  7.3 0.1 multiply_convert_fusion.1
  7.4 1.8 %collective-permute-start = (bf16[1024,128]{1,0:T(8,128)(2,1)S(1)}, bf16[1024,128]{1,0:T(8,128)(2,1)S(1)}, u32[]{:S(2)}, u32[]{:S(2)}) collective-permute-start(bf16[1024,128]{1,0:T(8,128)(2,1)S(1)} %multiply_convert_fusion.1), channel_id=1, source_target_pairs={{0,4},{4,8},{8,12},{12,16},{16,20},{20,24},{24,28},{1,5},{5,9},{9,... | collective-permute-start | bytes 786440 | tf_op jit(solution)/shard_map/ppermute | solution.py:248
  9.2 0.1 multiply_convert_fusion
  9.2 1.3 %collective-permute-start.1 = (bf16[1024,128]{1,0:T(8,128)(2,1)S(1)}, bf16[1024,128]{1,0:T(8,128)(2,1)S(1)}, u32[]{:S(2)}, u32[]{:S(2)}) collective-permute-start(bf16[1024,128]{1,0:T(8,128)(2,1)S(1)} %multiply_convert_fusion), channel_id=1, source_target_pairs={{4,0},{8,4},{12,8},{16,12},{20,16},{24,20},{28,24},{5,1},{9,5},{13... | collective-permute-start | bytes 786440 | tf_op jit(solution)/shard_map/ppermute | solution.py:249
  10.5 6.4 %collective-permute-done.3.after_ref = bf16[1,1,192,1024]{3,2,1,0:T(8,128)(2,1)S(1)} collective-permute-done((bf16[1,1,192,1024]{3,2,1,0:T(8,128)(2,1)S(1)}, bf16[1,1,192,1024]{3,2,1,0:T(8,128)(2,1)S(1)}, u32[]{:S(2)}, u32[]{:S(2)}) %collective-permute-start.3) | collective-permute-done | bytes 393248 | tf_op jit(solution)/shard_map/ppermute | solution.py:179
  17.0 0.1 pad_maximum_fusion.refs_0_
  17.0 1.6 %collective-permute-start.8 = (bf16[2,1,192,1024]{3,2,1,0:T(8,128)(2,1)S(1)}, bf16[2,1,192,1024]{3,2,1,0:T(8,128)(2,1)}, u32[]{:S(2)}, u32[]{:S(2)}) collective-permute-start(bf16[2,1,192,1024]{3,2,1,0:T(8,128)(2,1)S(1)} %pad_maximum_fusion.refs_0_), channel_id=1, source_target_pairs={{1,2},{2,1},{5,6},{6,5},{9,10},{10,9},{13,14},{14,13},{17,18},{18,... | collective-permute-start | bytes 2359304 | tf_op jit(solution)/shard_map/ppermute | solution.py:192
  18.6 0.0 collective-permute-done.kvh_ref
  18.6 8.4 %conv.1 = (bf16[1024,512]{1,0:T(8,128)(2,1)}, bf16[1024,512]{1,0:T(8,128)(2,1)}, bf16[1024,512]{1,0:T(8,128)(2,1)}, f32[64,128]{1,0:T(8,128)S(1)}, bf16[512,1024]{1,0:T(8,128)(2,1)S(1)}) custom-call(bf16[1024,512]{1,0:T(8,128)(2,1)S(1)} %copy-done, bf16[1024,512]{1,0:T(8,128)(2,1)S(1)} %copy-done.1, bf16[1024,512]{1,0:T(8,128)(2,1)S(1)} %copy-done.2, ...), custom_call_target="tpu_custom_call" | custom-call | flops 1073741824 | bytes 8388608 | tf_op jit(solution)/shard_map/conv/pallas_call | solution.py:60
  27.0 3.5 %collective-permute-done.4 = bf16[1,1,320,1024]{3,2,1,0:T(8,128)(2,1)S(1)} collective-permute-done((bf16[1,1,320,1024]{3,2,1,0:T(8,128)(2,1)S(1)}, bf16[1,1,320,1024]{3,2,1,0:T(8,128)(2,1)S(1)}, u32[]{:S(2)}, u32[]{:S(2)}) %collective-permute-start.4) | collective-permute-done | bytes 655392 | tf_op jit(solution)/shard_map/ppermute | solution.py:179
  30.6 0.1 pad_maximum_fusion.1.refs_0_
  30.7 1.5 %collective-permute-start.5 = (bf16[2,1,176,1024]{3,2,1,0:T(8,128)(2,1)S(1)}, bf16[2,1,176,1024]{3,2,1,0:T(8,128)(2,1)}, u32[]{:S(2)}, u32[]{:S(2)}) collective-permute-start(bf16[2,1,176,1024]{3,2,1,0:T(8,128)(2,1)S(1)} %pad_maximum_fusion.1.refs_0_), channel_id=1, source_target_pairs={{1,2},{2,1},{5,6},{6,5},{9,10},{10,9},{13,14},{14,13},{17,18},{18,... | collective-permute-start | bytes 2162696 | tf_op jit(solution)/shard_map/ppermute | solution.py:192
  32.2 0.1 pad_maximum_fusion.2.refs_0_
  32.3 1.3 %collective-permute-start.9 = (bf16[2,1,192,1024]{3,2,1,0:T(8,128)(2,1)}, bf16[2,1,192,1024]{3,2,1,0:T(8,128)(2,1)}, u32[]{:S(2)}, u32[]{:S(2)}) collective-permute-start(bf16[2,1,192,1024]{3,2,1,0:T(8,128)(2,1)} %collective-permute-done.8.refs_1_), channel_id=1, source_target_pairs={{1,0},{2,3},{5,4},{6,7},{9,8},{10,11},{13,12},{14,15},{17,16},{18,... | collective-permute-start | bytes 2359304 | tf_op jit(solution)/shard_map/ppermute | solution.py:200
  33.6 1.3 %collective-permute-start.6 = (bf16[2,1,176,1024]{3,2,1,0:T(8,128)(2,1)}, bf16[2,1,176,1024]{3,2,1,0:T(8,128)(2,1)}, u32[]{:S(2)}, u32[]{:S(2)}) collective-permute-start(bf16[2,1,176,1024]{3,2,1,0:T(8,128)(2,1)} %collective-permute-done.5.refs_5_.refs_1_), channel_id=1, source_target_pairs={{1,0},{2,3},{5,4},{6,7},{9,8},{10,11},{13,12},{14,15},{17,16},{18,... | collective-permute-start | bytes 2162696 | tf_op jit(solution)/shard_map/ppermute | solution.py:200
  34.9 1.5 %collective-permute-start.10 = (bf16[2,1,144,1024]{3,2,1,0:T(8,128)(2,1)S(1)}, bf16[2,1,144,1024]{3,2,1,0:T(8,128)(2,1)}, u32[]{:S(2)}, u32[]{:S(2)}) collective-permute-start(bf16[2,1,144,1024]{3,2,1,0:T(8,128)(2,1)S(1)} %pad_maximum_fusion.2.refs_0_), channel_id=1, source_target_pairs={{1,2},{2,1},{5,6},{6,5},{9,10},{10,9},{13,14},{14,13},{17,18},{18,... | collective-permute-start | bytes 1769480 | tf_op jit(solution)/shard_map/ppermute | solution.py:192
  36.4 0.1 stack.23.spot_ref
  36.5 20.7 %collective-permute-done.9.refs_2_ = bf16[2,1,192,1024]{3,2,1,0:T(8,128)(2,1)} collective-permute-done((bf16[2,1,192,1024]{3,2,1,0:T(8,128)(2,1)}, bf16[2,1,192,1024]{3,2,1,0:T(8,128)(2,1)}, u32[]{:S(2)}, u32[]{:S(2)}) %collective-permute-start.9) | collective-permute-done | bytes 786464 | tf_op jit(solution)/shard_map/ppermute | solution.py:200
  57.3 4.4 %product.3 = (bf16[2,192,512]{2,1,0:T(8,128)(2,1)S(1)}, f32[2,192,512]{2,1,0:T(8,128)S(1)}, bf16[2,192,512]{2,1,0:T(8,128)(2,1)S(1)}, f32[2,192,512]{2,1,0:T(8,128)S(1)}) custom-call(s32[7]{0:T(128)S(1)} %stack.23.spot_ref, bf16[2,1,192,1024]{3,2,1,0:T(8,128)(2,1)S(1)} %pad_maximum_fusion.refs_0_, bf16[2,1,192,1024]{3,2,1,0:T(8,128)(2,1)} %collective-permute-done.8.refs_1_, ...), custom_call_target="tpu_custom_call" | custom-call | flops 1610612736 | bytes 6815744 | tf_op jit(solution)/shard_map/product/pallas_call | solution.py:130
  61.6 1.6 %collective-permute-start.14 = (bf16[2,192,512]{2,1,0:T(8,128)(2,1)S(1)}, bf16[2,192,512]{2,1,0:T(8,128)(2,1)S(1)}, u32[]{:S(2)}, u32[]{:S(2)}) collective-permute-start(bf16[2,192,512]{2,1,0:T(8,128)(2,1)S(1)} %get-tuple-element.35.refs_5_), channel_id=1, source_target_pairs={{0,8},{4,12},{8,0},{12,4},{16,24},{20,28},{24,16},{28,20},{1,9},{5... | collective-permute-start | bytes 1179656 | tf_op jit(solution)/shard_map/ppermute | solution.py:228
  63.2 8.2 %collective-permute-done.6.refs_2_ = bf16[2,1,176,1024]{3,2,1,0:T(8,128)(2,1)} collective-permute-done((bf16[2,1,176,1024]{3,2,1,0:T(8,128)(2,1)}, bf16[2,1,176,1024]{3,2,1,0:T(8,128)(2,1)}, u32[]{:S(2)}, u32[]{:S(2)}) %collective-permute-start.6) | collective-permute-done | bytes 720928 | tf_op jit(solution)/shard_map/ppermute | solution.py:200
  71.4 4.2 %product.4 = (bf16[2,176,512]{2,1,0:T(8,128)(2,1)S(1)}, f32[2,176,512]{2,1,0:T(8,128)S(1)}, bf16[2,176,512]{2,1,0:T(8,128)(2,1)S(1)}, f32[2,176,512]{2,1,0:T(8,128)S(1)}) custom-call(s32[7]{0:T(128)S(1)} %stack.23.spot_ref, bf16[2,1,176,1024]{3,2,1,0:T(8,128)(2,1)S(1)} %pad_maximum_fusion.1.refs_0_, ...), custom_call_target="tpu_custom_call" | custom-call | flops 1476395008 | bytes 6422528 | tf_op jit(solution)/shard_map/product/pallas_call | solution.py:130
  75.6 0.1 collective-permute-start.11
  75.6 1.2 collective-permute-done.11
  76.8 1.5 %collective-permute-start.12 = (f32[64,128]{1,0:T(8,128)S(1)}, f32[64,128]{1,0:T(8,128)S(1)}, u32[]{:S(2)}, u32[]{:S(2)}) collective-permute-start(f32[64,128]{1,0:T(8,128)S(1)} %add.147), channel_id=1, source_target_pairs={{0,8},{4,12},{8,0},{12,4},{16,24},{20,28},{24,16},{28,20},{1,9},{5... | collective-permute-start | bytes 98312 | tf_op jit(solution)/shard_map/ppermute | solution.py:228
  78.3 2.4 %collective-permute-done.12 = f32[64,128]{1,0:T(8,128)S(1)} collective-permute-done((f32[64,128]{1,0:T(8,128)S(1)}, f32[64,128]{1,0:T(8,128)S(1)}, u32[]{:S(2)}, u32[]{:S(2)}) %collective-permute-start.12) | collective-permute-done | bytes 32800 | tf_op jit(solution)/shard_map/ppermute | solution.py:228
  80.8 1.5 %collective-permute-start.13 = (f32[64,128]{1,0:T(8,128)S(1)}, f32[64,128]{1,0:T(8,128)S(1)}, u32[]{:S(2)}, u32[]{:S(2)}) collective-permute-start(f32[64,128]{1,0:T(8,128)S(1)} %add.148), channel_id=1, source_target_pairs={{0,16},{4,20},{8,24},{12,28},{16,0},{20,4},{24,8},{28,12},{1,17},{... | collective-permute-start | bytes 98312 | tf_op jit(solution)/shard_map/ppermute | solution.py:228
  82.3 0.5 collective-permute-start.16
  82.8 1.3 %collective-permute-start.22 = (bf16[2,1,144,1024]{3,2,1,0:T(8,128)(2,1)}, bf16[2,1,144,1024]{3,2,1,0:T(8,128)(2,1)S(1)}, u32[]{:S(2)}, u32[]{:S(2)}) collective-permute-start(bf16[2,1,144,1024]{3,2,1,0:T(8,128)(2,1)} %collective-permute-done.10.refs_6_.refs_1_), channel_id=1, source_target_pairs={{1,0},{2,3},{5,4},{6,7},{9,8},{10,11},{13,12},{14,15},{17,16},{18,... | collective-permute-start | bytes 1769480 | tf_op jit(solution)/shard_map/ppermute | solution.py:200
  84.1 1.6 %collective-permute-start.18 = (bf16[2,176,512]{2,1,0:T(8,128)(2,1)S(1)}, bf16[2,176,512]{2,1,0:T(8,128)(2,1)S(1)}, u32[]{:S(2)}, u32[]{:S(2)}) collective-permute-start(bf16[2,176,512]{2,1,0:T(8,128)(2,1)S(1)} %get-tuple-element.36.refs_5_), channel_id=1, source_target_pairs={{0,8},{4,12},{8,0},{12,4},{16,24},{20,28},{24,16},{28,20},{1,9},{5... | collective-permute-start | bytes 1081352 | tf_op jit(solution)/shard_map/ppermute | solution.py:228
  85.6 1.5 %collective-permute-start.20 = (bf16[2,176,512]{2,1,0:T(8,128)(2,1)S(1)}, bf16[2,176,512]{2,1,0:T(8,128)(2,1)S(1)}, u32[]{:S(2)}, u32[]{:S(2)}) collective-permute-start(bf16[2,176,512]{2,1,0:T(8,128)(2,1)S(1)} %get-tuple-element.43), channel_id=1, source_target_pairs={{0,16},{4,20},{8,24},{12,28},{16,0},{20,4},{24,8},{28,12},{1,17},{... | collective-permute-start | bytes 1081352 | tf_op jit(solution)/shard_map/ppermute | solution.py:228
  87.2 0.6 add_multiply_fusion
  87.8 0.1 convert_add_fusion.1
  87.9 0.6 collective-permute-start.15
  88.5 5.8 %collective-permute-done.16 = bf16[2,192,512]{2,1,0:T(8,128)(2,1)S(1)} collective-permute-done((bf16[2,192,512]{2,1,0:T(8,128)(2,1)S(1)}, bf16[2,192,512]{2,1,0:T(8,128)(2,1)S(1)}, u32[]{:S(2)}, u32[]{:S(2)}) %collective-permute-start.16) | collective-permute-done | bytes 393248 | tf_op jit(solution)/shard_map/ppermute | solution.py:228
  94.3 0.1 convert_add_fusion
  94.5 1.6 %collective-permute-start.17 = (bf16[1,192,512]{2,1,0:T(8,128)(2,1)S(1)}, bf16[1,192,512]{2,1,0:T(8,128)(2,1)S(1)}, u32[]{:S(2)}, u32[]{:S(2)}) collective-permute-start(bf16[1,192,512]{2,1,0:T(8,128)(2,1)S(1)} %slice.158), channel_id=1, source_target_pairs={{0,8},{4,12},{8,0},{12,4},{16,24},{20,28},{24,16},{28,20},{1,9},{5... | collective-permute-start | bytes 589832 | tf_op jit(solution)/shard_map/ppermute | solution.py:228
  96.0 0.1 convert_add_fusion.3
  96.2 0.8 collective-permute-start.19
  97.0 5.1 %collective-permute-done.20 = bf16[2,176,512]{2,1,0:T(8,128)(2,1)S(1)} collective-permute-done((bf16[2,176,512]{2,1,0:T(8,128)(2,1)S(1)}, bf16[2,176,512]{2,1,0:T(8,128)(2,1)S(1)}, u32[]{:S(2)}, u32[]{:S(2)}) %collective-permute-start.20) | collective-permute-done | bytes 360480 | tf_op jit(solution)/shard_map/ppermute | solution.py:228
  102.1 0.1 convert_add_fusion.2
  102.2 1.6 %collective-permute-start.21 = (bf16[1,176,512]{2,1,0:T(8,128)(2,1)S(1)}, bf16[1,176,512]{2,1,0:T(8,128)(2,1)S(1)}, u32[]{:S(2)}, u32[]{:S(2)}) collective-permute-start(bf16[1,176,512]{2,1,0:T(8,128)(2,1)S(1)} %slice.160), channel_id=1, source_target_pairs={{0,8},{4,12},{8,0},{12,4},{16,24},{20,28},{24,16},{28,20},{1,9},{5... | collective-permute-start | bytes 540680 | tf_op jit(solution)/shard_map/ppermute | solution.py:228
  103.8 3.6 %product.5 = (bf16[2,144,512]{2,1,0:T(8,128)(2,1)S(1)}, f32[2,144,512]{2,1,0:T(8,128)S(1)}, bf16[2,144,512]{2,1,0:T(8,128)(2,1)S(1)}, f32[2,144,512]{2,1,0:T(8,128)S(1)}) custom-call(s32[7]{0:T(128)S(1)} %stack.23.spot_ref, bf16[2,1,144,1024]{3,2,1,0:T(8,128)(2,1)S(1)} %pad_maximum_fusion.2.refs_0_, ...), custom_call_target="tpu_custom_call" | custom-call | flops 1207959552 | bytes 5636096 | tf_op jit(solution)/shard_map/product/pallas_call | solution.py:130
  107.4 0.6 collective-permute-start.23
  108.0 0.7 collective-permute-start.25
  108.8 1.3 %collective-permute-done.19 = bf16[1,176,512]{2,1,0:T(8,128)(2,1)S(1)} collective-permute-done((bf16[1,176,512]{2,1,0:T(8,128)(2,1)S(1)}, bf16[1,176,512]{2,1,0:T(8,128)(2,1)S(1)}, u32[]{:S(2)}, u32[]{:S(2)}) %collective-permute-start.19) | collective-permute-done | bytes 180256 | tf_op jit(solution)/shard_map/ppermute | solution.py:228
  110.2 3.9 %collective-permute-done.23 = bf16[2,144,512]{2,1,0:T(8,128)(2,1)S(1)} collective-permute-done((bf16[2,144,512]{2,1,0:T(8,128)(2,1)S(1)}, bf16[2,144,512]{2,1,0:T(8,128)(2,1)S(1)}, u32[]{:S(2)}, u32[]{:S(2)}) %collective-permute-start.23) | collective-permute-done | bytes 294944 | tf_op jit(solution)/shard_map/ppermute | solution.py:228
  114.2 0.1 convert_add_fusion.5
  114.3 0.8 collective-permute-start.24
  115.0 0.8 collective-permute-done.25
  115.8 0.1 convert_add_fusion.4
  115.9 2.0 %collective-permute-start.26 = (bf16[1,144,512]{2,1,0:T(8,128)(2,1)S(1)}, bf16[1,144,512]{2,1,0:T(8,128)(2,1)S(1)}, u32[]{:S(2)}, u32[]{:S(2)}) collective-permute-start(bf16[1,144,512]{2,1,0:T(8,128)(2,1)S(1)} %slice.162), channel_id=1, source_target_pairs={{0,8},{4,12},{8,0},{12,4},{16,24},{20,28},{24,16},{28,20},{1,9},{5... | collective-permute-start | bytes 442376 | tf_op jit(solution)/shard_map/ppermute | solution.py:228
  118.0 1.5 %collective-permute-done.24 = bf16[1,144,512]{2,1,0:T(8,128)(2,1)S(1)} collective-permute-done((bf16[1,144,512]{2,1,0:T(8,128)(2,1)S(1)}, bf16[1,144,512]{2,1,0:T(8,128)(2,1)S(1)}, u32[]{:S(2)}, u32[]{:S(2)}) %collective-permute-start.24) | collective-permute-done | bytes 147488 | tf_op jit(solution)/shard_map/ppermute | solution.py:228
  119.5 1.6 %collective-permute-done.26 = bf16[1,144,512]{2,1,0:T(8,128)(2,1)S(1)} collective-permute-done((bf16[1,144,512]{2,1,0:T(8,128)(2,1)S(1)}, bf16[1,144,512]{2,1,0:T(8,128)(2,1)S(1)}, u32[]{:S(2)}, u32[]{:S(2)}) %collective-permute-start.26) | collective-permute-done | bytes 147488 | tf_op jit(solution)/shard_map/ppermute | solution.py:228
  121.2 1.5 %maximum_maximum_fusion = f32[512,1024]{1,0:T(8,128)} fusion(f32[144,512]{1,0:T(8,128)S(1)} %fusion.9, f32[144,512]{1,0:T(8,128)S(1)} %fusion.11, f32[176,512]{1,0:T(8,128)S(1)} %fusion.5, f32[176,512]{1,0:T(8,128)S(1)} %fusion.7, f32[192,512]{1,0:T(8,128)S(1)} %fusion.1, f32[192,512]{1,0:T(8,128)S(1)} %fusion.3), kind=kLoop, calls=%fused_computation | loop fusion | flops 2621440 | bytes 4194304 | tf_op jit(solution)/shard_map/concatenate | solution.py:286
  (43 shorter events, 0.7 us)
Async XLA Ops:
  1.9 2.1 %collective-permute-start.2 = (bf16[1,512,512]{2,1,0:T(8,128)(2,1)S(1)}, bf16[1,512,512]{2,1,0:T(8,128)(2,1)S(1)}, u32[]{:S(2)}, u32[]{:S(2)}) collective-permute-start(bf16[1,512,512]{2,1,0:T(8,128)(2,1)S(1)} %get-tuple-element.50), channel_id=1, source_target_pairs={{0,4},{4,0},{8,12},{12,8},{16,20},{20,16},{24,28},{28,24},{1,5},{5... | collective-permute-start | bytes 1572872 | tf_op jit(solution)/shard_map/ppermute | solution.py:228
  2.4 4.8 %copy-start.1 = (bf16[1024,512]{1,0:T(8,128)(2,1)S(1)}, bf16[1024,512]{1,0:T(8,128)(2,1)}, u32[]{:S(2)}) copy-start(bf16[1024,512]{1,0:T(8,128)(2,1)} %k_ref.1) | copy-start | bytes 3145732
  2.4 4.8 %copy-start.2 = (bf16[1024,512]{1,0:T(8,128)(2,1)S(1)}, bf16[1024,512]{1,0:T(8,128)(2,1)}, u32[]{:S(2)}) copy-start(bf16[1024,512]{1,0:T(8,128)(2,1)} %v_ref.1) | copy-start | bytes 3145732
  2.5 6.6 %copy-start = (bf16[1024,512]{1,0:T(8,128)(2,1)S(1)}, bf16[1024,512]{1,0:T(8,128)(2,1)}, u32[]{:S(2)}) copy-start(bf16[1024,512]{1,0:T(8,128)(2,1)} %q_ref.1) | copy-start | bytes 3145732
  2.5 6.6 %copy-start.3 = (bf16[1024,512]{1,0:T(8,128)(2,1)S(1)}, bf16[1024,512]{1,0:T(8,128)(2,1)}, u32[]{:S(2)}) copy-start(bf16[1024,512]{1,0:T(8,128)(2,1)} %go_ref.1) | copy-start | bytes 3145732
  4.0 12.9 %collective-permute-start.3 = (bf16[1,1,192,1024]{3,2,1,0:T(8,128)(2,1)S(1)}, bf16[1,1,192,1024]{3,2,1,0:T(8,128)(2,1)S(1)}, u32[]{:S(2)}, u32[]{:S(2)}) collective-permute-start(bf16[1,1,192,1024]{3,2,1,0:T(8,128)(2,1)S(1)} %maximum_bitcast_fusion.1), channel_id=1, source_target_pairs={{0,1},{1,0},{2,3},{3,2},{4,5},{5,4},{6,7},{7,6},{8,9},{9,8},{10,11... | collective-permute-start | bytes 1179656 | tf_op jit(solution)/shard_map/ppermute | solution.py:179
  7.1 11.5 %copy-start.4 = (bf16[64,128]{1,0:T(8,128)(2,1)S(1)}, bf16[64,128]{1,0:T(8,128)(2,1)}, u32[]{:S(2)}) copy-start(bf16[64,128]{1,0:T(8,128)(2,1)} %f_ref.1) | copy-start | bytes 49156
  7.2 23.3 %collective-permute-start.4 = (bf16[1,1,320,1024]{3,2,1,0:T(8,128)(2,1)S(1)}, bf16[1,1,320,1024]{3,2,1,0:T(8,128)(2,1)S(1)}, u32[]{:S(2)}, u32[]{:S(2)}) collective-permute-start(bf16[1,1,320,1024]{3,2,1,0:T(8,128)(2,1)S(1)} %maximum_bitcast_fusion), channel_id=1, source_target_pairs={{0,1},{1,0},{2,3},{3,2},{4,5},{5,4},{6,7},{7,6},{8,9},{9,8},{10,11... | collective-permute-start | bytes 1966088 | tf_op jit(solution)/shard_map/ppermute | solution.py:179
  7.4 11.2 %collective-permute-start = (bf16[1024,128]{1,0:T(8,128)(2,1)S(1)}, bf16[1024,128]{1,0:T(8,128)(2,1)S(1)}, u32[]{:S(2)}, u32[]{:S(2)}) collective-permute-start(bf16[1024,128]{1,0:T(8,128)(2,1)S(1)} %multiply_convert_fusion.1), channel_id=1, source_target_pairs={{0,4},{4,8},{8,12},{12,16},{16,20},{20,24},{24,28},{1,5},{5,9},{9,... | collective-permute-start | bytes 786440 | tf_op jit(solution)/shard_map/ppermute | solution.py:248
  9.2 9.4 %collective-permute-start.1 = (bf16[1024,128]{1,0:T(8,128)(2,1)S(1)}, bf16[1024,128]{1,0:T(8,128)(2,1)S(1)}, u32[]{:S(2)}, u32[]{:S(2)}) collective-permute-start(bf16[1024,128]{1,0:T(8,128)(2,1)S(1)} %multiply_convert_fusion), channel_id=1, source_target_pairs={{4,0},{8,4},{12,8},{16,12},{20,16},{24,20},{28,24},{5,1},{9,5},{13... | collective-permute-start | bytes 786440 | tf_op jit(solution)/shard_map/ppermute | solution.py:249
  17.0 15.3 %collective-permute-start.8 = (bf16[2,1,192,1024]{3,2,1,0:T(8,128)(2,1)S(1)}, bf16[2,1,192,1024]{3,2,1,0:T(8,128)(2,1)}, u32[]{:S(2)}, u32[]{:S(2)}) collective-permute-start(bf16[2,1,192,1024]{3,2,1,0:T(8,128)(2,1)S(1)} %pad_maximum_fusion.refs_0_), channel_id=1, source_target_pairs={{1,2},{2,1},{5,6},{6,5},{9,10},{10,9},{13,14},{14,13},{17,18},{18,... | collective-permute-start | bytes 2359304 | tf_op jit(solution)/shard_map/ppermute | solution.py:192
  30.7 3.0 %collective-permute-start.5 = (bf16[2,1,176,1024]{3,2,1,0:T(8,128)(2,1)S(1)}, bf16[2,1,176,1024]{3,2,1,0:T(8,128)(2,1)}, u32[]{:S(2)}, u32[]{:S(2)}) collective-permute-start(bf16[2,1,176,1024]{3,2,1,0:T(8,128)(2,1)S(1)} %pad_maximum_fusion.1.refs_0_), channel_id=1, source_target_pairs={{1,2},{2,1},{5,6},{6,5},{9,10},{10,9},{13,14},{14,13},{17,18},{18,... | collective-permute-start | bytes 2162696 | tf_op jit(solution)/shard_map/ppermute | solution.py:192
  32.2 4.3 %collective-permute-start.7 = (bf16[512,1024]{1,0:T(8,128)(2,1)S(1)}, bf16[512,1024]{1,0:T(8,128)(2,1)}, u32[]{:S(2)}, u32[]{:S(2)}) collective-permute-start(bf16[512,1024]{1,0:T(8,128)(2,1)S(1)} %get-tuple-element.33.refs_3_), channel_id=1, source_target_pairs={{0,4},{4,0},{8,12},{12,8},{16,20},{20,16},{24,28},{28,24},{1,5},{5... | collective-permute-start | bytes 3145736 | tf_op jit(solution)/shard_map/ppermute | solution.py:228
  32.3 24.9 %collective-permute-start.9 = (bf16[2,1,192,1024]{3,2,1,0:T(8,128)(2,1)}, bf16[2,1,192,1024]{3,2,1,0:T(8,128)(2,1)}, u32[]{:S(2)}, u32[]{:S(2)}) collective-permute-start(bf16[2,1,192,1024]{3,2,1,0:T(8,128)(2,1)} %collective-permute-done.8.refs_1_), channel_id=1, source_target_pairs={{1,0},{2,3},{5,4},{6,7},{9,8},{10,11},{13,12},{14,15},{17,16},{18,... | collective-permute-start | bytes 2359304 | tf_op jit(solution)/shard_map/ppermute | solution.py:200
  33.6 37.7 %collective-permute-start.6 = (bf16[2,1,176,1024]{3,2,1,0:T(8,128)(2,1)}, bf16[2,1,176,1024]{3,2,1,0:T(8,128)(2,1)}, u32[]{:S(2)}, u32[]{:S(2)}) collective-permute-start(bf16[2,1,176,1024]{3,2,1,0:T(8,128)(2,1)} %collective-permute-done.5.refs_5_.refs_1_), channel_id=1, source_target_pairs={{1,0},{2,3},{5,4},{6,7},{9,8},{10,11},{13,12},{14,15},{17,16},{18,... | collective-permute-start | bytes 2162696 | tf_op jit(solution)/shard_map/ppermute | solution.py:200
  34.9 28.3 %collective-permute-start.10 = (bf16[2,1,144,1024]{3,2,1,0:T(8,128)(2,1)S(1)}, bf16[2,1,144,1024]{3,2,1,0:T(8,128)(2,1)}, u32[]{:S(2)}, u32[]{:S(2)}) collective-permute-start(bf16[2,1,144,1024]{3,2,1,0:T(8,128)(2,1)S(1)} %pad_maximum_fusion.2.refs_0_), channel_id=1, source_target_pairs={{1,2},{2,1},{5,6},{6,5},{9,10},{10,9},{13,14},{14,13},{17,18},{18,... | collective-permute-start | bytes 1769480 | tf_op jit(solution)/shard_map/ppermute | solution.py:192
  61.6 26.1 %collective-permute-start.14 = (bf16[2,192,512]{2,1,0:T(8,128)(2,1)S(1)}, bf16[2,192,512]{2,1,0:T(8,128)(2,1)S(1)}, u32[]{:S(2)}, u32[]{:S(2)}) collective-permute-start(bf16[2,192,512]{2,1,0:T(8,128)(2,1)S(1)} %get-tuple-element.35.refs_5_), channel_id=1, source_target_pairs={{0,8},{4,12},{8,0},{12,4},{16,24},{20,28},{24,16},{28,20},{1,9},{5... | collective-permute-start | bytes 1179656 | tf_op jit(solution)/shard_map/ppermute | solution.py:228
  75.6 1.3 %collective-permute-start.11 = (f32[64,128]{1,0:T(8,128)S(1)}, f32[64,128]{1,0:T(8,128)S(1)}, u32[]{:S(2)}, u32[]{:S(2)}) collective-permute-start(f32[64,128]{1,0:T(8,128)S(1)} %get-tuple-element.37), channel_id=1, source_target_pairs={{0,4},{4,0},{8,12},{12,8},{16,20},{20,16},{24,28},{28,24},{1,5},{5... | collective-permute-start | bytes 98312 | tf_op jit(solution)/shard_map/ppermute | solution.py:228
  76.8 3.9 %collective-permute-start.12 = (f32[64,128]{1,0:T(8,128)S(1)}, f32[64,128]{1,0:T(8,128)S(1)}, u32[]{:S(2)}, u32[]{:S(2)}) collective-permute-start(f32[64,128]{1,0:T(8,128)S(1)} %add.147), channel_id=1, source_target_pairs={{0,8},{4,12},{8,0},{12,4},{16,24},{20,28},{24,16},{28,20},{1,9},{5... | collective-permute-start | bytes 98312 | tf_op jit(solution)/shard_map/ppermute | solution.py:228
  80.8 4.9 %collective-permute-start.13 = (f32[64,128]{1,0:T(8,128)S(1)}, f32[64,128]{1,0:T(8,128)S(1)}, u32[]{:S(2)}, u32[]{:S(2)}) collective-permute-start(f32[64,128]{1,0:T(8,128)S(1)} %add.148), channel_id=1, source_target_pairs={{0,16},{4,20},{8,24},{12,28},{16,0},{20,4},{24,8},{28,12},{1,17},{... | collective-permute-start | bytes 98312 | tf_op jit(solution)/shard_map/ppermute | solution.py:228
  82.3 12.1 %collective-permute-start.16 = (bf16[2,192,512]{2,1,0:T(8,128)(2,1)S(1)}, bf16[2,192,512]{2,1,0:T(8,128)(2,1)S(1)}, u32[]{:S(2)}, u32[]{:S(2)}) collective-permute-start(bf16[2,192,512]{2,1,0:T(8,128)(2,1)S(1)} %get-tuple-element.40), channel_id=1, source_target_pairs={{0,16},{4,20},{8,24},{12,28},{16,0},{20,4},{24,8},{28,12},{1,17},{... | collective-permute-start | bytes 1179656 | tf_op jit(solution)/shard_map/ppermute | solution.py:228
  82.8 21.0 %collective-permute-start.22 = (bf16[2,1,144,1024]{3,2,1,0:T(8,128)(2,1)}, bf16[2,1,144,1024]{3,2,1,0:T(8,128)(2,1)S(1)}, u32[]{:S(2)}, u32[]{:S(2)}) collective-permute-start(bf16[2,1,144,1024]{3,2,1,0:T(8,128)(2,1)} %collective-permute-done.10.refs_6_.refs_1_), channel_id=1, source_target_pairs={{1,0},{2,3},{5,4},{6,7},{9,8},{10,11},{13,12},{14,15},{17,16},{18,... | collective-permute-start | bytes 1769480 | tf_op jit(solution)/shard_map/ppermute | solution.py:200
  84.1 12.0 %collective-permute-start.18 = (bf16[2,176,512]{2,1,0:T(8,128)(2,1)S(1)}, bf16[2,176,512]{2,1,0:T(8,128)(2,1)S(1)}, u32[]{:S(2)}, u32[]{:S(2)}) collective-permute-start(bf16[2,176,512]{2,1,0:T(8,128)(2,1)S(1)} %get-tuple-element.36.refs_5_), channel_id=1, source_target_pairs={{0,8},{4,12},{8,0},{12,4},{16,24},{20,28},{24,16},{28,20},{1,9},{5... | collective-permute-start | bytes 1081352 | tf_op jit(solution)/shard_map/ppermute | solution.py:228
  85.6 16.4 %collective-permute-start.20 = (bf16[2,176,512]{2,1,0:T(8,128)(2,1)S(1)}, bf16[2,176,512]{2,1,0:T(8,128)(2,1)S(1)}, u32[]{:S(2)}, u32[]{:S(2)}) collective-permute-start(bf16[2,176,512]{2,1,0:T(8,128)(2,1)S(1)} %get-tuple-element.43), channel_id=1, source_target_pairs={{0,16},{4,20},{8,24},{12,28},{16,0},{20,4},{24,8},{28,12},{1,17},{... | collective-permute-start | bytes 1081352 | tf_op jit(solution)/shard_map/ppermute | solution.py:228
  87.9 20.0 %collective-permute-start.15 = (bf16[1,192,512]{2,1,0:T(8,128)(2,1)S(1)}, bf16[1,192,512]{2,1,0:T(8,128)(2,1)S(1)}, u32[]{:S(2)}, u32[]{:S(2)}) collective-permute-start(bf16[1,192,512]{2,1,0:T(8,128)(2,1)S(1)} %slice.159), channel_id=1, source_target_pairs={{0,16},{4,20},{8,24},{12,28},{16,0},{20,4},{24,8},{28,12},{1,17},{... | collective-permute-start | bytes 589832 | tf_op jit(solution)/shard_map/ppermute | solution.py:228
  94.5 14.3 %collective-permute-start.17 = (bf16[1,192,512]{2,1,0:T(8,128)(2,1)S(1)}, bf16[1,192,512]{2,1,0:T(8,128)(2,1)S(1)}, u32[]{:S(2)}, u32[]{:S(2)}) collective-permute-start(bf16[1,192,512]{2,1,0:T(8,128)(2,1)S(1)} %slice.158), channel_id=1, source_target_pairs={{0,8},{4,12},{8,0},{12,4},{16,24},{20,28},{24,16},{28,20},{1,9},{5... | collective-permute-start | bytes 589832 | tf_op jit(solution)/shard_map/ppermute | solution.py:228
  96.2 13.9 %collective-permute-start.19 = (bf16[1,176,512]{2,1,0:T(8,128)(2,1)S(1)}, bf16[1,176,512]{2,1,0:T(8,128)(2,1)S(1)}, u32[]{:S(2)}, u32[]{:S(2)}) collective-permute-start(bf16[1,176,512]{2,1,0:T(8,128)(2,1)S(1)} %slice.161), channel_id=1, source_target_pairs={{0,16},{4,20},{8,24},{12,28},{16,0},{20,4},{24,8},{28,12},{1,17},{... | collective-permute-start | bytes 540680 | tf_op jit(solution)/shard_map/ppermute | solution.py:228
  102.2 8.0 %collective-permute-start.21 = (bf16[1,176,512]{2,1,0:T(8,128)(2,1)S(1)}, bf16[1,176,512]{2,1,0:T(8,128)(2,1)S(1)}, u32[]{:S(2)}, u32[]{:S(2)}) collective-permute-start(bf16[1,176,512]{2,1,0:T(8,128)(2,1)S(1)} %slice.160), channel_id=1, source_target_pairs={{0,8},{4,12},{8,0},{12,4},{16,24},{20,28},{24,16},{28,20},{1,9},{5... | collective-permute-start | bytes 540680 | tf_op jit(solution)/shard_map/ppermute | solution.py:228
  107.4 6.8 %collective-permute-start.23 = (bf16[2,144,512]{2,1,0:T(8,128)(2,1)S(1)}, bf16[2,144,512]{2,1,0:T(8,128)(2,1)S(1)}, u32[]{:S(2)}, u32[]{:S(2)}) collective-permute-start(bf16[2,144,512]{2,1,0:T(8,128)(2,1)S(1)} %get-tuple-element.46), channel_id=1, source_target_pairs={{0,8},{4,12},{8,0},{12,4},{16,24},{20,28},{24,16},{28,20},{1,9},{5... | collective-permute-start | bytes 884744 | tf_op jit(solution)/shard_map/ppermute | solution.py:228
  108.0 7.8 %collective-permute-start.25 = (bf16[2,144,512]{2,1,0:T(8,128)(2,1)S(1)}, bf16[2,144,512]{2,1,0:T(8,128)(2,1)S(1)}, u32[]{:S(2)}, u32[]{:S(2)}) collective-permute-start(bf16[2,144,512]{2,1,0:T(8,128)(2,1)S(1)} %get-tuple-element.48), channel_id=1, source_target_pairs={{0,16},{4,20},{8,24},{12,28},{16,0},{20,4},{24,8},{28,12},{1,17},{... | collective-permute-start | bytes 884744 | tf_op jit(solution)/shard_map/ppermute | solution.py:228
  114.3 5.2 %collective-permute-start.24 = (bf16[1,144,512]{2,1,0:T(8,128)(2,1)S(1)}, bf16[1,144,512]{2,1,0:T(8,128)(2,1)S(1)}, u32[]{:S(2)}, u32[]{:S(2)}) collective-permute-start(bf16[1,144,512]{2,1,0:T(8,128)(2,1)S(1)} %slice.163), channel_id=1, source_target_pairs={{0,16},{4,20},{8,24},{12,28},{16,0},{20,4},{24,8},{28,12},{1,17},{... | collective-permute-start | bytes 442376 | tf_op jit(solution)/shard_map/ppermute | solution.py:228
  115.9 5.2 %collective-permute-start.26 = (bf16[1,144,512]{2,1,0:T(8,128)(2,1)S(1)}, bf16[1,144,512]{2,1,0:T(8,128)(2,1)S(1)}, u32[]{:S(2)}, u32[]{:S(2)}) collective-permute-start(bf16[1,144,512]{2,1,0:T(8,128)(2,1)S(1)} %slice.162), channel_id=1, source_target_pairs={{0,8},{4,12},{8,0},{12,4},{16,24},{20,28},{24,16},{28,20},{1,9},{5... | collective-permute-start | bytes 442376 | tf_op jit(solution)/shard_map/ppermute | solution.py:228

commit v2 on v1

--- a/solution.py
+++ b/solution.py
@@ -258,31 +258,33 @@
         stacks.append(jnp.concatenate([half[:, :, start : start + size] for half in halves], axis=0))
         start += size
 
-    done, products, sums = [], [], []
+    distance = 1
+    while distance < ctx_count:
+        lag_sums = lag_sums + flip(lag_sums, distance)
+        distance *= 2
+    grad_filters = lag_sums * (total_tokens * width) ** (-0.5)
+
     swapped = [gather_swap(stack, owners, "tp") for stack in stacks]
+    products = []
     for number, state in enumerate(swapped):
-        arrays, holders = gather_rest(*state, "tp", products[-2:-1] if number else stacks[1:])
+        arrays, holders = gather_rest(*state, "tp", [lag_sums][: number == 1] if number else stacks[1:])
         ahead = [arrays[-1] for arrays, _ in swapped[number + 1 : number + 2]]
-        orders = across
-        spot = jnp.stack([chip] + holders).astype(jnp.int32)
-        outs = product_call(orders, chips, spot, arrays, turned, sibling, products[-1:] + ahead)
-        products.append(outs[0])
-        columns, sums = [], []
-        for order, path in enumerate(orders):
+        spot = jnp.stack([chip, *holders]).astype(jnp.int32)
+        after = [outs[0] for outs in products[-1:]] + ahead
+        products.append(product_call(across, chips, spot, arrays, turned, sibling, after))
+    done = []
+    for number, outs in enumerate(products):
+        late = [outs[0] for outs in products[number + 1 :]] if number + 2 == len(products) else []
+        columns = []
+        for order, path in enumerate(across):
             send, keep = outs[2 * order], outs[2 * order + 1]
             for stage, bit in enumerate(path):
                 keep = keep + flip(send, 2 << bit).astype(F32)
                 if stage + 1 < len(path):
                     count = keep.shape[0] // 2
-                    send, keep = keep[count:].astype(BF16), keep[:count]
-                    sums.append(send)
+                    send, keep = tied(keep[count:].astype(BF16), late), keep[:count]
             columns.append(keep[0] * total_tokens ** (-0.5))
         done.append(jnp.concatenate(columns, axis=1))
-    lag_sums, distance = tied(lag_sums, products[-2:-1]), 1
-    while distance < ctx_count:
-        lag_sums = lag_sums + flip(lag_sums, distance)
-        distance *= 2
-    grad_filters = lag_sums * (total_tokens * width) ** (-0.5)
     grad_weight = jnp.concatenate(done, axis=0)
     return (grad_query, grad_key, grad_value, grad_filters, grad_weight)
 

time: 123 us -> 113 us (0.919)
  waiting for transfers between devices: 64.1 us -> 52.7 us
    ppermute x17, waiting for transfers between devices: 25.2 us -> 18.9 us  [flip(): lax.ppermute(array, 'ctx', [(i, i ^ distance) for i in range(ctx_count)])]
    ppermute x3, waiting for transfers between devices: 28.9 us -> 24.3 us  [gather_rest(): arrived = lax.ppermute(arrived, axis, hop_pairs(count, group, hop))]
    ppermute x17, starting transfers between devices: 17.3 us -> 19 us  [flip(): lax.ppermute(array, 'ctx', [(i, i ^ distance) for i in range(ctx_count)])]
    ppermute x3, starting transfers between devices: 4.6 us -> 2.96 us  [gather_swap(): arrived = lax.ppermute(stack, axis, hop_pairs(count, group, 0))]
  transfers between devices with their start and end apart: 27 -> 27, of which waited for: 14 -> 15; matrix products, arithmetic and copies ran while one was open for 2% -> 2% of each run, Pallas kernels for 17% -> 18%
where the time goes in v2:
time: 113 us; the launch traced here: 112 us
  waiting for transfers between devices  52.7 us (47%)
  starting transfers between devices  32.4 us (29%)
  Pallas kernels  20.7 us (18%)
  other arithmetic  3.42 us (3%)
  local copies, waits for them, and re-layouts  1.83 us (2%)
  between operations  1.19 us (1%)
    ppermute x3, waiting for transfers between devices, gather_rest(): arrived = lax.ppermute(arrived, axis, hop_pairs(count, group, hop))  24.3 us
    ppermute x17, starting transfers between devices, flip(): lax.ppermute(array, 'ctx', [(i, i ^ distance) for i in range(ctx_count)])  19 us
    ppermute x17, waiting for transfers between devices, flip(): lax.ppermute(array, 'ctx', [(i, i ^ distance) for i in range(ctx_count)])  18.9 us
    pallas_call x3, Pallas kernels, product_call(): pl.pallas_call(functools.partial(product_kernel, orders, len(sources)), g...  12.4 us
    ppermute x2, waiting for transfers between devices, gather_groups(): merged = arrived = lax.ppermute(stack, axis, hop_pairs(count, group, 0))  9.51 us
    pallas_call x1, Pallas kernels, conv_call(): pl.pallas_call(functools.partial(conv_kernel, width, taps), grid=(groups...  8.37 us
    ppermute x3, starting transfers between devices, gather_rest(): arrived = lax.ppermute(arrived, axis, hop_pairs(count, group, hop))  3.87 us
    ppermute x2, starting transfers between devices, gather_groups(): merged = arrived = lax.ppermute(stack, axis, hop_pairs(count, group, 0))  3.52 us
  transfers between devices with their start and end apart: 27, of which 15 were waited for; matrix products, arithmetic and copies ran while one was open for 2% of the time, Pallas kernels for 18%

profile of v2, /device:TPU:0, one launch (start us, length us, event | category | flops | bytes accessed | tf_op | source)
XLA Modules:
  0.0 112.3 jit_solution(16843957127566128562)
XLA Ops:
  0.7 1.4 %dynamic-slice_bitcast_fusion.1 = (bf16[1,512,512]{2,1,0:T(8,128)(2,1)S(1)}, bf16[1,512,512]{2,1,0:T(8,128)(2,1)S(1)}) fusion(bf16[1,2,512,512]{3,2,1,0:T(8,128)(2,1)} %bitcast.28, s32[]{:T(128)S(6)} %select_n.230, s32[]{:T(128)S(6)} %select_n.231), kind=kLoop, calls=%fused_computation.12 | loop fusion | bytes 2097160 | tf_op jit(solution)/shard_map/jit(dynamic_index_in_dim)/squeeze | solution.py:233
  2.1 0.5 collective-permute-start.2
  2.6 1.5 %collective-permute-done.2 = bf16[1,512,512]{2,1,0:T(8,128)(2,1)S(1)} collective-permute-done((bf16[1,512,512]{2,1,0:T(8,128)(2,1)S(1)}, bf16[1,512,512]{2,1,0:T(8,128)(2,1)S(1)}, u32[]{:S(2)}, u32[]{:S(2)}) %collective-permute-start.2) | collective-permute-done | bytes 524320 | tf_op jit(solution)/shard_map/ppermute | solution.py:228
  4.2 3.0 %collective-permute-start.3 = (bf16[1,1,192,1024]{3,2,1,0:T(8,128)(2,1)S(1)}, bf16[1,1,192,1024]{3,2,1,0:T(8,128)(2,1)S(1)}, u32[]{:S(2)}, u32[]{:S(2)}) collective-permute-start(bf16[1,1,192,1024]{3,2,1,0:T(8,128)(2,1)S(1)} %maximum_bitcast_fusion.1), channel_id=1, source_target_pairs={{0,1},{1,0},{2,3},{3,2},{4,5},{5,4},{6,7},{7,6},{8,9},{9,8},{10,11... | collective-permute-start | bytes 1179656 | tf_op jit(solution)/shard_map/ppermute | solution.py:179
  7.2 0.1 multiply_convert_fusion.1
  7.3 1.8 %collective-permute-start = (bf16[1024,128]{1,0:T(8,128)(2,1)S(1)}, bf16[1024,128]{1,0:T(8,128)(2,1)S(1)}, u32[]{:S(2)}, u32[]{:S(2)}) collective-permute-start(bf16[1024,128]{1,0:T(8,128)(2,1)S(1)} %multiply_convert_fusion.1), channel_id=1, source_target_pairs={{0,4},{4,8},{8,12},{12,16},{16,20},{20,24},{24,28},{1,5},{5,9},{9,... | collective-permute-start | bytes 786440 | tf_op jit(solution)/shard_map/ppermute | solution.py:248
  9.2 0.1 maximum_bitcast_fusion
  9.3 0.5 collective-permute-start.8
  9.8 0.1 multiply_convert_fusion
  9.9 1.3 %collective-permute-start.1 = (bf16[1024,128]{1,0:T(8,128)(2,1)S(1)}, bf16[1024,128]{1,0:T(8,128)(2,1)S(1)}, u32[]{:S(2)}, u32[]{:S(2)}) collective-permute-start(bf16[1024,128]{1,0:T(8,128)(2,1)S(1)} %multiply_convert_fusion), channel_id=1, source_target_pairs={{4,0},{8,4},{12,8},{16,12},{20,16},{24,20},{28,24},{5,1},{9,5},{13... | collective-permute-start | bytes 786440 | tf_op jit(solution)/shard_map/ppermute | solution.py:249
  11.2 6.0 %collective-permute-done.3.after_ref = bf16[1,1,192,1024]{3,2,1,0:T(8,128)(2,1)S(1)} collective-permute-done((bf16[1,1,192,1024]{3,2,1,0:T(8,128)(2,1)S(1)}, bf16[1,1,192,1024]{3,2,1,0:T(8,128)(2,1)S(1)}, u32[]{:S(2)}, u32[]{:S(2)}) %collective-permute-start.3) | collective-permute-done | bytes 393248 | tf_op jit(solution)/shard_map/ppermute | solution.py:179
  17.1 0.1 pad_maximum_fusion.refs_0_
  17.2 1.6 %collective-permute-start.7 = (bf16[2,1,192,1024]{3,2,1,0:T(8,128)(2,1)S(1)}, bf16[2,1,192,1024]{3,2,1,0:T(8,128)(2,1)}, u32[]{:S(2)}, u32[]{:S(2)}) collective-permute-start(bf16[2,1,192,1024]{3,2,1,0:T(8,128)(2,1)S(1)} %pad_maximum_fusion.refs_0_), channel_id=1, source_target_pairs={{1,2},{2,1},{5,6},{6,5},{9,10},{10,9},{13,14},{14,13},{17,18},{18,... | collective-permute-start | bytes 2359304 | tf_op jit(solution)/shard_map/ppermute | solution.py:192
  18.8 8.4 %conv.1 = (bf16[1024,512]{1,0:T(8,128)(2,1)}, bf16[1024,512]{1,0:T(8,128)(2,1)}, bf16[1024,512]{1,0:T(8,128)(2,1)}, f32[64,128]{1,0:T(8,128)S(1)}, bf16[512,1024]{1,0:T(8,128)(2,1)}) custom-call(bf16[1024,512]{1,0:T(8,128)(2,1)S(1)} %copy-done, bf16[1024,512]{1,0:T(8,128)(2,1)S(1)} %copy-done.1, bf16[1024,512]{1,0:T(8,128)(2,1)S(1)} %copy-done.2, ...), custom_call_target="tpu_custom_call" | custom-call | flops 1073741824 | bytes 8388608 | tf_op jit(solution)/shard_map/conv/pallas_call | solution.py:60
  27.2 3.5 %collective-permute-done.8 = bf16[1,1,320,1024]{3,2,1,0:T(8,128)(2,1)S(1)} collective-permute-done((bf16[1,1,320,1024]{3,2,1,0:T(8,128)(2,1)S(1)}, bf16[1,1,320,1024]{3,2,1,0:T(8,128)(2,1)S(1)}, u32[]{:S(2)}, u32[]{:S(2)}) %collective-permute-start.8) | collective-permute-done | bytes 655392 | tf_op jit(solution)/shard_map/ppermute | solution.py:179
  30.8 0.1 pad_maximum_fusion.1.refs_0_
  30.8 0.7 collective-permute-start.11
  31.6 0.1 collective-permute-start.10
  31.7 0.1 pad_maximum_fusion.2.refs_0_
  31.8 1.3 %collective-permute-start.9 = (bf16[2,1,192,1024]{3,2,1,0:T(8,128)(2,1)}, bf16[2,1,192,1024]{3,2,1,0:T(8,128)(2,1)}, u32[]{:S(2)}, u32[]{:S(2)}) collective-permute-start(bf16[2,1,192,1024]{3,2,1,0:T(8,128)(2,1)} %collective-permute-done.7.refs_1_), channel_id=1, source_target_pairs={{1,0},{2,3},{5,4},{6,7},{9,8},{10,11},{13,12},{14,15},{17,16},{18,... | collective-permute-start | bytes 2359304 | tf_op jit(solution)/shard_map/ppermute | solution.py:200
  33.1 0.6 collective-permute-start.4
  33.6 0.7 collective-permute-start.17
  34.3 0.2 collective-permute-done.4
  34.5 1.7 %collective-permute-start.5 = (f32[64,128]{1,0:T(8,128)S(1)}, f32[64,128]{1,0:T(8,128)S(1)}, u32[]{:S(2)}, u32[]{:S(2)}) collective-permute-start(f32[64,128]{1,0:T(8,128)S(1)} %add.141), channel_id=1, source_target_pairs={{0,8},{4,12},{8,0},{12,4},{16,24},{20,28},{24,16},{28,20},{1,9},{5... | collective-permute-start | bytes 98312 | tf_op jit(solution)/shard_map/ppermute | solution.py:228
  36.1 2.3 %collective-permute-done.5 = f32[64,128]{1,0:T(8,128)S(1)} collective-permute-done((f32[64,128]{1,0:T(8,128)S(1)}, f32[64,128]{1,0:T(8,128)S(1)}, u32[]{:S(2)}, u32[]{:S(2)}) %collective-permute-start.5) | collective-permute-done | bytes 32800 | tf_op jit(solution)/shard_map/ppermute | solution.py:228
  38.4 1.7 %collective-permute-start.6 = (f32[64,128]{1,0:T(8,128)S(1)}, f32[64,128]{1,0:T(8,128)S(1)}, u32[]{:S(2)}, u32[]{:S(2)}) collective-permute-start(f32[64,128]{1,0:T(8,128)S(1)} %add.142), channel_id=1, source_target_pairs={{0,16},{4,20},{8,24},{12,28},{16,0},{20,4},{24,8},{28,12},{1,17},{... | collective-permute-start | bytes 98312 | tf_op jit(solution)/shard_map/ppermute | solution.py:228
  40.1 2.2 %collective-permute-done.6 = f32[64,128]{1,0:T(8,128)S(1)} collective-permute-done((f32[64,128]{1,0:T(8,128)S(1)}, f32[64,128]{1,0:T(8,128)S(1)}, u32[]{:S(2)}, u32[]{:S(2)}) %collective-permute-start.6) | collective-permute-done | bytes 32800 | tf_op jit(solution)/shard_map/ppermute | solution.py:228
  42.3 0.6 broadcast_multiply_fusion
  43.0 1.3 %collective-permute-start.16 = (bf16[2,1,176,1024]{3,2,1,0:T(8,128)(2,1)S(1)}, bf16[2,1,176,1024]{3,2,1,0:T(8,128)(2,1)}, u32[]{:S(2)}, u32[]{:S(2)}) collective-permute-start(bf16[2,1,176,1024]{3,2,1,0:T(8,128)(2,1)S(1)} %collective-permute-done.11.refs_5_.refs_1_), channel_id=1, source_target_pairs={{1,0},{2,3},{5,4},{6,7},{9,8},{10,11},{13,12},{14,15},{17,16},{18,... | collective-permute-start | bytes 2162696 | tf_op jit(solution)/shard_map/ppermute | solution.py:200
  44.3 1.3 %collective-permute-start.19 = (bf16[2,1,144,1024]{3,2,1,0:T(8,128)(2,1)S(1)}, bf16[2,1,144,1024]{3,2,1,0:T(8,128)(2,1)}, u32[]{:S(2)}, u32[]{:S(2)}) collective-permute-start(bf16[2,1,144,1024]{3,2,1,0:T(8,128)(2,1)S(1)} %collective-permute-done.17.refs_6_.refs_1_), channel_id=1, source_target_pairs={{1,0},{2,3},{5,4},{6,7},{9,8},{10,11},{13,12},{14,15},{17,16},{18,... | collective-permute-start | bytes 1769480 | tf_op jit(solution)/shard_map/ppermute | solution.py:200
  45.6 0.1 stack.23.spot_ref
  45.7 10.4 %collective-permute-done.9.refs_2_ = bf16[2,1,192,1024]{3,2,1,0:T(8,128)(2,1)} collective-permute-done((bf16[2,1,192,1024]{3,2,1,0:T(8,128)(2,1)}, bf16[2,1,192,1024]{3,2,1,0:T(8,128)(2,1)}, u32[]{:S(2)}, u32[]{:S(2)}) %collective-permute-start.9) | collective-permute-done | bytes 786464 | tf_op jit(solution)/shard_map/ppermute | solution.py:200
  56.1 4.5 %product.3 = (bf16[2,192,512]{2,1,0:T(8,128)(2,1)S(1)}, f32[2,192,512]{2,1,0:T(8,128)S(1)}, bf16[2,192,512]{2,1,0:T(8,128)(2,1)S(1)}, f32[2,192,512]{2,1,0:T(8,128)S(1)}) custom-call(s32[7]{0:T(128)S(1)} %stack.23.spot_ref, bf16[2,1,192,1024]{3,2,1,0:T(8,128)(2,1)S(1)} %pad_maximum_fusion.refs_0_, bf16[2,1,192,1024]{3,2,1,0:T(8,128)(2,1)} %collective-permute-done.7.refs_1_, ...), custom_call_target="tpu_custom_call" | custom-call | flops 1610612736 | bytes 6815744 | tf_op jit(solution)/shard_map/product/pallas_call | solution.py:130
  60.6 1.6 %collective-permute-start.12 = (bf16[2,192,512]{2,1,0:T(8,128)(2,1)S(1)}, bf16[2,192,512]{2,1,0:T(8,128)(2,1)S(1)}, u32[]{:S(2)}, u32[]{:S(2)}) collective-permute-start(bf16[2,192,512]{2,1,0:T(8,128)(2,1)S(1)} %get-tuple-element.37.refs_5_), channel_id=1, source_target_pairs={{0,8},{4,12},{8,0},{12,4},{16,24},{20,28},{24,16},{28,20},{1,9},{5... | collective-permute-start | bytes 1179656 | tf_op jit(solution)/shard_map/ppermute | solution.py:228
  62.2 1.5 %collective-permute-start.14 = (bf16[2,192,512]{2,1,0:T(8,128)(2,1)S(1)}, bf16[2,192,512]{2,1,0:T(8,128)(2,1)S(1)}, u32[]{:S(2)}, u32[]{:S(2)}) collective-permute-start(bf16[2,192,512]{2,1,0:T(8,128)(2,1)S(1)} %get-tuple-element.39), channel_id=1, source_target_pairs={{0,16},{4,20},{8,24},{12,28},{16,0},{20,4},{24,8},{28,12},{1,17},{... | collective-permute-start | bytes 1179656 | tf_op jit(solution)/shard_map/ppermute | solution.py:228
  63.7 11.8 %collective-permute-done.16.refs_2_ = bf16[2,1,176,1024]{3,2,1,0:T(8,128)(2,1)} collective-permute-done((bf16[2,1,176,1024]{3,2,1,0:T(8,128)(2,1)S(1)}, bf16[2,1,176,1024]{3,2,1,0:T(8,128)(2,1)}, u32[]{:S(2)}, u32[]{:S(2)}) %collective-permute-start.16) | collective-permute-done | bytes 720928 | tf_op jit(solution)/shard_map/ppermute | solution.py:200
  75.5 4.1 %product.4 = (bf16[2,176,512]{2,1,0:T(8,128)(2,1)S(1)}, f32[2,176,512]{2,1,0:T(8,128)S(1)}, bf16[2,176,512]{2,1,0:T(8,128)(2,1)S(1)}, f32[2,176,512]{2,1,0:T(8,128)S(1)}) custom-call(s32[7]{0:T(128)S(1)} %stack.23.spot_ref, bf16[2,1,176,1024]{3,2,1,0:T(8,128)(2,1)S(1)} %pad_maximum_fusion.1.refs_0_, ...), custom_call_target="tpu_custom_call" | custom-call | flops 1476395008 | bytes 6422528 | tf_op jit(solution)/shard_map/product/pallas_call | solution.py:130
  79.6 1.6 %collective-permute-start.18 = (bf16[2,176,512]{2,1,0:T(8,128)(2,1)S(1)}, bf16[2,176,512]{2,1,0:T(8,128)(2,1)S(1)}, u32[]{:S(2)}, u32[]{:S(2)}) collective-permute-start(bf16[2,176,512]{2,1,0:T(8,128)(2,1)S(1)} %get-tuple-element.42.refs_5_), channel_id=1, source_target_pairs={{0,8},{4,12},{8,0},{12,4},{16,24},{20,28},{24,16},{28,20},{1,9},{5... | collective-permute-start | bytes 1081352 | tf_op jit(solution)/shard_map/ppermute | solution.py:228
  81.2 1.5 %collective-permute-start.21 = (bf16[2,176,512]{2,1,0:T(8,128)(2,1)S(1)}, bf16[2,176,512]{2,1,0:T(8,128)(2,1)S(1)}, u32[]{:S(2)}, u32[]{:S(2)}) collective-permute-start(bf16[2,176,512]{2,1,0:T(8,128)(2,1)S(1)} %get-tuple-element.46), channel_id=1, source_target_pairs={{0,16},{4,20},{8,24},{12,28},{16,0},{20,4},{24,8},{28,12},{1,17},{... | collective-permute-start | bytes 1081352 | tf_op jit(solution)/shard_map/ppermute | solution.py:228
  82.7 2.1 %collective-permute-done.19.refs_2_ = bf16[2,1,144,1024]{3,2,1,0:T(8,128)(2,1)} collective-permute-done((bf16[2,1,144,1024]{3,2,1,0:T(8,128)(2,1)S(1)}, bf16[2,1,144,1024]{3,2,1,0:T(8,128)(2,1)}, u32[]{:S(2)}, u32[]{:S(2)}) %collective-permute-start.19) | collective-permute-done | bytes 589856 | tf_op jit(solution)/shard_map/ppermute | solution.py:200
  84.8 3.8 %product.5 = (bf16[2,144,512]{2,1,0:T(8,128)(2,1)S(1)}, f32[2,144,512]{2,1,0:T(8,128)S(1)}, bf16[2,144,512]{2,1,0:T(8,128)(2,1)S(1)}, f32[2,144,512]{2,1,0:T(8,128)S(1)}) custom-call(s32[7]{0:T(128)S(1)} %stack.23.spot_ref, bf16[2,1,144,1024]{3,2,1,0:T(8,128)(2,1)S(1)} %pad_maximum_fusion.2.refs_0_, ...), custom_call_target="tpu_custom_call" | custom-call | flops 1207959552 | bytes 5636096 | tf_op jit(solution)/shard_map/product/pallas_call | solution.py:130
  88.6 1.6 %collective-permute-start.23 = (bf16[2,144,512]{2,1,0:T(8,128)(2,1)S(1)}, bf16[2,144,512]{2,1,0:T(8,128)(2,1)S(1)}, u32[]{:S(2)}, u32[]{:S(2)}) collective-permute-start(bf16[2,144,512]{2,1,0:T(8,128)(2,1)S(1)} %get-tuple-element.43), channel_id=1, source_target_pairs={{0,8},{4,12},{8,0},{12,4},{16,24},{20,28},{24,16},{28,20},{1,9},{5... | collective-permute-start | bytes 884744 | tf_op jit(solution)/shard_map/ppermute | solution.py:228
  90.1 1.5 %collective-permute-start.25 = (bf16[2,144,512]{2,1,0:T(8,128)(2,1)S(1)}, bf16[2,144,512]{2,1,0:T(8,128)(2,1)S(1)}, u32[]{:S(2)}, u32[]{:S(2)}) collective-permute-start(bf16[2,144,512]{2,1,0:T(8,128)(2,1)S(1)} %get-tuple-element.50), channel_id=1, source_target_pairs={{0,16},{4,20},{8,24},{12,28},{16,0},{20,4},{24,8},{28,12},{1,17},{... | collective-permute-start | bytes 884744 | tf_op jit(solution)/shard_map/ppermute | solution.py:228
  91.6 0.1 convert_add_fusion.1
  91.8 0.6 collective-permute-start.13
  92.4 0.1 convert_add_fusion
  92.5 4.6 %collective-permute-done.23 = bf16[2,144,512]{2,1,0:T(8,128)(2,1)S(1)} collective-permute-done((bf16[2,144,512]{2,1,0:T(8,128)(2,1)S(1)}, bf16[2,144,512]{2,1,0:T(8,128)(2,1)S(1)}, u32[]{:S(2)}, u32[]{:S(2)}) %collective-permute-start.23) | collective-permute-done | bytes 294944 | tf_op jit(solution)/shard_map/ppermute | solution.py:228
  97.1 1.5 %collective-permute-start.15 = (bf16[1,192,512]{2,1,0:T(8,128)(2,1)S(1)}, bf16[1,192,512]{2,1,0:T(8,128)(2,1)S(1)}, u32[]{:S(2)}, u32[]{:S(2)}) collective-permute-start(bf16[1,192,512]{2,1,0:T(8,128)(2,1)S(1)} %slice.158), channel_id=1, source_target_pairs={{0,8},{4,12},{8,0},{12,4},{16,24},{20,28},{24,16},{28,20},{1,9},{5... | collective-permute-start | bytes 589832 | tf_op jit(solution)/shard_map/ppermute | solution.py:228
  98.6 0.1 convert_add_fusion.5
  98.7 1.3 %collective-permute-done.25 = bf16[2,144,512]{2,1,0:T(8,128)(2,1)S(1)} collective-permute-done((bf16[2,144,512]{2,1,0:T(8,128)(2,1)S(1)}, bf16[2,144,512]{2,1,0:T(8,128)(2,1)S(1)}, u32[]{:S(2)}, u32[]{:S(2)}) %collective-permute-start.25) | collective-permute-done | bytes 294944 | tf_op jit(solution)/shard_map/ppermute | solution.py:228
  100.1 1.5 %collective-permute-start.24 = (bf16[1,144,512]{2,1,0:T(8,128)(2,1)S(1)}, bf16[1,144,512]{2,1,0:T(8,128)(2,1)S(1)}, u32[]{:S(2)}, u32[]{:S(2)}) collective-permute-start(bf16[1,144,512]{2,1,0:T(8,128)(2,1)S(1)} %slice.163), channel_id=1, source_target_pairs={{0,16},{4,20},{8,24},{12,28},{16,0},{20,4},{24,8},{28,12},{1,17},{... | collective-permute-start | bytes 442376 | tf_op jit(solution)/shard_map/ppermute | solution.py:228
  101.6 0.1 convert_add_fusion.4
  101.7 0.6 collective-permute-start.26
  102.3 0.1 convert_add_fusion.3
  102.5 0.6 collective-permute-start.20
  103.0 0.1 convert_add_fusion.2
  103.2 2.0 %collective-permute-done.24 = bf16[1,144,512]{2,1,0:T(8,128)(2,1)S(1)} collective-permute-done((bf16[1,144,512]{2,1,0:T(8,128)(2,1)S(1)}, bf16[1,144,512]{2,1,0:T(8,128)(2,1)S(1)}, u32[]{:S(2)}, u32[]{:S(2)}) %collective-permute-start.24) | collective-permute-done | bytes 147488 | tf_op jit(solution)/shard_map/ppermute | solution.py:228
  105.2 0.5 collective-permute-start.22
  105.8 1.1 %collective-permute-done.26 = bf16[1,144,512]{2,1,0:T(8,128)(2,1)S(1)} collective-permute-done((bf16[1,144,512]{2,1,0:T(8,128)(2,1)S(1)}, bf16[1,144,512]{2,1,0:T(8,128)(2,1)S(1)}, u32[]{:S(2)}, u32[]{:S(2)}) %collective-permute-start.26) | collective-permute-done | bytes 147488 | tf_op jit(solution)/shard_map/ppermute | solution.py:228
  107.0 0.1 fusion.3
  107.1 0.9 collective-permute-done.20
  108.1 2.6 %collective-permute-done.22 = bf16[1,176,512]{2,1,0:T(8,128)(2,1)S(1)} collective-permute-done((bf16[1,176,512]{2,1,0:T(8,128)(2,1)S(1)}, bf16[1,176,512]{2,1,0:T(8,128)(2,1)S(1)}, u32[]{:S(2)}, u32[]{:S(2)}) %collective-permute-start.22) | collective-permute-done | bytes 180256 | tf_op jit(solution)/shard_map/ppermute | solution.py:228
  110.7 0.1 fusion.5
  110.8 1.5 %maximum_maximum_fusion = f32[512,1024]{1,0:T(8,128)} fusion(f32[144,512]{1,0:T(8,128)S(1)} %fusion.9, f32[144,512]{1,0:T(8,128)S(1)} %fusion.11, f32[176,512]{1,0:T(8,128)S(1)} %fusion.5, f32[176,512]{1,0:T(8,128)S(1)} %fusion.7, f32[192,512]{1,0:T(8,128)S(1)} %fusion.1, f32[192,512]{1,0:T(8,128)S(1)} %fusion.3), kind=kLoop, calls=%fused_computation | loop fusion | flops 2621440 | bytes 4194304 | tf_op jit(solution)/shard_map/concatenate | solution.py:288
  (43 shorter events, 0.6 us)
Async XLA Ops:
  0.6 6.6 %copy-start.1 = (bf16[1024,512]{1,0:T(8,128)(2,1)S(1)}, bf16[1024,512]{1,0:T(8,128)(2,1)}, u32[]{:S(2)}) copy-start(bf16[1024,512]{1,0:T(8,128)(2,1)} %k_ref.1) | copy-start | bytes 3145732
  0.6 6.6 %copy-start.2 = (bf16[1024,512]{1,0:T(8,128)(2,1)S(1)}, bf16[1024,512]{1,0:T(8,128)(2,1)}, u32[]{:S(2)}) copy-start(bf16[1024,512]{1,0:T(8,128)(2,1)} %v_ref.1) | copy-start | bytes 3145732
  2.1 2.1 %collective-permute-start.2 = (bf16[1,512,512]{2,1,0:T(8,128)(2,1)S(1)}, bf16[1,512,512]{2,1,0:T(8,128)(2,1)S(1)}, u32[]{:S(2)}, u32[]{:S(2)}) collective-permute-start(bf16[1,512,512]{2,1,0:T(8,128)(2,1)S(1)} %get-tuple-element.54), channel_id=1, source_target_pairs={{0,4},{4,0},{8,12},{12,8},{16,20},{20,16},{24,28},{28,24},{1,5},{5... | collective-permute-start | bytes 1572872 | tf_op jit(solution)/shard_map/ppermute | solution.py:228
  4.2 5.6 %copy-start = (bf16[1024,512]{1,0:T(8,128)(2,1)S(1)}, bf16[1024,512]{1,0:T(8,128)(2,1)}, u32[]{:S(2)}) copy-start(bf16[1024,512]{1,0:T(8,128)(2,1)} %q_ref.1) | copy-start | bytes 3145732
  4.2 5.6 %copy-start.3 = (bf16[1024,512]{1,0:T(8,128)(2,1)S(1)}, bf16[1024,512]{1,0:T(8,128)(2,1)}, u32[]{:S(2)}) copy-start(bf16[1024,512]{1,0:T(8,128)(2,1)} %go_ref.1) | copy-start | bytes 3145732
  4.2 12.9 %collective-permute-start.3 = (bf16[1,1,192,1024]{3,2,1,0:T(8,128)(2,1)S(1)}, bf16[1,1,192,1024]{3,2,1,0:T(8,128)(2,1)S(1)}, u32[]{:S(2)}, u32[]{:S(2)}) collective-permute-start(bf16[1,1,192,1024]{3,2,1,0:T(8,128)(2,1)S(1)} %maximum_bitcast_fusion.1), channel_id=1, source_target_pairs={{0,1},{1,0},{2,3},{3,2},{4,5},{5,4},{6,7},{7,6},{8,9},{9,8},{10,11... | collective-permute-start | bytes 1179656 | tf_op jit(solution)/shard_map/ppermute | solution.py:179
  7.3 11.5 %collective-permute-start = (bf16[1024,128]{1,0:T(8,128)(2,1)S(1)}, bf16[1024,128]{1,0:T(8,128)(2,1)S(1)}, u32[]{:S(2)}, u32[]{:S(2)}) collective-permute-start(bf16[1024,128]{1,0:T(8,128)(2,1)S(1)} %multiply_convert_fusion.1), channel_id=1, source_target_pairs={{0,4},{4,8},{8,12},{12,16},{16,20},{20,24},{24,28},{1,5},{5,9},{9,... | collective-permute-start | bytes 786440 | tf_op jit(solution)/shard_map/ppermute | solution.py:248
  9.1 9.7 %copy-start.4 = (bf16[64,128]{1,0:T(8,128)(2,1)S(1)}, bf16[64,128]{1,0:T(8,128)(2,1)}, u32[]{:S(2)}) copy-start(bf16[64,128]{1,0:T(8,128)(2,1)} %f_ref.1) | copy-start | bytes 49156
  9.3 21.4 %collective-permute-start.8 = (bf16[1,1,320,1024]{3,2,1,0:T(8,128)(2,1)S(1)}, bf16[1,1,320,1024]{3,2,1,0:T(8,128)(2,1)S(1)}, u32[]{:S(2)}, u32[]{:S(2)}) collective-permute-start(bf16[1,1,320,1024]{3,2,1,0:T(8,128)(2,1)S(1)} %maximum_bitcast_fusion), channel_id=1, source_target_pairs={{0,1},{1,0},{2,3},{3,2},{4,5},{5,4},{6,7},{7,6},{8,9},{9,8},{10,11... | collective-permute-start | bytes 1966088 | tf_op jit(solution)/shard_map/ppermute | solution.py:179
  9.9 8.9 %collective-permute-start.1 = (bf16[1024,128]{1,0:T(8,128)(2,1)S(1)}, bf16[1024,128]{1,0:T(8,128)(2,1)S(1)}, u32[]{:S(2)}, u32[]{:S(2)}) collective-permute-start(bf16[1024,128]{1,0:T(8,128)(2,1)S(1)} %multiply_convert_fusion), channel_id=1, source_target_pairs={{4,0},{8,4},{12,8},{16,12},{20,16},{24,20},{28,24},{5,1},{9,5},{13... | collective-permute-start | bytes 786440 | tf_op jit(solution)/shard_map/ppermute | solution.py:249
  17.2 14.5 %collective-permute-start.7 = (bf16[2,1,192,1024]{3,2,1,0:T(8,128)(2,1)S(1)}, bf16[2,1,192,1024]{3,2,1,0:T(8,128)(2,1)}, u32[]{:S(2)}, u32[]{:S(2)}) collective-permute-start(bf16[2,1,192,1024]{3,2,1,0:T(8,128)(2,1)S(1)} %pad_maximum_fusion.refs_0_), channel_id=1, source_target_pairs={{1,2},{2,1},{5,6},{6,5},{9,10},{10,9},{13,14},{14,13},{17,18},{18,... | collective-permute-start | bytes 2359304 | tf_op jit(solution)/shard_map/ppermute | solution.py:192
  30.8 12.1 %collective-permute-start.11 = (bf16[2,1,176,1024]{3,2,1,0:T(8,128)(2,1)S(1)}, bf16[2,1,176,1024]{3,2,1,0:T(8,128)(2,1)S(1)}, u32[]{:S(2)}, u32[]{:S(2)}) collective-permute-start(bf16[2,1,176,1024]{3,2,1,0:T(8,128)(2,1)S(1)} %pad_maximum_fusion.1.refs_0_), channel_id=1, source_target_pairs={{1,2},{2,1},{5,6},{6,5},{9,10},{10,9},{13,14},{14,13},{17,18},{18,... | collective-permute-start | bytes 2162696 | tf_op jit(solution)/shard_map/ppermute | solution.py:192
  31.6 14.2 %collective-permute-start.10 = (bf16[512,1024]{1,0:T(8,128)(2,1)}, bf16[512,1024]{1,0:T(8,128)(2,1)}, u32[]{:S(2)}, u32[]{:S(2)}) collective-permute-start(bf16[512,1024]{1,0:T(8,128)(2,1)} %get-tuple-element.35.refs_3_), channel_id=1, source_target_pairs={{0,4},{4,0},{8,12},{12,8},{16,20},{20,16},{24,28},{28,24},{1,5},{5... | collective-permute-start | bytes 3145736 | tf_op jit(solution)/shard_map/ppermute | solution.py:228
  31.8 24.3 %collective-permute-start.9 = (bf16[2,1,192,1024]{3,2,1,0:T(8,128)(2,1)}, bf16[2,1,192,1024]{3,2,1,0:T(8,128)(2,1)}, u32[]{:S(2)}, u32[]{:S(2)}) collective-permute-start(bf16[2,1,192,1024]{3,2,1,0:T(8,128)(2,1)} %collective-permute-done.7.refs_1_), channel_id=1, source_target_pairs={{1,0},{2,3},{5,4},{6,7},{9,8},{10,11},{13,12},{14,15},{17,16},{18,... | collective-permute-start | bytes 2359304 | tf_op jit(solution)/shard_map/ppermute | solution.py:200
  33.1 1.4 %collective-permute-start.4 = (f32[64,128]{1,0:T(8,128)S(1)}, f32[64,128]{1,0:T(8,128)S(1)}, u32[]{:S(2)}, u32[]{:S(2)}) collective-permute-start(f32[64,128]{1,0:T(8,128)S(1)} %get-tuple-element.31), channel_id=1, source_target_pairs={{0,4},{4,0},{8,12},{12,8},{16,20},{20,16},{24,28},{28,24},{1,5},{5... | collective-permute-start | bytes 98312 | tf_op jit(solution)/shard_map/ppermute | solution.py:228
  33.6 10.6 %collective-permute-start.17 = (bf16[2,1,144,1024]{3,2,1,0:T(8,128)(2,1)S(1)}, bf16[2,1,144,1024]{3,2,1,0:T(8,128)(2,1)S(1)}, u32[]{:S(2)}, u32[]{:S(2)}) collective-permute-start(bf16[2,1,144,1024]{3,2,1,0:T(8,128)(2,1)S(1)} %pad_maximum_fusion.2.refs_0_), channel_id=1, source_target_pairs={{1,2},{2,1},{5,6},{6,5},{9,10},{10,9},{13,14},{14,13},{17,18},{18,... | collective-permute-start | bytes 1769480 | tf_op jit(solution)/shard_map/ppermute | solution.py:192
  34.5 3.9 %collective-permute-start.5 = (f32[64,128]{1,0:T(8,128)S(1)}, f32[64,128]{1,0:T(8,128)S(1)}, u32[]{:S(2)}, u32[]{:S(2)}) collective-permute-start(f32[64,128]{1,0:T(8,128)S(1)} %add.141), channel_id=1, source_target_pairs={{0,8},{4,12},{8,0},{12,4},{16,24},{20,28},{24,16},{28,20},{1,9},{5... | collective-permute-start | bytes 98312 | tf_op jit(solution)/shard_map/ppermute | solution.py:228
  38.4 3.9 %collective-permute-start.6 = (f32[64,128]{1,0:T(8,128)S(1)}, f32[64,128]{1,0:T(8,128)S(1)}, u32[]{:S(2)}, u32[]{:S(2)}) collective-permute-start(f32[64,128]{1,0:T(8,128)S(1)} %add.142), channel_id=1, source_target_pairs={{0,16},{4,20},{8,24},{12,28},{16,0},{20,4},{24,8},{28,12},{1,17},{... | collective-permute-start | bytes 98312 | tf_op jit(solution)/shard_map/ppermute | solution.py:228
  43.0 32.6 %collective-permute-start.16 = (bf16[2,1,176,1024]{3,2,1,0:T(8,128)(2,1)S(1)}, bf16[2,1,176,1024]{3,2,1,0:T(8,128)(2,1)}, u32[]{:S(2)}, u32[]{:S(2)}) collective-permute-start(bf16[2,1,176,1024]{3,2,1,0:T(8,128)(2,1)S(1)} %collective-permute-done.11.refs_5_.refs_1_), channel_id=1, source_target_pairs={{1,0},{2,3},{5,4},{6,7},{9,8},{10,11},{13,12},{14,15},{17,16},{18,... | collective-permute-start | bytes 2162696 | tf_op jit(solution)/shard_map/ppermute | solution.py:200
  44.3 40.5 %collective-permute-start.19 = (bf16[2,1,144,1024]{3,2,1,0:T(8,128)(2,1)S(1)}, bf16[2,1,144,1024]{3,2,1,0:T(8,128)(2,1)}, u32[]{:S(2)}, u32[]{:S(2)}) collective-permute-start(bf16[2,1,144,1024]{3,2,1,0:T(8,128)(2,1)S(1)} %collective-permute-done.17.refs_6_.refs_1_), channel_id=1, source_target_pairs={{1,0},{2,3},{5,4},{6,7},{9,8},{10,11},{13,12},{14,15},{17,16},{18,... | collective-permute-start | bytes 1769480 | tf_op jit(solution)/shard_map/ppermute | solution.py:200
  60.6 29.5 %collective-permute-start.12 = (bf16[2,192,512]{2,1,0:T(8,128)(2,1)S(1)}, bf16[2,192,512]{2,1,0:T(8,128)(2,1)S(1)}, u32[]{:S(2)}, u32[]{:S(2)}) collective-permute-start(bf16[2,192,512]{2,1,0:T(8,128)(2,1)S(1)} %get-tuple-element.37.refs_5_), channel_id=1, source_target_pairs={{0,8},{4,12},{8,0},{12,4},{16,24},{20,28},{24,16},{28,20},{1,9},{5... | collective-permute-start | bytes 1179656 | tf_op jit(solution)/shard_map/ppermute | solution.py:228
  62.2 29.6 %collective-permute-start.14 = (bf16[2,192,512]{2,1,0:T(8,128)(2,1)S(1)}, bf16[2,192,512]{2,1,0:T(8,128)(2,1)S(1)}, u32[]{:S(2)}, u32[]{:S(2)}) collective-permute-start(bf16[2,192,512]{2,1,0:T(8,128)(2,1)S(1)} %get-tuple-element.39), channel_id=1, source_target_pairs={{0,16},{4,20},{8,24},{12,28},{16,0},{20,4},{24,8},{28,12},{1,17},{... | collective-permute-start | bytes 1179656 | tf_op jit(solution)/shard_map/ppermute | solution.py:228
  79.6 22.1 %collective-permute-start.18 = (bf16[2,176,512]{2,1,0:T(8,128)(2,1)S(1)}, bf16[2,176,512]{2,1,0:T(8,128)(2,1)S(1)}, u32[]{:S(2)}, u32[]{:S(2)}) collective-permute-start(bf16[2,176,512]{2,1,0:T(8,128)(2,1)S(1)} %get-tuple-element.42.refs_5_), channel_id=1, source_target_pairs={{0,8},{4,12},{8,0},{12,4},{16,24},{20,28},{24,16},{28,20},{1,9},{5... | collective-permute-start | bytes 1081352 | tf_op jit(solution)/shard_map/ppermute | solution.py:228
  81.2 21.3 %collective-permute-start.21 = (bf16[2,176,512]{2,1,0:T(8,128)(2,1)S(1)}, bf16[2,176,512]{2,1,0:T(8,128)(2,1)S(1)}, u32[]{:S(2)}, u32[]{:S(2)}) collective-permute-start(bf16[2,176,512]{2,1,0:T(8,128)(2,1)S(1)} %get-tuple-element.46), channel_id=1, source_target_pairs={{0,16},{4,20},{8,24},{12,28},{16,0},{20,4},{24,8},{28,12},{1,17},{... | collective-permute-start | bytes 1081352 | tf_op jit(solution)/shard_map/ppermute | solution.py:228
  88.6 8.6 %collective-permute-start.23 = (bf16[2,144,512]{2,1,0:T(8,128)(2,1)S(1)}, bf16[2,144,512]{2,1,0:T(8,128)(2,1)S(1)}, u32[]{:S(2)}, u32[]{:S(2)}) collective-permute-start(bf16[2,144,512]{2,1,0:T(8,128)(2,1)S(1)} %get-tuple-element.43), channel_id=1, source_target_pairs={{0,8},{4,12},{8,0},{12,4},{16,24},{20,28},{24,16},{28,20},{1,9},{5... | collective-permute-start | bytes 884744 | tf_op jit(solution)/shard_map/ppermute | solution.py:228
  90.1 9.9 %collective-permute-start.25 = (bf16[2,144,512]{2,1,0:T(8,128)(2,1)S(1)}, bf16[2,144,512]{2,1,0:T(8,128)(2,1)S(1)}, u32[]{:S(2)}, u32[]{:S(2)}) collective-permute-start(bf16[2,144,512]{2,1,0:T(8,128)(2,1)S(1)} %get-tuple-element.50), channel_id=1, source_target_pairs={{0,16},{4,20},{8,24},{12,28},{16,0},{20,4},{24,8},{28,12},{1,17},{... | collective-permute-start | bytes 884744 | tf_op jit(solution)/shard_map/ppermute | solution.py:228
  91.8 15.2 %collective-permute-start.13 = (bf16[1,192,512]{2,1,0:T(8,128)(2,1)S(1)}, bf16[1,192,512]{2,1,0:T(8,128)(2,1)S(1)}, u32[]{:S(2)}, u32[]{:S(2)}) collective-permute-start(bf16[1,192,512]{2,1,0:T(8,128)(2,1)S(1)} %slice.159), channel_id=1, source_target_pairs={{0,16},{4,20},{8,24},{12,28},{16,0},{20,4},{24,8},{28,12},{1,17},{... | collective-permute-start | bytes 589832 | tf_op jit(solution)/shard_map/ppermute | solution.py:228
  97.1 9.9 %collective-permute-start.15 = (bf16[1,192,512]{2,1,0:T(8,128)(2,1)S(1)}, bf16[1,192,512]{2,1,0:T(8,128)(2,1)S(1)}, u32[]{:S(2)}, u32[]{:S(2)}) collective-permute-start(bf16[1,192,512]{2,1,0:T(8,128)(2,1)S(1)} %slice.158), channel_id=1, source_target_pairs={{0,8},{4,12},{8,0},{12,4},{16,24},{20,28},{24,16},{28,20},{1,9},{5... | collective-permute-start | bytes 589832 | tf_op jit(solution)/shard_map/ppermute | solution.py:228
  100.1 5.1 %collective-permute-start.24 = (bf16[1,144,512]{2,1,0:T(8,128)(2,1)S(1)}, bf16[1,144,512]{2,1,0:T(8,128)(2,1)S(1)}, u32[]{:S(2)}, u32[]{:S(2)}) collective-permute-start(bf16[1,144,512]{2,1,0:T(8,128)(2,1)S(1)} %slice.163), channel_id=1, source_target_pairs={{0,16},{4,20},{8,24},{12,28},{16,0},{20,4},{24,8},{28,12},{1,17},{... | collective-permute-start | bytes 442376 | tf_op jit(solution)/shard_map/ppermute | solution.py:228
  101.7 5.2 %collective-permute-start.26 = (bf16[1,144,512]{2,1,0:T(8,128)(2,1)S(1)}, bf16[1,144,512]{2,1,0:T(8,128)(2,1)S(1)}, u32[]{:S(2)}, u32[]{:S(2)}) collective-permute-start(bf16[1,144,512]{2,1,0:T(8,128)(2,1)S(1)} %slice.162), channel_id=1, source_target_pairs={{0,8},{4,12},{8,0},{12,4},{16,24},{20,28},{24,16},{28,20},{1,9},{5... | collective-permute-start | bytes 442376 | tf_op jit(solution)/shard_map/ppermute | solution.py:228
  102.5 5.6 %collective-permute-start.20 = (bf16[1,176,512]{2,1,0:T(8,128)(2,1)S(1)}, bf16[1,176,512]{2,1,0:T(8,128)(2,1)S(1)}, u32[]{:S(2)}, u32[]{:S(2)}) collective-permute-start(bf16[1,176,512]{2,1,0:T(8,128)(2,1)S(1)} %slice.161), channel_id=1, source_target_pairs={{0,16},{4,20},{8,24},{12,28},{16,0},{20,4},{24,8},{28,12},{1,17},{... | collective-permute-start | bytes 540680 | tf_op jit(solution)/shard_map/ppermute | solution.py:228
  105.2 5.5 %collective-permute-start.22 = (bf16[1,176,512]{2,1,0:T(8,128)(2,1)S(1)}, bf16[1,176,512]{2,1,0:T(8,128)(2,1)S(1)}, u32[]{:S(2)}, u32[]{:S(2)}) collective-permute-start(bf16[1,176,512]{2,1,0:T(8,128)(2,1)S(1)} %slice.160), channel_id=1, source_target_pairs={{0,8},{4,12},{8,0},{12,4},{16,24},{20,28},{24,16},{28,20},{1,9},{5... | collective-permute-start | bytes 540680 | tf_op jit(solution)/shard_map/ppermute | solution.py:228

commit v3 on v2

--- a/solution.py
+++ b/solution.py
@@ -6,7 +6,7 @@
 from jax.sharding import PartitionSpec as P
 
 F32, BF16 = jnp.float32, jnp.bfloat16
-SHARES, TILE = (12, 11, 9), 512
+SHARES, TILE = (12, 12, 8), 512
 
 def conv_kernel(width, taps, q_ref, k_ref, v_ref, go_ref, kvh_ref, ggh_ref, f_ref, after_ref, gq_ref, gk_ref, gv_ref, gf_ref, turned_ref, low_ref, high_ref):
     del after_ref
@@ -267,7 +267,7 @@
     swapped = [gather_swap(stack, owners, "tp") for stack in stacks]
     products = []
     for number, state in enumerate(swapped):
-        arrays, holders = gather_rest(*state, "tp", [lag_sums][: number == 1] if number else stacks[1:])
+        arrays, holders = gather_rest(*state, "tp", ([lag_sums], [outs[0] for outs in products[-2:-1]])[number > 1] if number else stacks[1:])
         ahead = [arrays[-1] for arrays, _ in swapped[number + 1 : number + 2]]
         spot = jnp.stack([chip, *holders]).astype(jnp.int32)
         after = [outs[0] for outs in products[-1:]] + ahead

time: 113 us -> 107 us (0.947)
  waiting for transfers between devices: 52.7 us -> 47.5 us
    ppermute x3, waiting for transfers between devices: 24.3 us -> 20 us  [gather_rest(): arrived = lax.ppermute(arrived, axis, hop_pairs(count, group, hop))]
    ppermute x3, starting transfers between devices: 2.96 us -> 4.58 us  [gather_swap(): arrived = lax.ppermute(stack, axis, hop_pairs(count, group, 0))]
    ppermute x17, waiting for transfers between devices: 18.9 us -> 17.4 us  [flip(): lax.ppermute(array, 'ctx', [(i, i ^ distance) for i in range(ctx_count)])]
  transfers between devices with their start and end apart: 27 -> 27, of which waited for: 15 -> 15; matrix products, arithmetic and copies ran while one was open for 2% -> 2% of each run, Pallas kernels for 18% -> 19%
where the time goes in v3:
time: 107 us; the launch traced here: 106 us
  waiting for transfers between devices  47.5 us (44%)
  starting transfers between devices  32.6 us (30%)
  Pallas kernels  20.2 us (19%)
  other arithmetic  3.47 us (3%)
  local copies, waits for them, and re-layouts  1.7 us (2%)
    ppermute x3, waiting for transfers between devices, gather_rest(): arrived = lax.ppermute(arrived, axis, hop_pairs(count, group, hop))  20 us
    ppermute x17, starting transfers between devices, flip(): lax.ppermute(array, 'ctx', [(i, i ^ distance) for i in range(ctx_count)])  18 us
    ppermute x17, waiting for transfers between devices, flip(): lax.ppermute(array, 'ctx', [(i, i ^ distance) for i in range(ctx_count)])  17.4 us
    pallas_call x3, Pallas kernels, product_call(): pl.pallas_call(functools.partial(product_kernel, orders, len(sources)), g...  11.8 us
    ppermute x2, waiting for transfers between devices, gather_groups(): merged = arrived = lax.ppermute(stack, axis, hop_pairs(count, group, 0))  9.97 us
    pallas_call x1, Pallas kernels, conv_call(): pl.pallas_call(functools.partial(conv_kernel, width, taps), grid=(groups...  8.36 us
    ppermute x3, starting transfers between devices, gather_swap(): arrived = lax.ppermute(stack, axis, hop_pairs(count, group, 0))  4.58 us
    ppermute x3, starting transfers between devices, gather_rest(): arrived = lax.ppermute(arrived, axis, hop_pairs(count, group, hop))  3.85 us
  transfers between devices with their start and end apart: 27, of which 15 were waited for; matrix products, arithmetic and copies ran while one was open for 2% of the time, Pallas kernels for 19%

profile of v3, /device:TPU:0, one launch (start us, length us, event | category | flops | bytes accessed | tf_op | source)
XLA Modules:
  0.0 106.5 jit_solution(14972145851804400878)
XLA Ops:
  0.7 1.3 %dynamic-slice_bitcast_fusion.1 = (bf16[1,512,512]{2,1,0:T(8,128)(2,1)S(1)}, bf16[1,512,512]{2,1,0:T(8,128)(2,1)S(1)}) fusion(bf16[1,2,512,512]{3,2,1,0:T(8,128)(2,1)} %bitcast.28, s32[]{:T(128)S(6)} %select_n.230, s32[]{:T(128)S(6)} %select_n.231), kind=kLoop, calls=%fused_computation.12 | loop fusion | bytes 2097160 | tf_op jit(solution)/shard_map/jit(dynamic_index_in_dim)/squeeze | solution.py:233
  1.9 0.5 collective-permute-start.2
  2.5 1.5 %collective-permute-done.2 = bf16[1,512,512]{2,1,0:T(8,128)(2,1)S(1)} collective-permute-done((bf16[1,512,512]{2,1,0:T(8,128)(2,1)S(1)}, bf16[1,512,512]{2,1,0:T(8,128)(2,1)S(1)}, u32[]{:S(2)}, u32[]{:S(2)}) %collective-permute-start.2) | collective-permute-done | bytes 524320 | tf_op jit(solution)/shard_map/ppermute | solution.py:228
  4.0 3.0 %collective-permute-start.3 = (bf16[1,1,192,1024]{3,2,1,0:T(8,128)(2,1)S(1)}, bf16[1,1,192,1024]{3,2,1,0:T(8,128)(2,1)S(1)}, u32[]{:S(2)}, u32[]{:S(2)}) collective-permute-start(bf16[1,1,192,1024]{3,2,1,0:T(8,128)(2,1)S(1)} %maximum_bitcast_fusion.1), channel_id=1, source_target_pairs={{0,1},{1,0},{2,3},{3,2},{4,5},{5,4},{6,7},{7,6},{8,9},{9,8},{10,11... | collective-permute-start | bytes 1179656 | tf_op jit(solution)/shard_map/ppermute | solution.py:179
  7.1 0.1 maximum_bitcast_fusion
  7.2 0.1 collective-permute-start.8
  7.3 0.1 multiply_convert_fusion.1
  7.4 1.8 %collective-permute-start = (bf16[1024,128]{1,0:T(8,128)(2,1)S(1)}, bf16[1024,128]{1,0:T(8,128)(2,1)S(1)}, u32[]{:S(2)}, u32[]{:S(2)}) collective-permute-start(bf16[1024,128]{1,0:T(8,128)(2,1)S(1)} %multiply_convert_fusion.1), channel_id=1, source_target_pairs={{0,4},{4,8},{8,12},{12,16},{16,20},{20,24},{24,28},{1,5},{5,9},{9,... | collective-permute-start | bytes 786440 | tf_op jit(solution)/shard_map/ppermute | solution.py:248
  9.2 0.1 multiply_convert_fusion
  9.2 1.3 %collective-permute-start.1 = (bf16[1024,128]{1,0:T(8,128)(2,1)S(1)}, bf16[1024,128]{1,0:T(8,128)(2,1)S(1)}, u32[]{:S(2)}, u32[]{:S(2)}) collective-permute-start(bf16[1024,128]{1,0:T(8,128)(2,1)S(1)} %multiply_convert_fusion), channel_id=1, source_target_pairs={{4,0},{8,4},{12,8},{16,12},{20,16},{24,20},{28,24},{5,1},{9,5},{13... | collective-permute-start | bytes 786440 | tf_op jit(solution)/shard_map/ppermute | solution.py:249
  10.5 6.4 %collective-permute-done.3.after_ref = bf16[1,1,192,1024]{3,2,1,0:T(8,128)(2,1)S(1)} collective-permute-done((bf16[1,1,192,1024]{3,2,1,0:T(8,128)(2,1)S(1)}, bf16[1,1,192,1024]{3,2,1,0:T(8,128)(2,1)S(1)}, u32[]{:S(2)}, u32[]{:S(2)}) %collective-permute-start.3) | collective-permute-done | bytes 393248 | tf_op jit(solution)/shard_map/ppermute | solution.py:179
  17.0 0.1 pad_maximum_fusion.refs_0_
  17.0 1.6 %collective-permute-start.7 = (bf16[2,1,192,1024]{3,2,1,0:T(8,128)(2,1)S(1)}, bf16[2,1,192,1024]{3,2,1,0:T(8,128)(2,1)}, u32[]{:S(2)}, u32[]{:S(2)}) collective-permute-start(bf16[2,1,192,1024]{3,2,1,0:T(8,128)(2,1)S(1)} %pad_maximum_fusion.refs_0_), channel_id=1, source_target_pairs={{1,2},{2,1},{5,6},{6,5},{9,10},{10,9},{13,14},{14,13},{17,18},{18,... | collective-permute-start | bytes 2359304 | tf_op jit(solution)/shard_map/ppermute | solution.py:192
  18.6 8.4 %conv.1 = (bf16[1024,512]{1,0:T(8,128)(2,1)}, bf16[1024,512]{1,0:T(8,128)(2,1)}, bf16[1024,512]{1,0:T(8,128)(2,1)}, f32[64,128]{1,0:T(8,128)S(1)}, bf16[512,1024]{1,0:T(8,128)(2,1)S(1)}) custom-call(bf16[1024,512]{1,0:T(8,128)(2,1)S(1)} %copy-done, bf16[1024,512]{1,0:T(8,128)(2,1)S(1)} %copy-done.1, bf16[1024,512]{1,0:T(8,128)(2,1)S(1)} %copy-done.2, ...), custom_call_target="tpu_custom_call" | custom-call | flops 1073741824 | bytes 8388608 | tf_op jit(solution)/shard_map/conv/pallas_call | solution.py:60
  27.0 3.6 %collective-permute-done.8 = bf16[1,1,320,1024]{3,2,1,0:T(8,128)(2,1)S(1)} collective-permute-done((bf16[1,1,320,1024]{3,2,1,0:T(8,128)(2,1)S(1)}, bf16[1,1,320,1024]{3,2,1,0:T(8,128)(2,1)S(1)}, u32[]{:S(2)}, u32[]{:S(2)}) %collective-permute-start.8) | collective-permute-done | bytes 655392 | tf_op jit(solution)/shard_map/ppermute | solution.py:179
  30.6 0.1 pad_maximum_fusion.1.refs_0_
  30.7 1.6 %collective-permute-start.11 = (bf16[2,1,192,1024]{3,2,1,0:T(8,128)(2,1)S(1)}, bf16[2,1,192,1024]{3,2,1,0:T(8,128)(2,1)}, u32[]{:S(2)}, u32[]{:S(2)}) collective-permute-start(bf16[2,1,192,1024]{3,2,1,0:T(8,128)(2,1)S(1)} %pad_maximum_fusion.1.refs_0_), channel_id=1, source_target_pairs={{1,2},{2,1},{5,6},{6,5},{9,10},{10,9},{13,14},{14,13},{17,18},{18,... | collective-permute-start | bytes 2359304 | tf_op jit(solution)/shard_map/ppermute | solution.py:192
  32.3 0.1 pad_maximum_fusion.2.refs_0_
  32.4 1.3 %collective-permute-start.9 = (bf16[2,1,192,1024]{3,2,1,0:T(8,128)(2,1)}, bf16[2,1,192,1024]{3,2,1,0:T(8,128)(2,1)}, u32[]{:S(2)}, u32[]{:S(2)}) collective-permute-start(bf16[2,1,192,1024]{3,2,1,0:T(8,128)(2,1)} %collective-permute-done.7.refs_1_), channel_id=1, source_target_pairs={{1,0},{2,3},{5,4},{6,7},{9,8},{10,11},{13,12},{14,15},{17,16},{18,... | collective-permute-start | bytes 2359304 | tf_op jit(solution)/shard_map/ppermute | solution.py:200
  33.7 0.6 collective-permute-start.4
  34.2 0.9 collective-permute-done.4
  35.1 1.7 %collective-permute-start.5 = (f32[64,128]{1,0:T(8,128)S(1)}, f32[64,128]{1,0:T(8,128)S(1)}, u32[]{:S(2)}, u32[]{:S(2)}) collective-permute-start(f32[64,128]{1,0:T(8,128)S(1)} %add.141), channel_id=1, source_target_pairs={{0,8},{4,12},{8,0},{12,4},{16,24},{20,28},{24,16},{28,20},{1,9},{5... | collective-permute-start | bytes 98312 | tf_op jit(solution)/shard_map/ppermute | solution.py:228
  36.8 2.3 %collective-permute-done.5 = f32[64,128]{1,0:T(8,128)S(1)} collective-permute-done((f32[64,128]{1,0:T(8,128)S(1)}, f32[64,128]{1,0:T(8,128)S(1)}, u32[]{:S(2)}, u32[]{:S(2)}) %collective-permute-start.5) | collective-permute-done | bytes 32800 | tf_op jit(solution)/shard_map/ppermute | solution.py:228
  39.0 1.7 %collective-permute-start.6 = (f32[64,128]{1,0:T(8,128)S(1)}, f32[64,128]{1,0:T(8,128)S(1)}, u32[]{:S(2)}, u32[]{:S(2)}) collective-permute-start(f32[64,128]{1,0:T(8,128)S(1)} %add.142), channel_id=1, source_target_pairs={{0,16},{4,20},{8,24},{12,28},{16,0},{20,4},{24,8},{28,12},{1,17},{... | collective-permute-start | bytes 98312 | tf_op jit(solution)/shard_map/ppermute | solution.py:228
  40.7 2.2 %collective-permute-done.6 = f32[64,128]{1,0:T(8,128)S(1)} collective-permute-done((f32[64,128]{1,0:T(8,128)S(1)}, f32[64,128]{1,0:T(8,128)S(1)}, u32[]{:S(2)}, u32[]{:S(2)}) %collective-permute-start.6) | collective-permute-done | bytes 32800 | tf_op jit(solution)/shard_map/ppermute | solution.py:228
  42.9 0.6 broadcast_multiply_fusion
  43.6 1.3 %collective-permute-start.16 = (bf16[2,1,192,1024]{3,2,1,0:T(8,128)(2,1)}, bf16[2,1,192,1024]{3,2,1,0:T(8,128)(2,1)}, u32[]{:S(2)}, u32[]{:S(2)}) collective-permute-start(bf16[2,1,192,1024]{3,2,1,0:T(8,128)(2,1)} %collective-permute-done.11.refs_5_.refs_1_), channel_id=1, source_target_pairs={{1,0},{2,3},{5,4},{6,7},{9,8},{10,11},{13,12},{14,15},{17,16},{18,... | collective-permute-start | bytes 2359304 | tf_op jit(solution)/shard_map/ppermute | solution.py:200
  44.9 1.5 %collective-permute-start.17 = (bf16[2,1,128,1024]{3,2,1,0:T(8,128)(2,1)S(1)}, bf16[2,1,128,1024]{3,2,1,0:T(8,128)(2,1)}, u32[]{:S(2)}, u32[]{:S(2)}) collective-permute-start(bf16[2,1,128,1024]{3,2,1,0:T(8,128)(2,1)S(1)} %pad_maximum_fusion.2.refs_0_), channel_id=1, source_target_pairs={{1,2},{2,1},{5,6},{6,5},{9,10},{10,9},{13,14},{14,13},{17,18},{18,... | collective-permute-start | bytes 1572872 | tf_op jit(solution)/shard_map/ppermute | solution.py:192
  46.3 0.1 stack.23.spot_ref
  46.4 9.5 %collective-permute-done.9.refs_2_ = bf16[2,1,192,1024]{3,2,1,0:T(8,128)(2,1)} collective-permute-done((bf16[2,1,192,1024]{3,2,1,0:T(8,128)(2,1)}, bf16[2,1,192,1024]{3,2,1,0:T(8,128)(2,1)}, u32[]{:S(2)}, u32[]{:S(2)}) %collective-permute-start.9) | collective-permute-done | bytes 786464 | tf_op jit(solution)/shard_map/ppermute | solution.py:200
  55.9 4.3 %product.3 = (bf16[2,192,512]{2,1,0:T(8,128)(2,1)S(1)}, f32[2,192,512]{2,1,0:T(8,128)S(1)}, bf16[2,192,512]{2,1,0:T(8,128)(2,1)S(1)}, f32[2,192,512]{2,1,0:T(8,128)S(1)}) custom-call(s32[7]{0:T(128)S(1)} %stack.23.spot_ref, bf16[2,1,192,1024]{3,2,1,0:T(8,128)(2,1)S(1)} %pad_maximum_fusion.refs_0_, bf16[2,1,192,1024]{3,2,1,0:T(8,128)(2,1)} %collective-permute-done.7.refs_1_, ...), custom_call_target="tpu_custom_call" | custom-call | flops 1610612736 | bytes 6815744 | tf_op jit(solution)/shard_map/product/pallas_call | solution.py:130
  60.2 1.6 %collective-permute-start.12 = (bf16[2,192,512]{2,1,0:T(8,128)(2,1)S(1)}, bf16[2,192,512]{2,1,0:T(8,128)(2,1)S(1)}, u32[]{:S(2)}, u32[]{:S(2)}) collective-permute-start(bf16[2,192,512]{2,1,0:T(8,128)(2,1)S(1)} %get-tuple-element.38.refs_5_), channel_id=1, source_target_pairs={{0,8},{4,12},{8,0},{12,4},{16,24},{20,28},{24,16},{28,20},{1,9},{5... | collective-permute-start | bytes 1179656 | tf_op jit(solution)/shard_map/ppermute | solution.py:228
  61.7 1.5 %collective-permute-start.14 = (bf16[2,192,512]{2,1,0:T(8,128)(2,1)S(1)}, bf16[2,192,512]{2,1,0:T(8,128)(2,1)S(1)}, u32[]{:S(2)}, u32[]{:S(2)}) collective-permute-start(bf16[2,192,512]{2,1,0:T(8,128)(2,1)S(1)} %get-tuple-element.40), channel_id=1, source_target_pairs={{0,16},{4,20},{8,24},{12,28},{16,0},{20,4},{24,8},{28,12},{1,17},{... | collective-permute-start | bytes 1179656 | tf_op jit(solution)/shard_map/ppermute | solution.py:228
  63.3 1.3 %collective-permute-start.19 = (bf16[2,1,128,1024]{3,2,1,0:T(8,128)(2,1)}, bf16[2,1,128,1024]{3,2,1,0:T(8,128)(2,1)S(1)}, u32[]{:S(2)}, u32[]{:S(2)}) collective-permute-start(bf16[2,1,128,1024]{3,2,1,0:T(8,128)(2,1)} %collective-permute-done.17.refs_6_.refs_1_), channel_id=1, source_target_pairs={{1,0},{2,3},{5,4},{6,7},{9,8},{10,11},{13,12},{14,15},{17,16},{18,... | collective-permute-start | bytes 1572872 | tf_op jit(solution)/shard_map/ppermute | solution.py:200
  64.6 10.3 %collective-permute-done.16.refs_2_ = bf16[2,1,192,1024]{3,2,1,0:T(8,128)(2,1)} collective-permute-done((bf16[2,1,192,1024]{3,2,1,0:T(8,128)(2,1)}, bf16[2,1,192,1024]{3,2,1,0:T(8,128)(2,1)}, u32[]{:S(2)}, u32[]{:S(2)}) %collective-permute-start.16) | collective-permute-done | bytes 786464 | tf_op jit(solution)/shard_map/ppermute | solution.py:200
  74.9 4.3 %product.4 = (bf16[2,192,512]{2,1,0:T(8,128)(2,1)S(1)}, f32[2,192,512]{2,1,0:T(8,128)S(1)}, bf16[2,192,512]{2,1,0:T(8,128)(2,1)S(1)}, f32[2,192,512]{2,1,0:T(8,128)S(1)}) custom-call(s32[7]{0:T(128)S(1)} %stack.23.spot_ref, bf16[2,1,192,1024]{3,2,1,0:T(8,128)(2,1)S(1)} %copy-done.5, bf16[2,1,192,1024]{3,2,1,0:T(8,128)(2,1)} %collective-permute-done.11.refs_5_.refs_1_, ...), custom_call_target="tpu_custom_call" | custom-call | flops 1610612736 | bytes 6815744 | tf_op jit(solution)/shard_map/product/pallas_call | solution.py:130
  79.2 1.6 %collective-permute-start.18 = (bf16[2,192,512]{2,1,0:T(8,128)(2,1)S(1)}, bf16[2,192,512]{2,1,0:T(8,128)(2,1)S(1)}, u32[]{:S(2)}, u32[]{:S(2)}) collective-permute-start(bf16[2,192,512]{2,1,0:T(8,128)(2,1)S(1)} %get-tuple-element.43.refs_5_), channel_id=1, source_target_pairs={{0,8},{4,12},{8,0},{12,4},{16,24},{20,28},{24,16},{28,20},{1,9},{5... | collective-permute-start | bytes 1179656 | tf_op jit(solution)/shard_map/ppermute | solution.py:228
  80.7 1.5 %collective-permute-start.21 = (bf16[2,192,512]{2,1,0:T(8,128)(2,1)S(1)}, bf16[2,192,512]{2,1,0:T(8,128)(2,1)S(1)}, u32[]{:S(2)}, u32[]{:S(2)}) collective-permute-start(bf16[2,192,512]{2,1,0:T(8,128)(2,1)S(1)} %get-tuple-element.48), channel_id=1, source_target_pairs={{0,16},{4,20},{8,24},{12,28},{16,0},{20,4},{24,8},{28,12},{1,17},{... | collective-permute-start | bytes 1179656 | tf_op jit(solution)/shard_map/ppermute | solution.py:228
  82.2 0.1 convert_add_fusion.3
  82.4 0.6 collective-permute-start.13
  83.0 0.1 convert_add_fusion.2
  83.1 0.6 collective-permute-start.15
  83.7 0.2 collective-permute-done.19.refs_2_
  83.9 3.3 %product.5 = (bf16[2,128,512]{2,1,0:T(8,128)(2,1)S(1)}, f32[2,128,512]{2,1,0:T(8,128)S(1)}, bf16[2,128,512]{2,1,0:T(8,128)(2,1)S(1)}, f32[2,128,512]{2,1,0:T(8,128)S(1)}) custom-call(s32[7]{0:T(128)S(1)} %stack.23.spot_ref, bf16[2,1,128,1024]{3,2,1,0:T(8,128)(2,1)S(1)} %pad_maximum_fusion.2.refs_0_, ...), custom_call_target="tpu_custom_call" | custom-call | flops 1073741824 | bytes 5242880 | tf_op jit(solution)/shard_map/product/pallas_call | solution.py:130
  87.2 1.6 %collective-permute-start.23 = (bf16[2,128,512]{2,1,0:T(8,128)(2,1)S(1)}, bf16[2,128,512]{2,1,0:T(8,128)(2,1)S(1)}, u32[]{:S(2)}, u32[]{:S(2)}) collective-permute-start(bf16[2,128,512]{2,1,0:T(8,128)(2,1)S(1)} %get-tuple-element.45), channel_id=1, source_target_pairs={{0,8},{4,12},{8,0},{12,4},{16,24},{20,28},{24,16},{28,20},{1,9},{5... | collective-permute-start | bytes 786440 | tf_op jit(solution)/shard_map/ppermute | solution.py:228
  88.8 3.2 %collective-permute-done.13 = bf16[1,192,512]{2,1,0:T(8,128)(2,1)S(1)} collective-permute-done((bf16[1,192,512]{2,1,0:T(8,128)(2,1)S(1)}, bf16[1,192,512]{2,1,0:T(8,128)(2,1)S(1)}, u32[]{:S(2)}, u32[]{:S(2)}) %collective-permute-start.13) | collective-permute-done | bytes 196640 | tf_op jit(solution)/shard_map/ppermute | solution.py:228
  92.0 1.5 %collective-permute-start.25 = (bf16[2,128,512]{2,1,0:T(8,128)(2,1)S(1)}, bf16[2,128,512]{2,1,0:T(8,128)(2,1)S(1)}, u32[]{:S(2)}, u32[]{:S(2)}) collective-permute-start(bf16[2,128,512]{2,1,0:T(8,128)(2,1)S(1)} %get-tuple-element.52), channel_id=1, source_target_pairs={{0,16},{4,20},{8,24},{12,28},{16,0},{20,4},{24,8},{28,12},{1,17},{... | collective-permute-start | bytes 786440 | tf_op jit(solution)/shard_map/ppermute | solution.py:228
  93.6 0.1 fusion.5
  93.7 0.1 convert_add_fusion.1
  93.8 0.6 collective-permute-start.20
  94.4 0.1 convert_add_fusion
  94.6 0.6 collective-permute-start.22
  95.2 1.4 %collective-permute-done.23 = bf16[2,128,512]{2,1,0:T(8,128)(2,1)S(1)} collective-permute-done((bf16[2,128,512]{2,1,0:T(8,128)(2,1)S(1)}, bf16[2,128,512]{2,1,0:T(8,128)(2,1)S(1)}, u32[]{:S(2)}, u32[]{:S(2)}) %collective-permute-start.23) | collective-permute-done | bytes 262176 | tf_op jit(solution)/shard_map/ppermute | solution.py:228
  96.5 0.1 convert_add_fusion.5
  96.6 1.6 %collective-permute-start.24 = (bf16[1,128,512]{2,1,0:T(8,128)(2,1)S(1)}, bf16[1,128,512]{2,1,0:T(8,128)(2,1)S(1)}, u32[]{:S(2)}, u32[]{:S(2)}) collective-permute-start(bf16[1,128,512]{2,1,0:T(8,128)(2,1)S(1)} %slice.163), channel_id=1, source_target_pairs={{0,16},{4,20},{8,24},{12,28},{16,0},{20,4},{24,8},{28,12},{1,17},{... | collective-permute-start | bytes 393224 | tf_op jit(solution)/shard_map/ppermute | solution.py:228
  98.2 1.6 %collective-permute-done.25 = bf16[2,128,512]{2,1,0:T(8,128)(2,1)S(1)} collective-permute-done((bf16[2,128,512]{2,1,0:T(8,128)(2,1)S(1)}, bf16[2,128,512]{2,1,0:T(8,128)(2,1)S(1)}, u32[]{:S(2)}, u32[]{:S(2)}) %collective-permute-start.25) | collective-permute-done | bytes 262176 | tf_op jit(solution)/shard_map/ppermute | solution.py:228
  99.8 0.1 convert_add_fusion.4
  99.9 0.4 collective-permute-start.26
  100.3 1.6 %collective-permute-done.20 = bf16[1,192,512]{2,1,0:T(8,128)(2,1)S(1)} collective-permute-done((bf16[1,192,512]{2,1,0:T(8,128)(2,1)S(1)}, bf16[1,192,512]{2,1,0:T(8,128)(2,1)S(1)}, u32[]{:S(2)}, u32[]{:S(2)}) %collective-permute-start.20) | collective-permute-done | bytes 196640 | tf_op jit(solution)/shard_map/ppermute | solution.py:228
  101.9 0.1 fusion.3
  102.0 0.1 fusion.1
  102.0 1.3 %collective-permute-done.24 = bf16[1,128,512]{2,1,0:T(8,128)(2,1)S(1)} collective-permute-done((bf16[1,128,512]{2,1,0:T(8,128)(2,1)S(1)}, bf16[1,128,512]{2,1,0:T(8,128)(2,1)S(1)}, u32[]{:S(2)}, u32[]{:S(2)}) %collective-permute-start.24) | collective-permute-done | bytes 131104 | tf_op jit(solution)/shard_map/ppermute | solution.py:228
  103.3 1.6 %collective-permute-done.26 = bf16[1,128,512]{2,1,0:T(8,128)(2,1)S(1)} collective-permute-done((bf16[1,128,512]{2,1,0:T(8,128)(2,1)S(1)}, bf16[1,128,512]{2,1,0:T(8,128)(2,1)S(1)}, u32[]{:S(2)}, u32[]{:S(2)}) %collective-permute-start.26) | collective-permute-done | bytes 131104 | tf_op jit(solution)/shard_map/ppermute | solution.py:228
  105.0 1.5 %maximum_maximum_fusion = f32[512,1024]{1,0:T(8,128)} fusion(f32[128,512]{1,0:T(8,128)S(1)} %fusion.9, f32[128,512]{1,0:T(8,128)S(1)} %fusion.11, f32[192,512]{1,0:T(8,128)S(1)} %fusion.1, f32[192,512]{1,0:T(8,128)S(1)} %fusion.3, f32[192,512]{1,0:T(8,128)S(1)} %fusion.5, f32[192,512]{1,0:T(8,128)S(1)} %fusion.7), kind=kLoop, calls=%fused_computation | loop fusion | flops 2621440 | bytes 4194304 | tf_op jit(solution)/shard_map/concatenate | solution.py:288
  (47 shorter events, 0.5 us)
Async XLA Ops:
  1.9 2.1 %collective-permute-start.2 = (bf16[1,512,512]{2,1,0:T(8,128)(2,1)S(1)}, bf16[1,512,512]{2,1,0:T(8,128)(2,1)S(1)}, u32[]{:S(2)}, u32[]{:S(2)}) collective-permute-start(bf16[1,512,512]{2,1,0:T(8,128)(2,1)S(1)} %get-tuple-element.56), channel_id=1, source_target_pairs={{0,4},{4,0},{8,12},{12,8},{16,20},{20,16},{24,28},{28,24},{1,5},{5... | collective-permute-start | bytes 1572872 | tf_op jit(solution)/shard_map/ppermute | solution.py:228
  2.5 4.8 %copy-start.1 = (bf16[1024,512]{1,0:T(8,128)(2,1)S(1)}, bf16[1024,512]{1,0:T(8,128)(2,1)}, u32[]{:S(2)}) copy-start(bf16[1024,512]{1,0:T(8,128)(2,1)} %k_ref.1) | copy-start | bytes 3145732
  2.5 4.8 %copy-start.2 = (bf16[1024,512]{1,0:T(8,128)(2,1)S(1)}, bf16[1024,512]{1,0:T(8,128)(2,1)}, u32[]{:S(2)}) copy-start(bf16[1024,512]{1,0:T(8,128)(2,1)} %v_ref.1) | copy-start | bytes 3145732
  2.5 6.6 %copy-start = (bf16[1024,512]{1,0:T(8,128)(2,1)S(1)}, bf16[1024,512]{1,0:T(8,128)(2,1)}, u32[]{:S(2)}) copy-start(bf16[1024,512]{1,0:T(8,128)(2,1)} %q_ref.1) | copy-start | bytes 3145732
  2.5 6.6 %copy-start.3 = (bf16[1024,512]{1,0:T(8,128)(2,1)S(1)}, bf16[1024,512]{1,0:T(8,128)(2,1)}, u32[]{:S(2)}) copy-start(bf16[1024,512]{1,0:T(8,128)(2,1)} %go_ref.1) | copy-start | bytes 3145732
  4.0 12.9 %collective-permute-start.3 = (bf16[1,1,192,1024]{3,2,1,0:T(8,128)(2,1)S(1)}, bf16[1,1,192,1024]{3,2,1,0:T(8,128)(2,1)S(1)}, u32[]{:S(2)}, u32[]{:S(2)}) collective-permute-start(bf16[1,1,192,1024]{3,2,1,0:T(8,128)(2,1)S(1)} %maximum_bitcast_fusion.1), channel_id=1, source_target_pairs={{0,1},{1,0},{2,3},{3,2},{4,5},{5,4},{6,7},{7,6},{8,9},{9,8},{10,11... | collective-permute-start | bytes 1179656 | tf_op jit(solution)/shard_map/ppermute | solution.py:179
  7.1 11.5 %copy-start.6 = (bf16[64,128]{1,0:T(8,128)(2,1)S(1)}, bf16[64,128]{1,0:T(8,128)(2,1)}, u32[]{:S(2)}) copy-start(bf16[64,128]{1,0:T(8,128)(2,1)} %f_ref.1) | copy-start | bytes 49156
  7.2 23.3 %collective-permute-start.8 = (bf16[1,1,320,1024]{3,2,1,0:T(8,128)(2,1)S(1)}, bf16[1,1,320,1024]{3,2,1,0:T(8,128)(2,1)S(1)}, u32[]{:S(2)}, u32[]{:S(2)}) collective-permute-start(bf16[1,1,320,1024]{3,2,1,0:T(8,128)(2,1)S(1)} %maximum_bitcast_fusion), channel_id=1, source_target_pairs={{0,1},{1,0},{2,3},{3,2},{4,5},{5,4},{6,7},{7,6},{8,9},{9,8},{10,11... | collective-permute-start | bytes 1966088 | tf_op jit(solution)/shard_map/ppermute | solution.py:179
  7.4 11.2 %collective-permute-start = (bf16[1024,128]{1,0:T(8,128)(2,1)S(1)}, bf16[1024,128]{1,0:T(8,128)(2,1)S(1)}, u32[]{:S(2)}, u32[]{:S(2)}) collective-permute-start(bf16[1024,128]{1,0:T(8,128)(2,1)S(1)} %multiply_convert_fusion.1), channel_id=1, source_target_pairs={{0,4},{4,8},{8,12},{12,16},{16,20},{20,24},{24,28},{1,5},{5,9},{9,... | collective-permute-start | bytes 786440 | tf_op jit(solution)/shard_map/ppermute | solution.py:248
  9.2 9.4 %collective-permute-start.1 = (bf16[1024,128]{1,0:T(8,128)(2,1)S(1)}, bf16[1024,128]{1,0:T(8,128)(2,1)S(1)}, u32[]{:S(2)}, u32[]{:S(2)}) collective-permute-start(bf16[1024,128]{1,0:T(8,128)(2,1)S(1)} %multiply_convert_fusion), channel_id=1, source_target_pairs={{4,0},{8,4},{12,8},{16,12},{20,16},{24,20},{28,24},{5,1},{9,5},{13... | collective-permute-start | bytes 786440 | tf_op jit(solution)/shard_map/ppermute | solution.py:249
  17.0 15.3 %collective-permute-start.7 = (bf16[2,1,192,1024]{3,2,1,0:T(8,128)(2,1)S(1)}, bf16[2,1,192,1024]{3,2,1,0:T(8,128)(2,1)}, u32[]{:S(2)}, u32[]{:S(2)}) collective-permute-start(bf16[2,1,192,1024]{3,2,1,0:T(8,128)(2,1)S(1)} %pad_maximum_fusion.refs_0_), channel_id=1, source_target_pairs={{1,2},{2,1},{5,6},{6,5},{9,10},{10,9},{13,14},{14,13},{17,18},{18,... | collective-permute-start | bytes 2359304 | tf_op jit(solution)/shard_map/ppermute | solution.py:192
  30.7 12.9 %copy-start.4 = (bf16[2,1,192,1024]{3,2,1,0:T(8,128)(2,1)}, bf16[2,1,192,1024]{3,2,1,0:T(8,128)(2,1)S(1)}, u32[]{:S(2)}) copy-start(bf16[2,1,192,1024]{3,2,1,0:T(8,128)(2,1)S(1)} %pad_maximum_fusion.1.refs_0_) | copy-start | bytes 2359300
  30.7 12.9 %collective-permute-start.11 = (bf16[2,1,192,1024]{3,2,1,0:T(8,128)(2,1)S(1)}, bf16[2,1,192,1024]{3,2,1,0:T(8,128)(2,1)}, u32[]{:S(2)}, u32[]{:S(2)}) collective-permute-start(bf16[2,1,192,1024]{3,2,1,0:T(8,128)(2,1)S(1)} %pad_maximum_fusion.1.refs_0_), channel_id=1, source_target_pairs={{1,2},{2,1},{5,6},{6,5},{9,10},{10,9},{13,14},{14,13},{17,18},{18,... | collective-permute-start | bytes 2359304 | tf_op jit(solution)/shard_map/ppermute | solution.py:192
  32.2 14.2 %collective-permute-start.10 = (bf16[512,1024]{1,0:T(8,128)(2,1)S(1)}, bf16[512,1024]{1,0:T(8,128)(2,1)S(1)}, u32[]{:S(2)}, u32[]{:S(2)}) collective-permute-start(bf16[512,1024]{1,0:T(8,128)(2,1)S(1)} %get-tuple-element.36.refs_3_), channel_id=1, source_target_pairs={{0,4},{4,0},{8,12},{12,8},{16,20},{20,16},{24,28},{28,24},{1,5},{5... | collective-permute-start | bytes 3145736 | tf_op jit(solution)/shard_map/ppermute | solution.py:228
  32.4 23.6 %collective-permute-start.9 = (bf16[2,1,192,1024]{3,2,1,0:T(8,128)(2,1)}, bf16[2,1,192,1024]{3,2,1,0:T(8,128)(2,1)}, u32[]{:S(2)}, u32[]{:S(2)}) collective-permute-start(bf16[2,1,192,1024]{3,2,1,0:T(8,128)(2,1)} %collective-permute-done.7.refs_1_), channel_id=1, source_target_pairs={{1,0},{2,3},{5,4},{6,7},{9,8},{10,11},{13,12},{14,15},{17,16},{18,... | collective-permute-start | bytes 2359304 | tf_op jit(solution)/shard_map/ppermute | solution.py:200
  33.7 1.4 %collective-permute-start.4 = (f32[64,128]{1,0:T(8,128)S(1)}, f32[64,128]{1,0:T(8,128)S(1)}, u32[]{:S(2)}, u32[]{:S(2)}) collective-permute-start(f32[64,128]{1,0:T(8,128)S(1)} %get-tuple-element.32), channel_id=1, source_target_pairs={{0,4},{4,0},{8,12},{12,8},{16,20},{20,16},{24,28},{28,24},{1,5},{5... | collective-permute-start | bytes 98312 | tf_op jit(solution)/shard_map/ppermute | solution.py:228
  35.1 3.9 %collective-permute-start.5 = (f32[64,128]{1,0:T(8,128)S(1)}, f32[64,128]{1,0:T(8,128)S(1)}, u32[]{:S(2)}, u32[]{:S(2)}) collective-permute-start(f32[64,128]{1,0:T(8,128)S(1)} %add.141), channel_id=1, source_target_pairs={{0,8},{4,12},{8,0},{12,4},{16,24},{20,28},{24,16},{28,20},{1,9},{5... | collective-permute-start | bytes 98312 | tf_op jit(solution)/shard_map/ppermute | solution.py:228
  39.0 3.9 %collective-permute-start.6 = (f32[64,128]{1,0:T(8,128)S(1)}, f32[64,128]{1,0:T(8,128)S(1)}, u32[]{:S(2)}, u32[]{:S(2)}) collective-permute-start(f32[64,128]{1,0:T(8,128)S(1)} %add.142), channel_id=1, source_target_pairs={{0,16},{4,20},{8,24},{12,28},{16,0},{20,4},{24,8},{28,12},{1,17},{... | collective-permute-start | bytes 98312 | tf_op jit(solution)/shard_map/ppermute | solution.py:228
  43.6 31.3 %collective-permute-start.16 = (bf16[2,1,192,1024]{3,2,1,0:T(8,128)(2,1)}, bf16[2,1,192,1024]{3,2,1,0:T(8,128)(2,1)}, u32[]{:S(2)}, u32[]{:S(2)}) collective-permute-start(bf16[2,1,192,1024]{3,2,1,0:T(8,128)(2,1)} %collective-permute-done.11.refs_5_.refs_1_), channel_id=1, source_target_pairs={{1,0},{2,3},{5,4},{6,7},{9,8},{10,11},{13,12},{14,15},{17,16},{18,... | collective-permute-start | bytes 2359304 | tf_op jit(solution)/shard_map/ppermute | solution.py:200
  44.9 18.4 %collective-permute-start.17 = (bf16[2,1,128,1024]{3,2,1,0:T(8,128)(2,1)S(1)}, bf16[2,1,128,1024]{3,2,1,0:T(8,128)(2,1)}, u32[]{:S(2)}, u32[]{:S(2)}) collective-permute-start(bf16[2,1,128,1024]{3,2,1,0:T(8,128)(2,1)S(1)} %pad_maximum_fusion.2.refs_0_), channel_id=1, source_target_pairs={{1,2},{2,1},{5,6},{6,5},{9,10},{10,9},{13,14},{14,13},{17,18},{18,... | collective-permute-start | bytes 1572872 | tf_op jit(solution)/shard_map/ppermute | solution.py:192
  46.4 28.5 %copy-start.5 = (bf16[2,1,192,1024]{3,2,1,0:T(8,128)(2,1)S(1)}, bf16[2,1,192,1024]{3,2,1,0:T(8,128)(2,1)}, u32[]{:S(2)}) copy-start(bf16[2,1,192,1024]{3,2,1,0:T(8,128)(2,1)} %copy-done.4) | copy-start | bytes 2359300
  60.2 22.0 %collective-permute-start.12 = (bf16[2,192,512]{2,1,0:T(8,128)(2,1)S(1)}, bf16[2,192,512]{2,1,0:T(8,128)(2,1)S(1)}, u32[]{:S(2)}, u32[]{:S(2)}) collective-permute-start(bf16[2,192,512]{2,1,0:T(8,128)(2,1)S(1)} %get-tuple-element.38.refs_5_), channel_id=1, source_target_pairs={{0,8},{4,12},{8,0},{12,4},{16,24},{20,28},{24,16},{28,20},{1,9},{5... | collective-permute-start | bytes 1179656 | tf_op jit(solution)/shard_map/ppermute | solution.py:228
  61.7 21.2 %collective-permute-start.14 = (bf16[2,192,512]{2,1,0:T(8,128)(2,1)S(1)}, bf16[2,192,512]{2,1,0:T(8,128)(2,1)S(1)}, u32[]{:S(2)}, u32[]{:S(2)}) collective-permute-start(bf16[2,192,512]{2,1,0:T(8,128)(2,1)S(1)} %get-tuple-element.40), channel_id=1, source_target_pairs={{0,16},{4,20},{8,24},{12,28},{16,0},{20,4},{24,8},{28,12},{1,17},{... | collective-permute-start | bytes 1179656 | tf_op jit(solution)/shard_map/ppermute | solution.py:228
  63.3 20.6 %collective-permute-start.19 = (bf16[2,1,128,1024]{3,2,1,0:T(8,128)(2,1)}, bf16[2,1,128,1024]{3,2,1,0:T(8,128)(2,1)S(1)}, u32[]{:S(2)}, u32[]{:S(2)}) collective-permute-start(bf16[2,1,128,1024]{3,2,1,0:T(8,128)(2,1)} %collective-permute-done.17.refs_6_.refs_1_), channel_id=1, source_target_pairs={{1,0},{2,3},{5,4},{6,7},{9,8},{10,11},{13,12},{14,15},{17,16},{18,... | collective-permute-start | bytes 1572872 | tf_op jit(solution)/shard_map/ppermute | solution.py:200
  79.2 14.5 %collective-permute-start.18 = (bf16[2,192,512]{2,1,0:T(8,128)(2,1)S(1)}, bf16[2,192,512]{2,1,0:T(8,128)(2,1)S(1)}, u32[]{:S(2)}, u32[]{:S(2)}) collective-permute-start(bf16[2,192,512]{2,1,0:T(8,128)(2,1)S(1)} %get-tuple-element.43.refs_5_), channel_id=1, source_target_pairs={{0,8},{4,12},{8,0},{12,4},{16,24},{20,28},{24,16},{28,20},{1,9},{5... | collective-permute-start | bytes 1179656 | tf_op jit(solution)/shard_map/ppermute | solution.py:228
  80.7 13.7 %collective-permute-start.21 = (bf16[2,192,512]{2,1,0:T(8,128)(2,1)S(1)}, bf16[2,192,512]{2,1,0:T(8,128)(2,1)S(1)}, u32[]{:S(2)}, u32[]{:S(2)}) collective-permute-start(bf16[2,192,512]{2,1,0:T(8,128)(2,1)S(1)} %get-tuple-element.48), channel_id=1, source_target_pairs={{0,16},{4,20},{8,24},{12,28},{16,0},{20,4},{24,8},{28,12},{1,17},{... | collective-permute-start | bytes 1179656 | tf_op jit(solution)/shard_map/ppermute | solution.py:228
  82.4 9.6 %collective-permute-start.13 = (bf16[1,192,512]{2,1,0:T(8,128)(2,1)S(1)}, bf16[1,192,512]{2,1,0:T(8,128)(2,1)S(1)}, u32[]{:S(2)}, u32[]{:S(2)}) collective-permute-start(bf16[1,192,512]{2,1,0:T(8,128)(2,1)S(1)} %slice.161), channel_id=1, source_target_pairs={{0,16},{4,20},{8,24},{12,28},{16,0},{20,4},{24,8},{28,12},{1,17},{... | collective-permute-start | bytes 589832 | tf_op jit(solution)/shard_map/ppermute | solution.py:228
  83.1 10.5 %collective-permute-start.15 = (bf16[1,192,512]{2,1,0:T(8,128)(2,1)S(1)}, bf16[1,192,512]{2,1,0:T(8,128)(2,1)S(1)}, u32[]{:S(2)}, u32[]{:S(2)}) collective-permute-start(bf16[1,192,512]{2,1,0:T(8,128)(2,1)S(1)} %slice.160), channel_id=1, source_target_pairs={{0,8},{4,12},{8,0},{12,4},{16,24},{20,28},{24,16},{28,20},{1,9},{5... | collective-permute-start | bytes 589832 | tf_op jit(solution)/shard_map/ppermute | solution.py:228
  87.2 9.3 %collective-permute-start.23 = (bf16[2,128,512]{2,1,0:T(8,128)(2,1)S(1)}, bf16[2,128,512]{2,1,0:T(8,128)(2,1)S(1)}, u32[]{:S(2)}, u32[]{:S(2)}) collective-permute-start(bf16[2,128,512]{2,1,0:T(8,128)(2,1)S(1)} %get-tuple-element.45), channel_id=1, source_target_pairs={{0,8},{4,12},{8,0},{12,4},{16,24},{20,28},{24,16},{28,20},{1,9},{5... | collective-permute-start | bytes 786440 | tf_op jit(solution)/shard_map/ppermute | solution.py:228
  92.0 7.8 %collective-permute-start.25 = (bf16[2,128,512]{2,1,0:T(8,128)(2,1)S(1)}, bf16[2,128,512]{2,1,0:T(8,128)(2,1)S(1)}, u32[]{:S(2)}, u32[]{:S(2)}) collective-permute-start(bf16[2,128,512]{2,1,0:T(8,128)(2,1)S(1)} %get-tuple-element.52), channel_id=1, source_target_pairs={{0,16},{4,20},{8,24},{12,28},{16,0},{20,4},{24,8},{28,12},{1,17},{... | collective-permute-start | bytes 786440 | tf_op jit(solution)/shard_map/ppermute | solution.py:228
  93.8 8.1 %collective-permute-start.20 = (bf16[1,192,512]{2,1,0:T(8,128)(2,1)S(1)}, bf16[1,192,512]{2,1,0:T(8,128)(2,1)S(1)}, u32[]{:S(2)}, u32[]{:S(2)}) collective-permute-start(bf16[1,192,512]{2,1,0:T(8,128)(2,1)S(1)} %slice.159), channel_id=1, source_target_pairs={{0,16},{4,20},{8,24},{12,28},{16,0},{20,4},{24,8},{28,12},{1,17},{... | collective-permute-start | bytes 589832 | tf_op jit(solution)/shard_map/ppermute | solution.py:228
  94.6 7.4 %collective-permute-start.22 = (bf16[1,192,512]{2,1,0:T(8,128)(2,1)S(1)}, bf16[1,192,512]{2,1,0:T(8,128)(2,1)S(1)}, u32[]{:S(2)}, u32[]{:S(2)}) collective-permute-start(bf16[1,192,512]{2,1,0:T(8,128)(2,1)S(1)} %slice.158), channel_id=1, source_target_pairs={{0,8},{4,12},{8,0},{12,4},{16,24},{20,28},{24,16},{28,20},{1,9},{5... | collective-permute-start | bytes 589832 | tf_op jit(solution)/shard_map/ppermute | solution.py:228
  96.6 6.7 %collective-permute-start.24 = (bf16[1,128,512]{2,1,0:T(8,128)(2,1)S(1)}, bf16[1,128,512]{2,1,0:T(8,128)(2,1)S(1)}, u32[]{:S(2)}, u32[]{:S(2)}) collective-permute-start(bf16[1,128,512]{2,1,0:T(8,128)(2,1)S(1)} %slice.163), channel_id=1, source_target_pairs={{0,16},{4,20},{8,24},{12,28},{16,0},{20,4},{24,8},{28,12},{1,17},{... | collective-permute-start | bytes 393224 | tf_op jit(solution)/shard_map/ppermute | solution.py:228
  99.9 5.0 %collective-permute-start.26 = (bf16[1,128,512]{2,1,0:T(8,128)(2,1)S(1)}, bf16[1,128,512]{2,1,0:T(8,128)(2,1)S(1)}, u32[]{:S(2)}, u32[]{:S(2)}) collective-permute-start(bf16[1,128,512]{2,1,0:T(8,128)(2,1)S(1)} %slice.162), channel_id=1, source_target_pairs={{0,8},{4,12},{8,0},{12,4},{16,24},{20,28},{24,16},{28,20},{1,9},{5... | collective-permute-start | bytes 393224 | tf_op jit(solution)/shard_map/ppermute | solution.py:228

commit v4 on v3

--- a/solution.py
+++ b/solution.py
@@ -272,19 +272,23 @@
         spot = jnp.stack([chip, *holders]).astype(jnp.int32)
         after = [outs[0] for outs in products[-1:]] + ahead
         products.append(product_call(across, chips, spot, arrays, turned, sibling, after))
-    done = []
-    for number, outs in enumerate(products):
+    done, sums = [None] * len(products), []
+    for number in reversed(range(len(products))):
         late = [outs[0] for outs in products[number + 1 :]] if number + 2 == len(products) else []
-        columns = []
+        columns, ended = [], list(sums)
         for order, path in enumerate(across):
-            send, keep = outs[2 * order], outs[2 * order + 1]
+            send, keep = products[number][2 * order : 2 * order + 2]
             for stage, bit in enumerate(path):
-                keep = keep + flip(send, 2 << bit).astype(F32)
+                arrived = flip(send, 2 << bit)
                 if stage + 1 < len(path):
+                    keep = keep + arrived.astype(F32)
                     count = keep.shape[0] // 2
                     send, keep = tied(keep[count:].astype(BF16), late), keep[:count]
+                    sums += [send] if number + 1 == len(products) else []
+                else:
+                    keep = keep + tied(arrived, ended).astype(F32)
             columns.append(keep[0] * total_tokens ** (-0.5))
-        done.append(jnp.concatenate(columns, axis=1))
+        done[number] = jnp.concatenate(columns, axis=1)
     grad_weight = jnp.concatenate(done, axis=0)
     return (grad_query, grad_key, grad_value, grad_filters, grad_weight)
 

time: 107 us -> 106 us (level)
  waiting for transfers between devices: 47.5 us -> 45.3 us
  starting transfers between devices: 32.6 us -> 33.7 us
    ppermute x17, waiting for transfers between devices: 17.4 us -> 15.3 us  [flip(): lax.ppermute(array, 'ctx', [(i, i ^ distance) for i in range(ctx_count)])]
    ppermute x17, starting transfers between devices: 18 us -> 19.1 us  [flip(): lax.ppermute(array, 'ctx', [(i, i ^ distance) for i in range(ctx_count)])]
  transfers between devices with their start and end apart: 27 -> 27, of which waited for: 15 -> 13; matrix products, arithmetic and copies ran while one was open for 2% -> 2% of each run, Pallas kernels for 19% -> 19%
where the time goes in v4:
time: 106 us; the launch traced here: 105 us
  waiting for transfers between devices  45.3 us (43%)
  starting transfers between devices  33.7 us (32%)
  Pallas kernels  20.2 us (19%)
  other arithmetic  3.46 us (3%)
  local copies, waits for them, and re-layouts  1.7 us (2%)
  between operations  1.07 us (1%)
    ppermute x3, waiting for transfers between devices, gather_rest(): arrived = lax.ppermute(arrived, axis, hop_pairs(count, group, hop))  20 us
    ppermute x17, starting transfers between devices, flip(): lax.ppermute(array, 'ctx', [(i, i ^ distance) for i in range(ctx_count)])  19.1 us
    ppermute x17, waiting for transfers between devices, flip(): lax.ppermute(array, 'ctx', [(i, i ^ distance) for i in range(ctx_count)])  15.3 us
    pallas_call x3, Pallas kernels, product_call(): pl.pallas_call(functools.partial(product_kernel, orders, len(sources)), g...  11.8 us
    ppermute x2, waiting for transfers between devices, gather_groups(): merged = arrived = lax.ppermute(stack, axis, hop_pairs(count, group, 0))  9.97 us
    pallas_call x1, Pallas kernels, conv_call(): pl.pallas_call(functools.partial(conv_kernel, width, taps), grid=(groups...  8.36 us
    ppermute x3, starting transfers between devices, gather_swap(): arrived = lax.ppermute(stack, axis, hop_pairs(count, group, 0))  4.58 us
    ppermute x3, starting transfers between devices, gather_rest(): arrived = lax.ppermute(arrived, axis, hop_pairs(count, group, hop))  3.85 us
  transfers between devices with their start and end apart: 27, of which 13 were waited for; matrix products, arithmetic and copies ran while one was open for 2% of the time, Pallas kernels for 19%

profile of v4, /device:TPU:0, one launch (start us, length us, event | category | flops | bytes accessed | tf_op | source)
XLA Modules:
  0.0 105.4 jit_solution(3812120970044493826)
XLA Ops:
  0.7 1.3 %dynamic-slice_bitcast_fusion.1 = (bf16[1,512,512]{2,1,0:T(8,128)(2,1)S(1)}, bf16[1,512,512]{2,1,0:T(8,128)(2,1)S(1)}) fusion(bf16[1,2,512,512]{3,2,1,0:T(8,128)(2,1)} %bitcast.28, s32[]{:T(128)S(6)} %select_n.230, s32[]{:T(128)S(6)} %select_n.231), kind=kLoop, calls=%fused_computation.12 | loop fusion | bytes 2097160 | tf_op jit(solution)/shard_map/jit(dynamic_index_in_dim)/squeeze | solution.py:233
  1.9 0.5 collective-permute-start.2
  2.5 0.0 copy-start.3
  2.5 1.5 %collective-permute-done.2 = bf16[1,512,512]{2,1,0:T(8,128)(2,1)S(1)} collective-permute-done((bf16[1,512,512]{2,1,0:T(8,128)(2,1)S(1)}, bf16[1,512,512]{2,1,0:T(8,128)(2,1)S(1)}, u32[]{:S(2)}, u32[]{:S(2)}) %collective-permute-start.2) | collective-permute-done | bytes 524320 | tf_op jit(solution)/shard_map/ppermute | solution.py:228
  4.0 3.0 %collective-permute-start.3 = (bf16[1,1,192,1024]{3,2,1,0:T(8,128)(2,1)S(1)}, bf16[1,1,192,1024]{3,2,1,0:T(8,128)(2,1)S(1)}, u32[]{:S(2)}, u32[]{:S(2)}) collective-permute-start(bf16[1,1,192,1024]{3,2,1,0:T(8,128)(2,1)S(1)} %maximum_bitcast_fusion.1), channel_id=1, source_target_pairs={{0,1},{1,0},{2,3},{3,2},{4,5},{5,4},{6,7},{7,6},{8,9},{9,8},{10,11... | collective-permute-start | bytes 1179656 | tf_op jit(solution)/shard_map/ppermute | solution.py:179
  7.1 0.1 maximum_bitcast_fusion
  7.2 0.1 collective-permute-start.8
  7.3 0.1 multiply_convert_fusion.1
  7.4 1.8 %collective-permute-start = (bf16[1024,128]{1,0:T(8,128)(2,1)S(1)}, bf16[1024,128]{1,0:T(8,128)(2,1)S(1)}, u32[]{:S(2)}, u32[]{:S(2)}) collective-permute-start(bf16[1024,128]{1,0:T(8,128)(2,1)S(1)} %multiply_convert_fusion.1), channel_id=1, source_target_pairs={{0,4},{4,8},{8,12},{12,16},{16,20},{20,24},{24,28},{1,5},{5,9},{9,... | collective-permute-start | bytes 786440 | tf_op jit(solution)/shard_map/ppermute | solution.py:248
  9.2 0.1 multiply_convert_fusion
  9.2 1.3 %collective-permute-start.1 = (bf16[1024,128]{1,0:T(8,128)(2,1)S(1)}, bf16[1024,128]{1,0:T(8,128)(2,1)S(1)}, u32[]{:S(2)}, u32[]{:S(2)}) collective-permute-start(bf16[1024,128]{1,0:T(8,128)(2,1)S(1)} %multiply_convert_fusion), channel_id=1, source_target_pairs={{4,0},{8,4},{12,8},{16,12},{20,16},{24,20},{28,24},{5,1},{9,5},{13... | collective-permute-start | bytes 786440 | tf_op jit(solution)/shard_map/ppermute | solution.py:249
  10.5 6.4 %collective-permute-done.3.after_ref = bf16[1,1,192,1024]{3,2,1,0:T(8,128)(2,1)S(1)} collective-permute-done((bf16[1,1,192,1024]{3,2,1,0:T(8,128)(2,1)S(1)}, bf16[1,1,192,1024]{3,2,1,0:T(8,128)(2,1)S(1)}, u32[]{:S(2)}, u32[]{:S(2)}) %collective-permute-start.3) | collective-permute-done | bytes 393248 | tf_op jit(solution)/shard_map/ppermute | solution.py:179
  17.0 0.1 pad_maximum_fusion.refs_0_
  17.0 1.6 %collective-permute-start.7 = (bf16[2,1,192,1024]{3,2,1,0:T(8,128)(2,1)S(1)}, bf16[2,1,192,1024]{3,2,1,0:T(8,128)(2,1)}, u32[]{:S(2)}, u32[]{:S(2)}) collective-permute-start(bf16[2,1,192,1024]{3,2,1,0:T(8,128)(2,1)S(1)} %pad_maximum_fusion.refs_0_), channel_id=1, source_target_pairs={{1,2},{2,1},{5,6},{6,5},{9,10},{10,9},{13,14},{14,13},{17,18},{18,... | collective-permute-start | bytes 2359304 | tf_op jit(solution)/shard_map/ppermute | solution.py:192
  18.6 8.4 %conv.1 = (bf16[1024,512]{1,0:T(8,128)(2,1)}, bf16[1024,512]{1,0:T(8,128)(2,1)}, bf16[1024,512]{1,0:T(8,128)(2,1)}, f32[64,128]{1,0:T(8,128)S(1)}, bf16[512,1024]{1,0:T(8,128)(2,1)S(1)}) custom-call(bf16[1024,512]{1,0:T(8,128)(2,1)S(1)} %copy-done, bf16[1024,512]{1,0:T(8,128)(2,1)S(1)} %copy-done.1, bf16[1024,512]{1,0:T(8,128)(2,1)S(1)} %copy-done.2, ...), custom_call_target="tpu_custom_call" | custom-call | flops 1073741824 | bytes 8388608 | tf_op jit(solution)/shard_map/conv/pallas_call | solution.py:60
  27.0 3.6 %collective-permute-done.8 = bf16[1,1,320,1024]{3,2,1,0:T(8,128)(2,1)S(1)} collective-permute-done((bf16[1,1,320,1024]{3,2,1,0:T(8,128)(2,1)S(1)}, bf16[1,1,320,1024]{3,2,1,0:T(8,128)(2,1)S(1)}, u32[]{:S(2)}, u32[]{:S(2)}) %collective-permute-start.8) | collective-permute-done | bytes 655392 | tf_op jit(solution)/shard_map/ppermute | solution.py:179
  30.6 0.1 pad_maximum_fusion.1.refs_0_
  30.7 1.6 %collective-permute-start.11 = (bf16[2,1,192,1024]{3,2,1,0:T(8,128)(2,1)S(1)}, bf16[2,1,192,1024]{3,2,1,0:T(8,128)(2,1)}, u32[]{:S(2)}, u32[]{:S(2)}) collective-permute-start(bf16[2,1,192,1024]{3,2,1,0:T(8,128)(2,1)S(1)} %pad_maximum_fusion.1.refs_0_), channel_id=1, source_target_pairs={{1,2},{2,1},{5,6},{6,5},{9,10},{10,9},{13,14},{14,13},{17,18},{18,... | collective-permute-start | bytes 2359304 | tf_op jit(solution)/shard_map/ppermute | solution.py:192
  32.3 0.1 pad_maximum_fusion.2.refs_0_
  32.4 1.3 %collective-permute-start.9 = (bf16[2,1,192,1024]{3,2,1,0:T(8,128)(2,1)}, bf16[2,1,192,1024]{3,2,1,0:T(8,128)(2,1)}, u32[]{:S(2)}, u32[]{:S(2)}) collective-permute-start(bf16[2,1,192,1024]{3,2,1,0:T(8,128)(2,1)} %collective-permute-done.7.refs_1_), channel_id=1, source_target_pairs={{1,0},{2,3},{5,4},{6,7},{9,8},{10,11},{13,12},{14,15},{17,16},{18,... | collective-permute-start | bytes 2359304 | tf_op jit(solution)/shard_map/ppermute | solution.py:200
  33.7 0.6 collective-permute-start.4
  34.2 0.9 collective-permute-done.4
  35.1 1.7 %collective-permute-start.5 = (f32[64,128]{1,0:T(8,128)S(1)}, f32[64,128]{1,0:T(8,128)S(1)}, u32[]{:S(2)}, u32[]{:S(2)}) collective-permute-start(f32[64,128]{1,0:T(8,128)S(1)} %add.141), channel_id=1, source_target_pairs={{0,8},{4,12},{8,0},{12,4},{16,24},{20,28},{24,16},{28,20},{1,9},{5... | collective-permute-start | bytes 98312 | tf_op jit(solution)/shard_map/ppermute | solution.py:228
  36.8 2.3 %collective-permute-done.5 = f32[64,128]{1,0:T(8,128)S(1)} collective-permute-done((f32[64,128]{1,0:T(8,128)S(1)}, f32[64,128]{1,0:T(8,128)S(1)}, u32[]{:S(2)}, u32[]{:S(2)}) %collective-permute-start.5) | collective-permute-done | bytes 32800 | tf_op jit(solution)/shard_map/ppermute | solution.py:228
  39.0 1.7 %collective-permute-start.6 = (f32[64,128]{1,0:T(8,128)S(1)}, f32[64,128]{1,0:T(8,128)S(1)}, u32[]{:S(2)}, u32[]{:S(2)}) collective-permute-start(f32[64,128]{1,0:T(8,128)S(1)} %add.142), channel_id=1, source_target_pairs={{0,16},{4,20},{8,24},{12,28},{16,0},{20,4},{24,8},{28,12},{1,17},{... | collective-permute-start | bytes 98312 | tf_op jit(solution)/shard_map/ppermute | solution.py:228
  40.7 2.2 %collective-permute-done.6 = f32[64,128]{1,0:T(8,128)S(1)} collective-permute-done((f32[64,128]{1,0:T(8,128)S(1)}, f32[64,128]{1,0:T(8,128)S(1)}, u32[]{:S(2)}, u32[]{:S(2)}) %collective-permute-start.6) | collective-permute-done | bytes 32800 | tf_op jit(solution)/shard_map/ppermute | solution.py:228
  42.9 0.6 broadcast_multiply_fusion
  43.6 1.3 %collective-permute-start.16 = (bf16[2,1,192,1024]{3,2,1,0:T(8,128)(2,1)}, bf16[2,1,192,1024]{3,2,1,0:T(8,128)(2,1)}, u32[]{:S(2)}, u32[]{:S(2)}) collective-permute-start(bf16[2,1,192,1024]{3,2,1,0:T(8,128)(2,1)} %collective-permute-done.11.refs_5_.refs_1_), channel_id=1, source_target_pairs={{1,0},{2,3},{5,4},{6,7},{9,8},{10,11},{13,12},{14,15},{17,16},{18,... | collective-permute-start | bytes 2359304 | tf_op jit(solution)/shard_map/ppermute | solution.py:200
  44.9 1.5 %collective-permute-start.14 = (bf16[2,1,128,1024]{3,2,1,0:T(8,128)(2,1)S(1)}, bf16[2,1,128,1024]{3,2,1,0:T(8,128)(2,1)}, u32[]{:S(2)}, u32[]{:S(2)}) collective-permute-start(bf16[2,1,128,1024]{3,2,1,0:T(8,128)(2,1)S(1)} %pad_maximum_fusion.2.refs_0_), channel_id=1, source_target_pairs={{1,2},{2,1},{5,6},{6,5},{9,10},{10,9},{13,14},{14,13},{17,18},{18,... | collective-permute-start | bytes 1572872 | tf_op jit(solution)/shard_map/ppermute | solution.py:192
  46.3 0.1 stack.23.spot_ref
  46.4 9.5 %collective-permute-done.9.refs_2_ = bf16[2,1,192,1024]{3,2,1,0:T(8,128)(2,1)} collective-permute-done((bf16[2,1,192,1024]{3,2,1,0:T(8,128)(2,1)}, bf16[2,1,192,1024]{3,2,1,0:T(8,128)(2,1)}, u32[]{:S(2)}, u32[]{:S(2)}) %collective-permute-start.9) | collective-permute-done | bytes 786464 | tf_op jit(solution)/shard_map/ppermute | solution.py:200
  55.9 4.3 %product.3 = (bf16[2,192,512]{2,1,0:T(8,128)(2,1)S(1)}, f32[2,192,512]{2,1,0:T(8,128)S(1)}, bf16[2,192,512]{2,1,0:T(8,128)(2,1)S(1)}, f32[2,192,512]{2,1,0:T(8,128)S(1)}) custom-call(s32[7]{0:T(128)S(1)} %stack.23.spot_ref, bf16[2,1,192,1024]{3,2,1,0:T(8,128)(2,1)S(1)} %pad_maximum_fusion.refs_0_, bf16[2,1,192,1024]{3,2,1,0:T(8,128)(2,1)} %collective-permute-done.7.refs_1_, ...), custom_call_target="tpu_custom_call" | custom-call | flops 1610612736 | bytes 6815744 | tf_op jit(solution)/shard_map/product/pallas_call | solution.py:130
  60.2 1.6 %collective-permute-start.19 = (bf16[2,192,512]{2,1,0:T(8,128)(2,1)S(1)}, bf16[2,192,512]{2,1,0:T(8,128)(2,1)S(1)}, u32[]{:S(2)}, u32[]{:S(2)}) collective-permute-start(bf16[2,192,512]{2,1,0:T(8,128)(2,1)S(1)} %get-tuple-element.52), channel_id=1, source_target_pairs={{0,16},{4,20},{8,24},{12,28},{16,0},{20,4},{24,8},{28,12},{1,17},{... | collective-permute-start | bytes 1179656 | tf_op jit(solution)/shard_map/ppermute | solution.py:228
  61.8 1.5 %collective-permute-start.12 = (bf16[2,192,512]{2,1,0:T(8,128)(2,1)S(1)}, bf16[2,192,512]{2,1,0:T(8,128)(2,1)S(1)}, u32[]{:S(2)}, u32[]{:S(2)}) collective-permute-start(bf16[2,192,512]{2,1,0:T(8,128)(2,1)S(1)} %get-tuple-element.42.refs_5_), channel_id=1, source_target_pairs={{0,8},{4,12},{8,0},{12,4},{16,24},{20,28},{24,16},{28,20},{1,9},{5... | collective-permute-start | bytes 1179656 | tf_op jit(solution)/shard_map/ppermute | solution.py:228
  63.3 1.3 %collective-permute-start.15 = (bf16[2,1,128,1024]{3,2,1,0:T(8,128)(2,1)}, bf16[2,1,128,1024]{3,2,1,0:T(8,128)(2,1)S(1)}, u32[]{:S(2)}, u32[]{:S(2)}) collective-permute-start(bf16[2,1,128,1024]{3,2,1,0:T(8,128)(2,1)} %collective-permute-done.14.refs_6_.refs_1_), channel_id=1, source_target_pairs={{1,0},{2,3},{5,4},{6,7},{9,8},{10,11},{13,12},{14,15},{17,16},{18,... | collective-permute-start | bytes 1572872 | tf_op jit(solution)/shard_map/ppermute | solution.py:200
  64.6 10.3 %collective-permute-done.16.refs_2_ = bf16[2,1,192,1024]{3,2,1,0:T(8,128)(2,1)} collective-permute-done((bf16[2,1,192,1024]{3,2,1,0:T(8,128)(2,1)}, bf16[2,1,192,1024]{3,2,1,0:T(8,128)(2,1)}, u32[]{:S(2)}, u32[]{:S(2)}) %collective-permute-start.16) | collective-permute-done | bytes 786464 | tf_op jit(solution)/shard_map/ppermute | solution.py:200
  74.9 4.3 %product.4 = (bf16[2,192,512]{2,1,0:T(8,128)(2,1)S(1)}, f32[2,192,512]{2,1,0:T(8,128)S(1)}, bf16[2,192,512]{2,1,0:T(8,128)(2,1)S(1)}, f32[2,192,512]{2,1,0:T(8,128)S(1)}) custom-call(s32[7]{0:T(128)S(1)} %stack.23.spot_ref, bf16[2,1,192,1024]{3,2,1,0:T(8,128)(2,1)S(1)} %copy-done.5, bf16[2,1,192,1024]{3,2,1,0:T(8,128)(2,1)} %collective-permute-done.11.refs_5_.refs_1_, ...), custom_call_target="tpu_custom_call" | custom-call | flops 1610612736 | bytes 6815744 | tf_op jit(solution)/shard_map/product/pallas_call | solution.py:130
  79.2 1.6 %collective-permute-start.23 = (bf16[2,192,512]{2,1,0:T(8,128)(2,1)S(1)}, bf16[2,192,512]{2,1,0:T(8,128)(2,1)S(1)}, u32[]{:S(2)}, u32[]{:S(2)}) collective-permute-start(bf16[2,192,512]{2,1,0:T(8,128)(2,1)S(1)} %get-tuple-element.58), channel_id=1, source_target_pairs={{0,16},{4,20},{8,24},{12,28},{16,0},{20,4},{24,8},{28,12},{1,17},{... | collective-permute-start | bytes 1179656 | tf_op jit(solution)/shard_map/ppermute | solution.py:228
  80.7 1.5 %collective-permute-start.21 = (bf16[2,192,512]{2,1,0:T(8,128)(2,1)S(1)}, bf16[2,192,512]{2,1,0:T(8,128)(2,1)S(1)}, u32[]{:S(2)}, u32[]{:S(2)}) collective-permute-start(bf16[2,192,512]{2,1,0:T(8,128)(2,1)S(1)} %get-tuple-element.45.refs_5_), channel_id=1, source_target_pairs={{0,8},{4,12},{8,0},{12,4},{16,24},{20,28},{24,16},{28,20},{1,9},{5... | collective-permute-start | bytes 1179656 | tf_op jit(solution)/shard_map/ppermute | solution.py:228
  82.2 0.1 convert_add_fusion.2
  82.4 0.6 collective-permute-start.20
  83.0 0.1 convert_add_fusion.3
  83.1 0.6 collective-permute-start.13
  83.7 0.2 collective-permute-done.15.refs_2_
  83.9 3.3 %product.5 = (bf16[2,128,512]{2,1,0:T(8,128)(2,1)S(1)}, f32[2,128,512]{2,1,0:T(8,128)S(1)}, bf16[2,128,512]{2,1,0:T(8,128)(2,1)S(1)}, f32[2,128,512]{2,1,0:T(8,128)S(1)}) custom-call(s32[7]{0:T(128)S(1)} %stack.23.spot_ref, bf16[2,1,128,1024]{3,2,1,0:T(8,128)(2,1)S(1)} %pad_maximum_fusion.2.refs_0_, ...), custom_call_target="tpu_custom_call" | custom-call | flops 1073741824 | bytes 5242880 | tf_op jit(solution)/shard_map/product/pallas_call | solution.py:130
  87.2 1.6 %collective-permute-start.18 = (bf16[2,128,512]{2,1,0:T(8,128)(2,1)S(1)}, bf16[2,128,512]{2,1,0:T(8,128)(2,1)S(1)}, u32[]{:S(2)}, u32[]{:S(2)}) collective-permute-start(bf16[2,128,512]{2,1,0:T(8,128)(2,1)S(1)} %get-tuple-element.49), channel_id=1, source_target_pairs={{0,16},{4,20},{8,24},{12,28},{16,0},{20,4},{24,8},{28,12},{1,17},{... | collective-permute-start | bytes 786440 | tf_op jit(solution)/shard_map/ppermute | solution.py:228
  88.8 1.5 %collective-permute-start.17 = (bf16[2,128,512]{2,1,0:T(8,128)(2,1)S(1)}, bf16[2,128,512]{2,1,0:T(8,128)(2,1)S(1)}, u32[]{:S(2)}, u32[]{:S(2)}) collective-permute-start(bf16[2,128,512]{2,1,0:T(8,128)(2,1)S(1)} %get-tuple-element.47), channel_id=1, source_target_pairs={{0,8},{4,12},{8,0},{12,4},{16,24},{20,28},{24,16},{28,20},{1,9},{5... | collective-permute-start | bytes 786440 | tf_op jit(solution)/shard_map/ppermute | solution.py:228
  90.3 0.1 convert_add_fusion
  90.4 0.1 convert_add_fusion.1
  90.6 0.6 collective-permute-start.22
  91.2 5.3 %collective-permute-done.18 = bf16[2,128,512]{2,1,0:T(8,128)(2,1)S(1)} collective-permute-done((bf16[2,128,512]{2,1,0:T(8,128)(2,1)S(1)}, bf16[2,128,512]{2,1,0:T(8,128)(2,1)S(1)}, u32[]{:S(2)}, u32[]{:S(2)}) %collective-permute-start.18) | collective-permute-done | bytes 262176 | tf_op jit(solution)/shard_map/ppermute | solution.py:228
  96.5 1.5 %collective-permute-start.24 = (bf16[1,192,512]{2,1,0:T(8,128)(2,1)S(1)}, bf16[1,192,512]{2,1,0:T(8,128)(2,1)S(1)}, u32[]{:S(2)}, u32[]{:S(2)}) collective-permute-start(bf16[1,192,512]{2,1,0:T(8,128)(2,1)S(1)} %slice.158), channel_id=1, source_target_pairs={{0,8},{4,12},{8,0},{12,4},{16,24},{20,28},{24,16},{28,20},{1,9},{5... | collective-permute-start | bytes 589832 | tf_op jit(solution)/shard_map/ppermute | solution.py:228
  98.0 0.1 convert_add_fusion.4
  98.1 0.6 collective-permute-start.26
  98.7 0.1 convert_add_fusion.5
  98.9 1.6 %collective-permute-start.25 = (bf16[1,128,512]{2,1,0:T(8,128)(2,1)S(1)}, bf16[1,128,512]{2,1,0:T(8,128)(2,1)S(1)}, u32[]{:S(2)}, u32[]{:S(2)}) collective-permute-start(bf16[1,128,512]{2,1,0:T(8,128)(2,1)S(1)} %slice.163), channel_id=1, source_target_pairs={{0,16},{4,20},{8,24},{12,28},{16,0},{20,4},{24,8},{28,12},{1,17},{... | collective-permute-start | bytes 393224 | tf_op jit(solution)/shard_map/ppermute | solution.py:228
  100.4 0.1 fusion.5
  100.5 0.1 fusion.7
  100.6 1.6 %collective-permute-done.24 = bf16[1,192,512]{2,1,0:T(8,128)(2,1)S(1)} collective-permute-done((bf16[1,192,512]{2,1,0:T(8,128)(2,1)S(1)}, bf16[1,192,512]{2,1,0:T(8,128)(2,1)S(1)}, u32[]{:S(2)}, u32[]{:S(2)}) %collective-permute-start.24) | collective-permute-done | bytes 196640 | tf_op jit(solution)/shard_map/ppermute | solution.py:228
  102.2 0.1 fusion.1
  102.3 0.1 fusion.3
  102.3 1.3 %collective-permute-done.26 = bf16[1,128,512]{2,1,0:T(8,128)(2,1)S(1)} collective-permute-done((bf16[1,128,512]{2,1,0:T(8,128)(2,1)S(1)}, bf16[1,128,512]{2,1,0:T(8,128)(2,1)S(1)}, u32[]{:S(2)}, u32[]{:S(2)}) %collective-permute-start.26) | collective-permute-done | bytes 131104 | tf_op jit(solution)/shard_map/ppermute | solution.py:228
  103.6 0.2 collective-permute-done.25
  103.9 1.5 %maximum_maximum_fusion = f32[512,1024]{1,0:T(8,128)} fusion(f32[128,512]{1,0:T(8,128)S(1)} %fusion.9, f32[128,512]{1,0:T(8,128)S(1)} %fusion.11, f32[192,512]{1,0:T(8,128)S(1)} %fusion.1, f32[192,512]{1,0:T(8,128)S(1)} %fusion.3, f32[192,512]{1,0:T(8,128)S(1)} %fusion.5, f32[192,512]{1,0:T(8,128)S(1)} %fusion.7), kind=kLoop, calls=%fused_computation | loop fusion | flops 2621440 | bytes 4194304 | tf_op jit(solution)/shard_map/concatenate | solution.py:292
  (47 shorter events, 0.5 us)
Async XLA Ops:
  1.9 2.1 %collective-permute-start.2 = (bf16[1,512,512]{2,1,0:T(8,128)(2,1)S(1)}, bf16[1,512,512]{2,1,0:T(8,128)(2,1)S(1)}, u32[]{:S(2)}, u32[]{:S(2)}) collective-permute-start(bf16[1,512,512]{2,1,0:T(8,128)(2,1)S(1)} %get-tuple-element.64), channel_id=1, source_target_pairs={{0,4},{4,0},{8,12},{12,8},{16,20},{20,16},{24,28},{28,24},{1,5},{5... | collective-permute-start | bytes 1572872 | tf_op jit(solution)/shard_map/ppermute | solution.py:228
  2.5 4.8 %copy-start.1 = (bf16[1024,512]{1,0:T(8,128)(2,1)S(1)}, bf16[1024,512]{1,0:T(8,128)(2,1)}, u32[]{:S(2)}) copy-start(bf16[1024,512]{1,0:T(8,128)(2,1)} %k_ref.1) | copy-start | bytes 3145732
  2.5 4.8 %copy-start.2 = (bf16[1024,512]{1,0:T(8,128)(2,1)S(1)}, bf16[1024,512]{1,0:T(8,128)(2,1)}, u32[]{:S(2)}) copy-start(bf16[1024,512]{1,0:T(8,128)(2,1)} %v_ref.1) | copy-start | bytes 3145732
  2.5 6.6 %copy-start = (bf16[1024,512]{1,0:T(8,128)(2,1)S(1)}, bf16[1024,512]{1,0:T(8,128)(2,1)}, u32[]{:S(2)}) copy-start(bf16[1024,512]{1,0:T(8,128)(2,1)} %q_ref.1) | copy-start | bytes 3145732
  2.5 6.6 %copy-start.3 = (bf16[1024,512]{1,0:T(8,128)(2,1)S(1)}, bf16[1024,512]{1,0:T(8,128)(2,1)}, u32[]{:S(2)}) copy-start(bf16[1024,512]{1,0:T(8,128)(2,1)} %go_ref.1) | copy-start | bytes 3145732
  4.0 12.9 %collective-permute-start.3 = (bf16[1,1,192,1024]{3,2,1,0:T(8,128)(2,1)S(1)}, bf16[1,1,192,1024]{3,2,1,0:T(8,128)(2,1)S(1)}, u32[]{:S(2)}, u32[]{:S(2)}) collective-permute-start(bf16[1,1,192,1024]{3,2,1,0:T(8,128)(2,1)S(1)} %maximum_bitcast_fusion.1), channel_id=1, source_target_pairs={{0,1},{1,0},{2,3},{3,2},{4,5},{5,4},{6,7},{7,6},{8,9},{9,8},{10,11... | collective-permute-start | bytes 1179656 | tf_op jit(solution)/shard_map/ppermute | solution.py:179
  7.1 11.5 %copy-start.6 = (bf16[64,128]{1,0:T(8,128)(2,1)S(1)}, bf16[64,128]{1,0:T(8,128)(2,1)}, u32[]{:S(2)}) copy-start(bf16[64,128]{1,0:T(8,128)(2,1)} %f_ref.1) | copy-start | bytes 49156
  7.2 23.3 %collective-permute-start.8 = (bf16[1,1,320,1024]{3,2,1,0:T(8,128)(2,1)S(1)}, bf16[1,1,320,1024]{3,2,1,0:T(8,128)(2,1)S(1)}, u32[]{:S(2)}, u32[]{:S(2)}) collective-permute-start(bf16[1,1,320,1024]{3,2,1,0:T(8,128)(2,1)S(1)} %maximum_bitcast_fusion), channel_id=1, source_target_pairs={{0,1},{1,0},{2,3},{3,2},{4,5},{5,4},{6,7},{7,6},{8,9},{9,8},{10,11... | collective-permute-start | bytes 1966088 | tf_op jit(solution)/shard_map/ppermute | solution.py:179
  7.4 11.2 %collective-permute-start = (bf16[1024,128]{1,0:T(8,128)(2,1)S(1)}, bf16[1024,128]{1,0:T(8,128)(2,1)S(1)}, u32[]{:S(2)}, u32[]{:S(2)}) collective-permute-start(bf16[1024,128]{1,0:T(8,128)(2,1)S(1)} %multiply_convert_fusion.1), channel_id=1, source_target_pairs={{0,4},{4,8},{8,12},{12,16},{16,20},{20,24},{24,28},{1,5},{5,9},{9,... | collective-permute-start | bytes 786440 | tf_op jit(solution)/shard_map/ppermute | solution.py:248
  9.2 9.4 %collective-permute-start.1 = (bf16[1024,128]{1,0:T(8,128)(2,1)S(1)}, bf16[1024,128]{1,0:T(8,128)(2,1)S(1)}, u32[]{:S(2)}, u32[]{:S(2)}) collective-permute-start(bf16[1024,128]{1,0:T(8,128)(2,1)S(1)} %multiply_convert_fusion), channel_id=1, source_target_pairs={{4,0},{8,4},{12,8},{16,12},{20,16},{24,20},{28,24},{5,1},{9,5},{13... | collective-permute-start | bytes 786440 | tf_op jit(solution)/shard_map/ppermute | solution.py:249
  17.0 15.3 %collective-permute-start.7 = (bf16[2,1,192,1024]{3,2,1,0:T(8,128)(2,1)S(1)}, bf16[2,1,192,1024]{3,2,1,0:T(8,128)(2,1)}, u32[]{:S(2)}, u32[]{:S(2)}) collective-permute-start(bf16[2,1,192,1024]{3,2,1,0:T(8,128)(2,1)S(1)} %pad_maximum_fusion.refs_0_), channel_id=1, source_target_pairs={{1,2},{2,1},{5,6},{6,5},{9,10},{10,9},{13,14},{14,13},{17,18},{18,... | collective-permute-start | bytes 2359304 | tf_op jit(solution)/shard_map/ppermute | solution.py:192
  30.7 12.9 %copy-start.4 = (bf16[2,1,192,1024]{3,2,1,0:T(8,128)(2,1)}, bf16[2,1,192,1024]{3,2,1,0:T(8,128)(2,1)S(1)}, u32[]{:S(2)}) copy-start(bf16[2,1,192,1024]{3,2,1,0:T(8,128)(2,1)S(1)} %pad_maximum_fusion.1.refs_0_) | copy-start | bytes 2359300
  30.7 12.9 %collective-permute-start.11 = (bf16[2,1,192,1024]{3,2,1,0:T(8,128)(2,1)S(1)}, bf16[2,1,192,1024]{3,2,1,0:T(8,128)(2,1)}, u32[]{:S(2)}, u32[]{:S(2)}) collective-permute-start(bf16[2,1,192,1024]{3,2,1,0:T(8,128)(2,1)S(1)} %pad_maximum_fusion.1.refs_0_), channel_id=1, source_target_pairs={{1,2},{2,1},{5,6},{6,5},{9,10},{10,9},{13,14},{14,13},{17,18},{18,... | collective-permute-start | bytes 2359304 | tf_op jit(solution)/shard_map/ppermute | solution.py:192
  32.2 14.2 %collective-permute-start.10 = (bf16[512,1024]{1,0:T(8,128)(2,1)S(1)}, bf16[512,1024]{1,0:T(8,128)(2,1)S(1)}, u32[]{:S(2)}, u32[]{:S(2)}) collective-permute-start(bf16[512,1024]{1,0:T(8,128)(2,1)S(1)} %get-tuple-element.40.refs_3_), channel_id=1, source_target_pairs={{0,4},{4,0},{8,12},{12,8},{16,20},{20,16},{24,28},{28,24},{1,5},{5... | collective-permute-start | bytes 3145736 | tf_op jit(solution)/shard_map/ppermute | solution.py:228
  32.4 23.6 %collective-permute-start.9 = (bf16[2,1,192,1024]{3,2,1,0:T(8,128)(2,1)}, bf16[2,1,192,1024]{3,2,1,0:T(8,128)(2,1)}, u32[]{:S(2)}, u32[]{:S(2)}) collective-permute-start(bf16[2,1,192,1024]{3,2,1,0:T(8,128)(2,1)} %collective-permute-done.7.refs_1_), channel_id=1, source_target_pairs={{1,0},{2,3},{5,4},{6,7},{9,8},{10,11},{13,12},{14,15},{17,16},{18,... | collective-permute-start | bytes 2359304 | tf_op jit(solution)/shard_map/ppermute | solution.py:200
  33.7 1.4 %collective-permute-start.4 = (f32[64,128]{1,0:T(8,128)S(1)}, f32[64,128]{1,0:T(8,128)S(1)}, u32[]{:S(2)}, u32[]{:S(2)}) collective-permute-start(f32[64,128]{1,0:T(8,128)S(1)} %get-tuple-element.36), channel_id=1, source_target_pairs={{0,4},{4,0},{8,12},{12,8},{16,20},{20,16},{24,28},{28,24},{1,5},{5... | collective-permute-start | bytes 98312 | tf_op jit(solution)/shard_map/ppermute | solution.py:228
  35.1 3.9 %collective-permute-start.5 = (f32[64,128]{1,0:T(8,128)S(1)}, f32[64,128]{1,0:T(8,128)S(1)}, u32[]{:S(2)}, u32[]{:S(2)}) collective-permute-start(f32[64,128]{1,0:T(8,128)S(1)} %add.141), channel_id=1, source_target_pairs={{0,8},{4,12},{8,0},{12,4},{16,24},{20,28},{24,16},{28,20},{1,9},{5... | collective-permute-start | bytes 98312 | tf_op jit(solution)/shard_map/ppermute | solution.py:228
  39.0 3.9 %collective-permute-start.6 = (f32[64,128]{1,0:T(8,128)S(1)}, f32[64,128]{1,0:T(8,128)S(1)}, u32[]{:S(2)}, u32[]{:S(2)}) collective-permute-start(f32[64,128]{1,0:T(8,128)S(1)} %add.142), channel_id=1, source_target_pairs={{0,16},{4,20},{8,24},{12,28},{16,0},{20,4},{24,8},{28,12},{1,17},{... | collective-permute-start | bytes 98312 | tf_op jit(solution)/shard_map/ppermute | solution.py:228
  43.6 31.3 %collective-permute-start.16 = (bf16[2,1,192,1024]{3,2,1,0:T(8,128)(2,1)}, bf16[2,1,192,1024]{3,2,1,0:T(8,128)(2,1)}, u32[]{:S(2)}, u32[]{:S(2)}) collective-permute-start(bf16[2,1,192,1024]{3,2,1,0:T(8,128)(2,1)} %collective-permute-done.11.refs_5_.refs_1_), channel_id=1, source_target_pairs={{1,0},{2,3},{5,4},{6,7},{9,8},{10,11},{13,12},{14,15},{17,16},{18,... | collective-permute-start | bytes 2359304 | tf_op jit(solution)/shard_map/ppermute | solution.py:200
  44.9 18.4 %collective-permute-start.14 = (bf16[2,1,128,1024]{3,2,1,0:T(8,128)(2,1)S(1)}, bf16[2,1,128,1024]{3,2,1,0:T(8,128)(2,1)}, u32[]{:S(2)}, u32[]{:S(2)}) collective-permute-start(bf16[2,1,128,1024]{3,2,1,0:T(8,128)(2,1)S(1)} %pad_maximum_fusion.2.refs_0_), channel_id=1, source_target_pairs={{1,2},{2,1},{5,6},{6,5},{9,10},{10,9},{13,14},{14,13},{17,18},{18,... | collective-permute-start | bytes 1572872 | tf_op jit(solution)/shard_map/ppermute | solution.py:192
  46.4 28.5 %copy-start.5 = (bf16[2,1,192,1024]{3,2,1,0:T(8,128)(2,1)S(1)}, bf16[2,1,192,1024]{3,2,1,0:T(8,128)(2,1)}, u32[]{:S(2)}) copy-start(bf16[2,1,192,1024]{3,2,1,0:T(8,128)(2,1)} %copy-done.4) | copy-start | bytes 2359300
  60.2 22.0 %collective-permute-start.19 = (bf16[2,192,512]{2,1,0:T(8,128)(2,1)S(1)}, bf16[2,192,512]{2,1,0:T(8,128)(2,1)S(1)}, u32[]{:S(2)}, u32[]{:S(2)}) collective-permute-start(bf16[2,192,512]{2,1,0:T(8,128)(2,1)S(1)} %get-tuple-element.52), channel_id=1, source_target_pairs={{0,16},{4,20},{8,24},{12,28},{16,0},{20,4},{24,8},{28,12},{1,17},{... | collective-permute-start | bytes 1179656 | tf_op jit(solution)/shard_map/ppermute | solution.py:228
  61.8 21.2 %collective-permute-start.12 = (bf16[2,192,512]{2,1,0:T(8,128)(2,1)S(1)}, bf16[2,192,512]{2,1,0:T(8,128)(2,1)S(1)}, u32[]{:S(2)}, u32[]{:S(2)}) collective-permute-start(bf16[2,192,512]{2,1,0:T(8,128)(2,1)S(1)} %get-tuple-element.42.refs_5_), channel_id=1, source_target_pairs={{0,8},{4,12},{8,0},{12,4},{16,24},{20,28},{24,16},{28,20},{1,9},{5... | collective-permute-start | bytes 1179656 | tf_op jit(solution)/shard_map/ppermute | solution.py:228
  63.3 20.6 %collective-permute-start.15 = (bf16[2,1,128,1024]{3,2,1,0:T(8,128)(2,1)}, bf16[2,1,128,1024]{3,2,1,0:T(8,128)(2,1)S(1)}, u32[]{:S(2)}, u32[]{:S(2)}) collective-permute-start(bf16[2,1,128,1024]{3,2,1,0:T(8,128)(2,1)} %collective-permute-done.14.refs_6_.refs_1_), channel_id=1, source_target_pairs={{1,0},{2,3},{5,4},{6,7},{9,8},{10,11},{13,12},{14,15},{17,16},{18,... | collective-permute-start | bytes 1572872 | tf_op jit(solution)/shard_map/ppermute | solution.py:200
  79.2 9.7 %collective-permute-start.23 = (bf16[2,192,512]{2,1,0:T(8,128)(2,1)S(1)}, bf16[2,192,512]{2,1,0:T(8,128)(2,1)S(1)}, u32[]{:S(2)}, u32[]{:S(2)}) collective-permute-start(bf16[2,192,512]{2,1,0:T(8,128)(2,1)S(1)} %get-tuple-element.58), channel_id=1, source_target_pairs={{0,16},{4,20},{8,24},{12,28},{16,0},{20,4},{24,8},{28,12},{1,17},{... | collective-permute-start | bytes 1179656 | tf_op jit(solution)/shard_map/ppermute | solution.py:228
  80.7 9.7 %collective-permute-start.21 = (bf16[2,192,512]{2,1,0:T(8,128)(2,1)S(1)}, bf16[2,192,512]{2,1,0:T(8,128)(2,1)S(1)}, u32[]{:S(2)}, u32[]{:S(2)}) collective-permute-start(bf16[2,192,512]{2,1,0:T(8,128)(2,1)S(1)} %get-tuple-element.45.refs_5_), channel_id=1, source_target_pairs={{0,8},{4,12},{8,0},{12,4},{16,24},{20,28},{24,16},{28,20},{1,9},{5... | collective-permute-start | bytes 1179656 | tf_op jit(solution)/shard_map/ppermute | solution.py:228
  82.4 16.5 %collective-permute-start.20 = (bf16[1,192,512]{2,1,0:T(8,128)(2,1)S(1)}, bf16[1,192,512]{2,1,0:T(8,128)(2,1)S(1)}, u32[]{:S(2)}, u32[]{:S(2)}) collective-permute-start(bf16[1,192,512]{2,1,0:T(8,128)(2,1)S(1)} %slice.160), channel_id=1, source_target_pairs={{0,8},{4,12},{8,0},{12,4},{16,24},{20,28},{24,16},{28,20},{1,9},{5... | collective-permute-start | bytes 589832 | tf_op jit(solution)/shard_map/ppermute | solution.py:228
  83.1 17.4 %collective-permute-start.13 = (bf16[1,192,512]{2,1,0:T(8,128)(2,1)S(1)}, bf16[1,192,512]{2,1,0:T(8,128)(2,1)S(1)}, u32[]{:S(2)}, u32[]{:S(2)}) collective-permute-start(bf16[1,192,512]{2,1,0:T(8,128)(2,1)S(1)} %slice.161), channel_id=1, source_target_pairs={{0,16},{4,20},{8,24},{12,28},{16,0},{20,4},{24,8},{28,12},{1,17},{... | collective-permute-start | bytes 589832 | tf_op jit(solution)/shard_map/ppermute | solution.py:228
  87.2 9.3 %collective-permute-start.18 = (bf16[2,128,512]{2,1,0:T(8,128)(2,1)S(1)}, bf16[2,128,512]{2,1,0:T(8,128)(2,1)S(1)}, u32[]{:S(2)}, u32[]{:S(2)}) collective-permute-start(bf16[2,128,512]{2,1,0:T(8,128)(2,1)S(1)} %get-tuple-element.49), channel_id=1, source_target_pairs={{0,16},{4,20},{8,24},{12,28},{16,0},{20,4},{24,8},{28,12},{1,17},{... | collective-permute-start | bytes 786440 | tf_op jit(solution)/shard_map/ppermute | solution.py:228
  88.8 9.3 %collective-permute-start.17 = (bf16[2,128,512]{2,1,0:T(8,128)(2,1)S(1)}, bf16[2,128,512]{2,1,0:T(8,128)(2,1)S(1)}, u32[]{:S(2)}, u32[]{:S(2)}) collective-permute-start(bf16[2,128,512]{2,1,0:T(8,128)(2,1)S(1)} %get-tuple-element.47), channel_id=1, source_target_pairs={{0,8},{4,12},{8,0},{12,4},{16,24},{20,28},{24,16},{28,20},{1,9},{5... | collective-permute-start | bytes 786440 | tf_op jit(solution)/shard_map/ppermute | solution.py:228
  90.6 11.6 %collective-permute-start.22 = (bf16[1,192,512]{2,1,0:T(8,128)(2,1)S(1)}, bf16[1,192,512]{2,1,0:T(8,128)(2,1)S(1)}, u32[]{:S(2)}, u32[]{:S(2)}) collective-permute-start(bf16[1,192,512]{2,1,0:T(8,128)(2,1)S(1)} %slice.159), channel_id=1, source_target_pairs={{0,16},{4,20},{8,24},{12,28},{16,0},{20,4},{24,8},{28,12},{1,17},{... | collective-permute-start | bytes 589832 | tf_op jit(solution)/shard_map/ppermute | solution.py:228
  96.5 5.7 %collective-permute-start.24 = (bf16[1,192,512]{2,1,0:T(8,128)(2,1)S(1)}, bf16[1,192,512]{2,1,0:T(8,128)(2,1)S(1)}, u32[]{:S(2)}, u32[]{:S(2)}) collective-permute-start(bf16[1,192,512]{2,1,0:T(8,128)(2,1)S(1)} %slice.158), channel_id=1, source_target_pairs={{0,8},{4,12},{8,0},{12,4},{16,24},{20,28},{24,16},{28,20},{1,9},{5... | collective-permute-start | bytes 589832 | tf_op jit(solution)/shard_map/ppermute | solution.py:228
  98.1 5.5 %collective-permute-start.26 = (bf16[1,128,512]{2,1,0:T(8,128)(2,1)S(1)}, bf16[1,128,512]{2,1,0:T(8,128)(2,1)S(1)}, u32[]{:S(2)}, u32[]{:S(2)}) collective-permute-start(bf16[1,128,512]{2,1,0:T(8,128)(2,1)S(1)} %slice.162), channel_id=1, source_target_pairs={{0,8},{4,12},{8,0},{12,4},{16,24},{20,28},{24,16},{28,20},{1,9},{5... | collective-permute-start | bytes 393224 | tf_op jit(solution)/shard_map/ppermute | solution.py:228
  98.9 5.0 %collective-permute-start.25 = (bf16[1,128,512]{2,1,0:T(8,128)(2,1)S(1)}, bf16[1,128,512]{2,1,0:T(8,128)(2,1)S(1)}, u32[]{:S(2)}, u32[]{:S(2)}) collective-permute-start(bf16[1,128,512]{2,1,0:T(8,128)(2,1)S(1)} %slice.163), channel_id=1, source_target_pairs={{0,16},{4,20},{8,24},{12,28},{16,0},{20,4},{24,8},{28,12},{1,17},{... | collective-permute-start | bytes 393224 | tf_op jit(solution)/shard_map/ppermute | solution.py:228
